TPU v7x, 32 devices: a whole 2x2x4 slice. The times are simulated.
32 devices in a mesh: fsdp: 4 (over y, core), ctx: 4 (over z), tp: 2 (over x).
Axes of the slice: x: 2, y: 2, z: 4, core: 2. Of those that a mesh axis runs over, the one named last changes fastest.
Arguments:
- hidden_in: bfloat16 [2, 4, 1024, 2048], P(None, 'fsdp', ('ctx', 'tp')), may hold values from -6 to 6
- cotangent: bfloat16 [2, 4, 1024, 2048], P(None, 'fsdp', ('ctx', 'tp')), may hold values from -6 to 6
- block_ids: int32 [2, 4, 1024], P(None, 'fsdp'), may hold values from 0 to 7, never falling along the last dimension, each value on 1 to 256 neighbouring positions
- positions: int32 [2, 4, 1024], P(None, 'fsdp', 'ctx'), may hold values from 0 to 5115, as said below
- attn_gain: bfloat16 [2048], P(('fsdp', 'ctx')), may hold values from 0.5 to 1.5
- wqkv: bfloat16 [2048, 4096], P(('fsdp', 'ctx'), 'tp'), may hold values from -0.125 to 0.125
- wo: bfloat16 [2048, 2048], P('tp', ('fsdp', 'ctx')), may hold values from -0.75 to 0.75
- ffn_gain: bfloat16 [2048], P(('fsdp', 'ctx')), may hold values from 0.5 to 1.5
- w_gate: bfloat16 [2048, 8192], P(('fsdp', 'ctx'), 'tp'), may hold values from -0.125 to 0.125
- w_up: bfloat16 [2048, 8192], P(('fsdp', 'ctx'), 'tp'), may hold values from -0.125 to 0.125
- w_down: bfloat16 [8192, 2048], P('tp', ('fsdp', 'ctx')), may hold values from -0.09375 to 0.09375
Outputs:
- hidden_out: bfloat16 [2, 4, 1024, 2048], P(None, 'fsdp', ('ctx', 'tp'))
- grad_in: bfloat16 [2, 4, 1024, 2048], P(None, 'fsdp', ('ctx', 'tp'))
- grad_attn_gain: float32 [2048], P(('fsdp', 'ctx'))
- grad_wqkv: float32 [2048, 4096], P(('fsdp', 'ctx'), 'tp')
- grad_wo: float32 [2048, 2048], P('tp', ('fsdp', 'ctx'))
- grad_ffn_gain: float32 [2048], P(('fsdp', 'ctx'))
- grad_gate: float32 [2048, 8192], P(('fsdp', 'ctx'), 'tp')
- grad_up: float32 [2048, 8192], P(('fsdp', 'ctx'), 'tp')
- grad_down: float32 [8192, 2048], P('tp', ('fsdp', 'ctx'))
Inputs may be any that keep to these rules, and one draw needn't show every extreme that they name: `block_ids`: within each sequence block ids never fall and each block holds 1 to 256 tokens. Within each sequence positions rise from token to token by a step of 1 to 4; a sequence starts at a position from 0 to 1023.
All inputs are finite; a program needn't handle non-finite values.
Results may differ from a plain program's by a relative error of at most 0.02.
Values may be sent and summed in bfloat16 or wider, within the bound.
A program may use at most 192 MiB of HBM per device.

v0:
```python
import jax
import jax.numpy as jnp
from jax import lax
from jax.sharding import PartitionSpec as P

HEADS = 16
KV_HEADS = 8
HEAD_DIM = 128


EPS = 1e-05
THETA = 1000000.0
MASKED = -1e30


def rope_tables(position_ids):
    half_dim = HEAD_DIM // 2
    inverse = THETA ** (-(jnp.arange(half_dim, dtype=jnp.float32) * 2.0 / HEAD_DIM))
    angles = position_ids.astype(jnp.float32)[..., None] * inverse
    angles = jnp.concatenate([angles, angles], axis=-1)
    return (jnp.cos(angles), jnp.sin(angles))


def turned(values):
    half_dim = values.shape[-1] // 2
    return jnp.concatenate([-values[..., half_dim:], values[..., :half_dim]], axis=-1)


def turned_back(values):
    half_dim = values.shape[-1] // 2
    return jnp.concatenate([values[..., half_dim:], -values[..., :half_dim]], axis=-1)


def norm_rows(stream, gain_row):
    factor = lax.rsqrt(jnp.mean(stream * stream, axis=-1, keepdims=True) + EPS)
    normed = stream * factor
    return (normed, factor, (normed * gain_row).astype(jnp.bfloat16))


def norm_back(grad_out, normed, factor, gain_row):
    grad_normed = grad_out * gain_row
    inner_mean = jnp.mean(grad_normed * normed, axis=-1, keepdims=True)
    return (factor * (grad_normed - normed * inner_mean), jnp.sum(grad_out * normed, axis=(0, 1)))


def fetch_weights(wqkv, attn_gain, wo, w_gate, w_up, w_down, ffn_gain):
    return (
        lax.all_gather(wqkv, ("fsdp", "ctx"), axis=0, tiled=True),
        lax.all_gather(attn_gain, ("fsdp", "ctx"), axis=0, tiled=True),
        lax.all_gather(wo, ("fsdp", "ctx"), axis=1, tiled=True),
        lax.all_gather(w_gate, ("fsdp", "ctx"), axis=0, tiled=True),
        lax.all_gather(w_up, ("fsdp", "ctx"), axis=0, tiled=True),
        lax.all_gather(w_down, ("fsdp", "ctx"), axis=1, tiled=True),
        lax.all_gather(ffn_gain, ("fsdp", "ctx"), axis=0, tiled=True),
    )


def spread_rows(local_rows):
    return lax.all_gather(local_rows, "tp", axis=1, tiled=True)


def fold_rows(partial_rows):
    return lax.psum_scatter(
        partial_rows.astype(jnp.bfloat16), "tp", scatter_dimension=1, tiled=True
    ).astype(jnp.float32)


def body(
    hidden_in, cotangent, block_ids, positions, attn_gain, wqkv, wo, ffn_gain, w_gate, w_up, w_down
):
    micro_count = hidden_in.shape[0]
    seq_count = hidden_in.shape[1]
    block_len = positions.shape[2]
    group_size = HEADS // KV_HEADS
    kv_local = KV_HEADS // lax.axis_size("tp")
    score_scale = HEAD_DIM ** (-0.5)
    first_row = lax.axis_index("ctx") * block_len
    acc_qkv = jnp.zeros(wqkv.shape, jnp.float32)
    acc_out = jnp.zeros(wo.shape, jnp.float32)
    acc_gate = jnp.zeros(w_gate.shape, jnp.float32)
    acc_up = jnp.zeros(w_up.shape, jnp.float32)
    acc_down = jnp.zeros(w_down.shape, jnp.float32)
    acc_gain_attn = jnp.zeros(attn_gain.shape, jnp.float32)
    acc_gain_ffn = jnp.zeros(ffn_gain.shape, jnp.float32)
    outputs = []
    input_grads = []
    for micro_step in range(micro_count):
        front_weights = fetch_weights(wqkv, attn_gain, wo, w_gate, w_up, w_down, ffn_gain)
        (
            query_key_value_complete,
            gain_attn,
            output_weight_complete,
            gate_weight_complete,
            up_weight_complete,
            down_weight_complete,
            gain_ffn,
        ) = front_weights
        gain_attn = gain_attn.astype(jnp.float32)
        gain_ffn = gain_ffn.astype(jnp.float32)
        stream = hidden_in[micro_step].astype(jnp.float32)
        seq_ids = block_ids[micro_step]
        query_ids = lax.dynamic_slice_in_dim(seq_ids, first_row, block_len, 1)
        allowed = seq_ids[:, None, None, None, :] <= query_ids[:, None, None, :, None]
        cos_table, sin_table = rope_tables(positions[micro_step])
        cos_heads = cos_table[:, :, None, None]
        sin_heads = sin_table[:, :, None, None]
        cos_keys = cos_table[:, :, None]
        sin_keys = sin_table[:, :, None]
        normed_one, factor_one, attn_rows = norm_rows(stream, gain_attn)
        attention_input = spread_rows(attn_rows)
        projection_output = jnp.einsum(
            "nve,ew->nvw",
            attention_input,
            query_key_value_complete,
            preferred_element_type=jnp.float32,
        )
        projection_output = projection_output.reshape(
            seq_count, block_len, kv_local, group_size + 2, HEAD_DIM
        )
        query_part = projection_output[:, :, :, :group_size]
        key_part = projection_output[:, :, :, group_size]
        query_rows_local = (query_part * cos_heads + turned(query_part) * sin_heads).astype(
            jnp.bfloat16
        )
        keys_own = (key_part * cos_keys + turned(key_part) * sin_keys).astype(jnp.bfloat16)
        values_own = projection_output[:, :, :, group_size + 1].astype(jnp.bfloat16)
        keys_all, values_all = (
            lax.all_gather(keys_own, "ctx", axis=1, tiled=True),
            lax.all_gather(values_own, "ctx", axis=1, tiled=True),
        )
        unnormalized_scores = jnp.einsum(
            "slhgd,smhd->shglm", query_rows_local, keys_all, preferred_element_type=jnp.float32
        )
        scores = jnp.where(allowed, unnormalized_scores * score_scale, MASKED)
        row_max = jnp.max(scores, axis=-1, keepdims=True)
        exponent = jnp.exp(scores - row_max)
        row_total = jnp.sum(exponent, axis=-1, keepdims=True)
        attention_probability = exponent / row_total
        log_total = row_max + jnp.log(row_total)
        combined_head_output = jnp.einsum(
            "shglm,smhd->slhgd",
            attention_probability.astype(jnp.bfloat16),
            values_all,
            preferred_element_type=jnp.float32,
        )
        combined_head_output = combined_head_output.reshape(seq_count, block_len, -1).astype(
            jnp.bfloat16
        )
        stream_mid = stream + fold_rows(
            jnp.einsum(
                "tfq,qu->tfu",
                combined_head_output,
                output_weight_complete,
                preferred_element_type=jnp.float32,
            )
        )
        normed_two, factor_two, ffn_rows = norm_rows(stream_mid, gain_ffn)
        feedforward_input = spread_rows(ffn_rows)
        gate_preactivation = jnp.einsum(
            "qch,hj->qcj",
            feedforward_input,
            gate_weight_complete,
            preferred_element_type=jnp.float32,
        )
        up_preactivation = jnp.einsum(
            "qch,hj->qcj", feedforward_input, up_weight_complete, preferred_element_type=jnp.float32
        )
        gate_sig = jax.nn.sigmoid(gate_preactivation)
        gate_act = gate_preactivation * gate_sig
        hidden_activation = (gate_act * up_preactivation).astype(jnp.bfloat16)
        stream_out = stream_mid + fold_rows(
            jnp.einsum(
                "xir,ro->xio",
                hidden_activation,
                down_weight_complete,
                preferred_element_type=jnp.float32,
            )
        )
        outputs.append(stream_out.astype(jnp.bfloat16))
        back_weights = fetch_weights(wqkv, attn_gain, wo, w_gate, w_up, w_down, ffn_gain)
        (
            query_key_value_backward,
            spare_one,
            output_weight_backward,
            gate_weight_backward,
            up_weight_backward,
            down_weight_backward,
            spare_two,
        ) = back_weights
        grad_out = cotangent[micro_step].astype(jnp.float32)
        down_input_gradient = spread_rows(grad_out.astype(jnp.bfloat16))
        grad_hidden = jnp.einsum(
            "aiq,mq->aim",
            down_input_gradient,
            down_weight_backward,
            preferred_element_type=jnp.float32,
        )
        grad_down_w = jnp.einsum(
            "azc,aze->ce",
            hidden_activation,
            down_input_gradient,
            preferred_element_type=jnp.float32,
        )
        gate_preactivation_gradient = (
            grad_hidden
            * up_preactivation
            * gate_sig
            * (1.0 + gate_preactivation * (1.0 - gate_sig))
        ).astype(jnp.bfloat16)
        up_preactivation_gradient = (grad_hidden * gate_act).astype(jnp.bfloat16)
        grad_ffn_part = jnp.einsum(
            "knw,jw->knj",
            gate_preactivation_gradient,
            gate_weight_backward,
            preferred_element_type=jnp.float32,
        )
        grad_ffn_part = grad_ffn_part + jnp.einsum(
            "knw,jw->knj",
            up_preactivation_gradient,
            up_weight_backward,
            preferred_element_type=jnp.float32,
        )
        grad_ffn_rows = fold_rows(grad_ffn_part)
        grad_gate_w = jnp.einsum(
            "oye,oyk->ek",
            feedforward_input,
            gate_preactivation_gradient,
            preferred_element_type=jnp.float32,
        )
        grad_up_w = jnp.einsum(
            "oye,oyk->ek",
            feedforward_input,
            up_preactivation_gradient,
            preferred_element_type=jnp.float32,
        )
        grad_mid_norm, gain_ffn_part = norm_back(grad_ffn_rows, normed_two, factor_two, gain_ffn)
        grad_mid = grad_out + grad_mid_norm
        attention_output_gradient = spread_rows(grad_mid.astype(jnp.bfloat16))
        grad_mixed = jnp.einsum(
            "xji,wi->xjw",
            attention_output_gradient,
            output_weight_backward,
            preferred_element_type=jnp.float32,
        )
        grad_mixed = grad_mixed.astype(jnp.bfloat16).reshape(
            seq_count, block_len, kv_local, group_size, HEAD_DIM
        )
        grad_wo_w = jnp.einsum(
            "pnt,pnb->tb",
            combined_head_output,
            attention_output_gradient,
            preferred_element_type=jnp.float32,
        )
        raw_again = jnp.einsum(
            "slhgd,smhd->shglm", query_rows_local, keys_all, preferred_element_type=jnp.float32
        )
        prob_again = jnp.exp(jnp.where(allowed, raw_again * score_scale, MASKED) - log_total)
        grad_prob = jnp.einsum(
            "slhgd,smhd->shglm", grad_mixed, values_all, preferred_element_type=jnp.float32
        )
        inner_prob = jnp.sum(grad_prob * prob_again, axis=-1, keepdims=True)
        grad_scores = (score_scale * prob_again * (grad_prob - inner_prob)).astype(jnp.bfloat16)
        grad_queries = jnp.einsum(
            "shglm,smhd->slhgd", grad_scores, keys_all, preferred_element_type=jnp.float32
        )
        grad_keys_all = jnp.einsum(
            "shglm,slhgd->smhd", grad_scores, query_rows_local, preferred_element_type=jnp.float32
        )
        grad_values_all = jnp.einsum(
            "shglm,slhgd->smhd",
            prob_again.astype(jnp.bfloat16),
            grad_mixed,
            preferred_element_type=jnp.float32,
        )
        grad_keys, grad_values = (
            lax.psum_scatter(
                grad_keys_all.astype(jnp.bfloat16), "ctx", scatter_dimension=1, tiled=True
            ).astype(jnp.float32),
            lax.psum_scatter(
                grad_values_all.astype(jnp.bfloat16), "ctx", scatter_dimension=1, tiled=True
            ).astype(jnp.float32),
        )
        grad_query_pre = grad_queries * cos_heads + turned_back(grad_queries * sin_heads)
        grad_key_pre = grad_keys * cos_keys + turned_back(grad_keys * sin_keys)
        projection_output_gradient = jnp.concatenate(
            [grad_query_pre, grad_key_pre[:, :, :, None], grad_values[:, :, :, None]], axis=3
        )
        projection_output_gradient = projection_output_gradient.astype(jnp.bfloat16).reshape(
            seq_count, block_len, -1
        )
        grad_attn_rows = fold_rows(
            jnp.einsum(
                "bxp,ip->bxi",
                projection_output_gradient,
                query_key_value_backward,
                preferred_element_type=jnp.float32,
            )
        )
        grad_qkv_w = jnp.einsum(
            "hmg,hmo->go",
            attention_input,
            projection_output_gradient,
            preferred_element_type=jnp.float32,
        )
        grad_in_norm, gain_attn_part = norm_back(grad_attn_rows, normed_one, factor_one, gain_attn)
        input_grads.append((grad_mid + grad_in_norm).astype(jnp.bfloat16))
        summed = (
            lax.psum_scatter(grad_qkv_w, ("fsdp", "ctx"), scatter_dimension=0, tiled=True),
            lax.psum_scatter(gain_attn_part, ("fsdp", "ctx"), scatter_dimension=0, tiled=True),
            lax.psum_scatter(grad_wo_w, ("fsdp", "ctx"), scatter_dimension=1, tiled=True),
            lax.psum_scatter(grad_gate_w, ("fsdp", "ctx"), scatter_dimension=0, tiled=True),
            lax.psum_scatter(grad_up_w, ("fsdp", "ctx"), scatter_dimension=0, tiled=True),
            lax.psum_scatter(grad_down_w, ("fsdp", "ctx"), scatter_dimension=1, tiled=True),
            lax.psum_scatter(gain_ffn_part, ("fsdp", "ctx"), scatter_dimension=0, tiled=True),
        )
        acc_qkv = acc_qkv + summed[0]
        acc_gain_attn = acc_gain_attn + summed[1]
        acc_out = acc_out + summed[2]
        acc_gate = acc_gate + summed[3]
        acc_up = acc_up + summed[4]
        acc_down = acc_down + summed[5]
        acc_gain_ffn = acc_gain_ffn + summed[6]
    gain_attn_sum, gain_ffn_sum = lax.psum((acc_gain_attn, acc_gain_ffn), "tp")
    return (
        jnp.stack(outputs),
        jnp.stack(input_grads),
        gain_attn_sum,
        acc_qkv,
        acc_out,
        gain_ffn_sum,
        acc_gate,
        acc_up,
        acc_down,
    )


def solution(mesh):
    return jax.shard_map(
        body,
        mesh=mesh,
        in_specs=(
            P(None, "fsdp", ("ctx", "tp"), None),
            P(None, "fsdp", ("ctx", "tp"), None),
            P(None, "fsdp", None),
            P(None, "fsdp", "ctx"),
            P(("fsdp", "ctx")),
            P(("fsdp", "ctx"), "tp"),
            P("tp", ("fsdp", "ctx")),
            P(("fsdp", "ctx")),
            P(("fsdp", "ctx"), "tp"),
            P(("fsdp", "ctx"), "tp"),
            P("tp", ("fsdp", "ctx")),
        ),
        out_specs=(
            P(None, "fsdp", ("ctx", "tp"), None),
            P(None, "fsdp", ("ctx", "tp"), None),
            P(("fsdp", "ctx")),
            P(("fsdp", "ctx"), "tp"),
            P("tp", ("fsdp", "ctx")),
            P(("fsdp", "ctx")),
            P(("fsdp", "ctx"), "tp"),
            P(("fsdp", "ctx"), "tp"),
            P("tp", ("fsdp", "ctx")),
        ),
        check_vma=False,
    )
```

profile of v0, /device:TPU:1, one launch (start us, length us, event | category | flops | bytes accessed | tf_op | source)
XLA Modules:
  0.0 2474.1 jit_solution(7586854633854979743)
XLA Ops:
  8.0 30.6 %all-gather.4 = bf16[16,1,128]{2,1,0:T(2,128)(2,1)S(1)} all-gather(bf16[1,1,128]{2,1,0:T(2,128)(2,1)} %bitcast.461), channel_id=1, replica_groups=mesh['fsdp'=4,'ctx'=4,'tp'=2] {'fsdp','ctx'}, dimensions={0}, use_global_device_ids=true | all-gather | bytes 4352 | tf_op jit(solution)/shard_map/all_gather | solution.py:49
  44.0 43.8 %all-gather.26.cloned.1.call-done = bf16[2048,2048]{1,0:T(8,128)(2,1)} async-done(((bf16[128,2048]{1,0:T(8,128)(2,1)}), bf16[2048,2048]{1,0:T(8,128)(2,1)}) %all-gather.26.cloned.1.call-update) | async-done | bytes 8388624 | tf_op jit(solution)/shard_map/all_gather | solution.py:48
  87.8 12.4 copy.41
  100.1 8.9 all-gather.24.cloned.1.call-done
  109.0 6.1 convolution_bitcast_fusion.1
  118.0 14.5 all-gather.40.cloned.1.call-done
  132.5 6.1 convolution_bitcast_fusion
  146.9 16.6 all-gather.28.cloned.1.call-done
  170.7 23.2 all-gather.50.cloned.1.call-done
  193.9 5.2 fusion.56
  199.2 50.0 %all-gather.30.cloned.1.call-done = bf16[1024,2048]{1,0:T(8,128)(2,1)} async-done(((bf16[1024,128]{1,0:T(8,128)(2,1)}), bf16[1024,2048]{1,0:T(8,128)(2,1)}) %all-gather.30.cloned.1.call-update) | async-done | bytes 4194320 | tf_op jit(solution)/shard_map/all_gather | solution.py:50
  249.2 4.4 fusion.32
  253.7 24.3 all-gather.42.cloned.1.call-done
  285.1 23.5 all-gather.52.cloned.1.call-done
  308.6 5.4 fusion.59
  317.2 29.4 %all-gather.5 = bf16[16,1,128]{2,1,0:T(2,128)(2,1)S(1)} all-gather(bf16[1,1,128]{2,1,0:T(2,128)(2,1)S(1)} %bitcast.462), channel_id=1, replica_groups=mesh['fsdp'=4,'ctx'=4,'tp'=2] {'fsdp','ctx'}, dimensions={0}, use_global_device_ids=true | all-gather | bytes 4352 | tf_op jit(solution)/shard_map/all_gather | solution.py:54
  346.6 7.9 reduce-scatter.22.cloned.1.call-done
  363.4 16.8 all-gather.32.cloned.1.call-done
  380.2 129.4 %all-gather.34.cloned.1.call-done = bf16[2048,4096]{1,0:T(8,128)(2,1)} async-done(((bf16[128,4096]{1,0:T(8,128)(2,1)}), bf16[2048,4096]{1,0:T(8,128)(2,1)}) %all-gather.34.cloned.1.call-update) | async-done | bytes 16777232 | tf_op jit(solution)/shard_map/all_gather | solution.py:51
  509.6 12.6 fusion.131
  522.2 114.7 %all-gather.36.cloned.1.call-done = bf16[2048,4096]{1,0:T(8,128)(2,1)} async-done(((bf16[128,4096]{1,0:T(8,128)(2,1)}), bf16[2048,4096]{1,0:T(8,128)(2,1)}) %all-gather.36.cloned.1.call-update) | async-done | bytes 16777232 | tf_op jit(solution)/shard_map/all_gather | solution.py:52
  636.9 10.2 fusion.129
  647.1 10.9 all-gather.54.cloned.1.call-done
  658.0 132.7 %all-gather.38.cloned.1.call-done = bf16[4096,2048]{1,0:T(8,128)(2,1)} async-done(((bf16[4096,128]{1,0:T(8,128)(2,1)}), bf16[4096,2048]{1,0:T(8,128)(2,1)}) %all-gather.38.cloned.1.call-update) | async-done | bytes 16777232 | tf_op jit(solution)/shard_map/all_gather | solution.py:53
  790.7 13.9 multiply_convert_fusion.2
  804.6 12.2 fusion.165
  816.9 13.0 fusion.31
  830.0 12.7 fusion.122
  842.6 10.9 fusion.120
  853.6 13.5 multiply_convert_fusion
  867.1 12.2 fusion.166
  879.4 12.5 fusion.30
  891.9 12.3 fusion.29
  904.5 5.4 reduce-scatter.34.cloned.1.call-done
  912.6 20.3 reduce-scatter.24.cloned.1.call-done
  937.1 20.7 all-gather.46.cloned.1.call-done
  957.8 3.8 convolution_convert_fusion.7
  961.8 5.5 fusion.3
  974.5 5.9 fusion.49
  981.3 3.8 convolution_convert_fusion.6
  985.3 5.5 fusion
  1002.0 6.0 fusion.53
  1009.5 4.3 broadcast_multiply_fusion
  1015.9 24.0 reduce-scatter.30.cloned.1.call-done
  1041.0 6.9 fusion.34
  1049.9 18.2 reduce-scatter.36.cloned.1.call-done
  1070.2 26.5 %reduce-scatter.38.cloned.1.call-done = bf16[1,256,4,128]{1,3,2,0:T(8,128)(2,1)} async-done(((bf16[1,1024,4,128]{1,3,2,0:T(8,128)(2,1)}), bf16[1,256,4,128]{1,3,2,0:T(8,128)(2,1)}) %reduce-scatter.38.cloned.1.call-update) | async-done | bytes 262160 | tf_op jit(solution)/shard_map/reduce_scatter | solution.py:279
  1097.7 6.9 fusion.35
  1104.7 12.0 fusion.28
  1119.3 4.6 convolution_add_fusion.4
  1124.2 3.6 fusion.133
  1127.8 9.5 convolution_add_fusion.3
  1138.6 15.2 fusion.127
  1153.8 25.5 %convolution_add_fusion.2 = f32[2048,4096]{1,0:T(8,128)} fusion(f32[2048,4096]{1,0:T(8,128)} %fusion.127, bf16[256,4096]{1,0:T(8,128)(2,1)S(1)} %copy-done.38, bf16[1,256,2048]{2,1,0:T(8,128)(2,1)S(1)} %copy-done.28), kind=kOutput, calls=%fused_computation.2 | convolution fusion | flops 4303355904 | bytes 70254592 | tf_op jit(solution)/shard_map/oye,oyk->ek/dot_general | solution.py:224
  1179.6 16.8 fusion.125
  1196.4 24.8 %convolution_add_fusion.1 = f32[2048,4096]{1,0:T(8,128)} fusion(f32[2048,4096]{1,0:T(8,128)} %fusion.125, bf16[256,4096]{1,0:T(8,128)(2,1)S(1)} %copy-done.37, bf16[1,256,2048]{2,1,0:T(8,128)(2,1)S(1)} %copy-done.28), kind=kOutput, calls=%fused_computation.1 | convolution fusion | flops 4303355904 | bytes 70254592 | tf_op jit(solution)/shard_map/oye,oyk->ek/dot_general | solution.py:230
  1222.9 14.9 fusion.114
  1237.8 25.0 %convolution_add_fusion = f32[4096,2048]{1,0:T(8,128)} fusion(f32[4096,2048]{1,0:T(8,128)} %fusion.114, bf16[256,4096]{1,0:T(8,128)(2,1)S(1)} %copy-done.35, bf16[1,1,256,2048]{3,2,1,0:T(8,128)(2,1)S(1)} %copy-done.43), kind=kOutput, calls=%fused_computation | convolution fusion | flops 4303355904 | bytes 70254592 | tf_op jit(solution)/shard_map/azc,aze->ce/dot_general | solution.py:198
  1266.8 58.0 %all-reduce.2 = (f32[2048]{0:T(1024)S(1)}, f32[2048]{0:T(1024)S(1)}) all-reduce(f32[2048]{0:T(1024)S(1)} %add.253, f32[2048]{0:T(1024)S(1)} %add.256), channel_id=25, replica_groups=mesh['fsdp'=4,'ctx'=4,'tp'=2] {'fsdp','ctx'}, use_global_device_ids=true, to_apply=%region_27.28.clone | all-reduce | flops 4096 | bytes 32768
  1325.0 4.7 all-reduce.3
  1335.0 122.3 %reduce-scatter.42.cloned.1.call-done = f32[128,2048]{1,0:T(8,128)} async-done(((f32[2048,2048]{1,0:T(8,128)}), f32[128,2048]{1,0:T(8,128)}) %reduce-scatter.42.cloned.1.call-update) | async-done | bytes 1048592 | tf_op jit(solution)/shard_map/reduce_scatter | solution.py:308
  1457.3 336.6 %reduce-scatter.46.cloned.1.call-done = f32[128,4096]{1,0:T(8,128)} async-done(((f32[2048,4096]{1,0:T(8,128)}), f32[128,4096]{1,0:T(8,128)}) %reduce-scatter.46.cloned.1.call-update) | async-done | bytes 2097168 | tf_op jit(solution)/shard_map/reduce_scatter | solution.py:311
  1793.9 336.5 %reduce-scatter.48.cloned.1.call-done = f32[128,4096]{1,0:T(8,128)} async-done(((f32[2048,4096]{1,0:T(8,128)}), f32[128,4096]{1,0:T(8,128)}) %reduce-scatter.48.cloned.1.call-update) | async-done | bytes 2097168 | tf_op jit(solution)/shard_map/reduce_scatter | solution.py:312
  2130.4 336.6 %reduce-scatter.50.cloned.1.call-done = f32[4096,128]{1,0:T(8,128)} async-done(((f32[4096,2048]{1,0:T(8,128)}), f32[4096,128]{1,0:T(8,128)}) %reduce-scatter.50.cloned.1.call-update) | async-done | bytes 2097168 | tf_op jit(solution)/shard_map/reduce_scatter | solution.py:313
  (307 shorter events, 94.5 us)
Async XLA Ops:
  7.2 36.2 %copy-start.64 = (s32[2,1,256]{2,1,0:T(1,128)S(1)}, s32[2,1,256]{2,1,0:T(1,128)}, u32[]{:S(2)}) copy-start(s32[2,1,256]{2,1,0:T(1,128)} %param.14) | copy-start | bytes 6148
  7.2 80.6 %all-gather.26.cloned.1.call-start = ((), (), s32[]{:S(2)}) async-start(), calls=%async_computation.18 | async-start | bytes 8912896 | tf_op jit(solution)/shard_map/all_gather | solution.py:48
  7.9 101.1 %all-gather.24.cloned.1.call-start = ((), (), s32[]{:S(2)}) async-start(), calls=%async_computation.17 | async-start | bytes 1572864 | tf_op jit(solution)/shard_map/all_gather | solution.py:59
  42.6 89.9 %all-gather.40.cloned.1.call-start = ((), (), s32[]{:S(2)}) async-start(), calls=%async_computation.27 | async-start | bytes 1572864 | tf_op jit(solution)/shard_map/all_gather | solution.py:59
  43.3 120.1 %all-gather.28.cloned.1.call-start = ((), (), s32[]{:S(2)}) async-start(), calls=%async_computation.19 | async-start | bytes 1310720 | tf_op jit(solution)/shard_map/all_gather | solution.py:128
  44.0 102.0 %copy-start.12 = (f32[256,128]{0,1:T(8,128)}, f32[256,128]{0,1:T(8,128)S(1)}, u32[]{:S(2)}) copy-start(f32[256,128]{0,1:T(8,128)S(1)} %get-tuple-element.63) | copy-start | bytes 393220
  44.0 102.0 %copy-start.31 = (f32[256,128]{0,1:T(8,128)}, f32[256,128]{0,1:T(8,128)S(1)}, u32[]{:S(2)}) copy-start(f32[256,128]{0,1:T(8,128)S(1)} %get-tuple-element.62) | copy-start | bytes 393220
  116.1 77.8 %all-gather.50.cloned.1.call-start = ((), (), s32[]{:S(2)}) async-start(), calls=%async_computation.42 | async-start | bytes 1310720 | tf_op jit(solution)/shard_map/all_gather | solution.py:129
  116.9 132.3 %all-gather.30.cloned.1.call-start = ((), (), s32[]{:S(2)}) async-start(), calls=%async_computation.20 | async-start | bytes 4456448 | tf_op jit(solution)/shard_map/all_gather | solution.py:50
  117.5 160.5 %all-gather.42.cloned.1.call-start = ((), (), s32[]{:S(2)}) async-start(), calls=%async_computation.28 | async-start | bytes 1310720 | tf_op jit(solution)/shard_map/all_gather | solution.py:128
  118.0 28.2 %copy-start.14 = (f32[256,128]{0,1:T(8,128)}, f32[256,128]{0,1:T(8,128)S(1)}, u32[]{:S(2)}) copy-start(f32[256,128]{0,1:T(8,128)S(1)} %get-tuple-element.65) | copy-start | bytes 393220
  118.0 28.2 %copy-start.33 = (f32[256,128]{0,1:T(8,128)}, f32[256,128]{0,1:T(8,128)S(1)}, u32[]{:S(2)}) copy-start(f32[256,128]{0,1:T(8,128)S(1)} %get-tuple-element.64) | copy-start | bytes 393220
  140.8 167.9 %all-gather.52.cloned.1.call-start = ((), (), s32[]{:S(2)}) async-start(), calls=%async_computation.43 | async-start | bytes 1310720 | tf_op jit(solution)/shard_map/all_gather | solution.py:129
  146.2 20.1 copy-start.20
  146.6 131.4 %copy-start.18 = (bf16[256,4,2,128]{0,3,2,1:T(8,128)(2,1)}, bf16[256,4,2,128]{0,3,2,1:T(8,128)(2,1)S(1)}, u32[]{:S(2)}) copy-start(bf16[256,4,2,128]{0,3,2,1:T(8,128)(2,1)S(1)} %fusion.144) | copy-start | bytes 1572868
  146.6 200.0 %reduce-scatter.18.cloned.1.call-start = ((), (), s32[]{:S(2)}) async-start(), calls=%async_computation.21 | async-start | bytes 1572864 | tf_op jit(solution)/shard_map/reduce_scatter | solution.py:63
  199.2 81.6 %copy-start.47 = (bf16[4,128,2,256]{3,1,2,0:T(8,128)(2,1)}, bf16[4,128,2,256]{3,1,2,0:T(8,128)(2,1)S(1)}, u32[]{:S(2)}) copy-start(bf16[4,128,2,256]{3,1,2,0:T(8,128)(2,1)S(1)} %fusion.56) | copy-start | bytes 1572868
  199.2 78.8 %copy-start.36 = (pred[256,1024]{0,1:T(8,128)(4,1)S(1)}, pred[256,1024]{0,1:T(8,128)(4,1)}, u32[]{:S(2)}) copy-start(pred[256,1024]{0,1:T(8,128)(4,1)} %broadcast_compare_fusion) | copy-start | bytes 786436
  253.6 100.9 %reduce-scatter.22.cloned.1.call-start = ((), (), s32[]{:S(2)}) async-start(), calls=%async_computation.29 | async-start | bytes 1572864 | tf_op jit(solution)/shard_map/reduce_scatter | solution.py:63
  314.0 40.5 %copy-start.2 = (bf16[2,1,128,2048]{3,2,1,0:T(8,128)(2,1)S(1)}, bf16[2,1,128,2048]{3,2,1,0:T(8,128)(2,1)}, u32[]{:S(2)}) copy-start(bf16[2,1,128,2048]{3,2,1,0:T(8,128)(2,1)} %param.11) | copy-start | bytes 3145732
  317.1 43.0 %copy-start.10 = (bf16[2,1,128,2048]{3,2,1,0:T(8,128)(2,1)S(1)}, bf16[2,1,128,2048]{3,2,1,0:T(8,128)(2,1)}, u32[]{:S(2)}) copy-start(bf16[2,1,128,2048]{3,2,1,0:T(8,128)(2,1)} %param.12) | copy-start | bytes 3145732
  317.1 63.1 %all-gather.32.cloned.1.call-start = ((), (), s32[]{:S(2)}) async-start(), calls=%async_computation.22 | async-start | bytes 1572864 | tf_op jit(solution)/shard_map/all_gather | solution.py:59
  346.6 586.3 %copy-start.49 = (f32[16,1,128]{2,1,0:T(1,128)}, f32[16,1,128]{2,1,0:T(1,128)S(1)}, u32[]{:S(2)}) copy-start(f32[16,1,128]{2,1,0:T(1,128)S(1)} %convert_element_type.563) | copy-start | bytes 24580
  356.1 576.8 %copy-start.58 = (f32[128]{0:T(128)}, f32[128]{0:T(128)S(1)}, u32[]{:S(2)}) copy-start(f32[128]{0:T(128)S(1)} %add_rsqrt_fusion.2) | copy-start | bytes 1540
  356.2 576.7 %copy-start.56 = (f32[128]{0:T(128)}, f32[128]{0:T(128)S(1)}, u32[]{:S(2)}) copy-start(f32[128]{0:T(128)S(1)} %add_rsqrt_fusion) | copy-start | bytes 1540
  358.7 150.9 %all-gather.34.cloned.1.call-start = ((), (), s32[]{:S(2)}) async-start(), calls=%async_computation.23 | async-start | bytes 17825792 | tf_op jit(solution)/shard_map/all_gather | solution.py:51
  359.3 277.6 %all-gather.36.cloned.1.call-start = ((), (), s32[]{:S(2)}) async-start(), calls=%async_computation.24 | async-start | bytes 17825792 | tf_op jit(solution)/shard_map/all_gather | solution.py:52
  360.1 297.9 %all-gather.54.cloned.1.call-start = ((), (), s32[]{:S(2)}) async-start(), calls=%async_computation.44 | async-start | bytes 1572864 | tf_op jit(solution)/shard_map/all_gather | solution.py:59
  361.2 429.5 %all-gather.38.cloned.1.call-start = ((), (), s32[]{:S(2)}) async-start(), calls=%async_computation.25 | async-start | bytes 17825792 | tf_op jit(solution)/shard_map/all_gather | solution.py:53
  361.8 468.2 %all-gather.44.cloned.1.call-start = ((), (), s32[]{:S(2)}) async-start(), calls=%async_computation.30 | async-start | bytes 1572864 | tf_op jit(solution)/shard_map/all_gather | solution.py:59
  362.3 491.2 %all-gather.56.cloned.1.call-start = ((), (), s32[]{:S(2)}) async-start(), calls=%async_computation.45 | async-start | bytes 1572864 | tf_op jit(solution)/shard_map/all_gather | solution.py:59
  362.9 541.5 %reduce-scatter.26.cloned.1.call-start = ((), (), s32[]{:S(2)}) async-start(), calls=%async_computation.32 | async-start | bytes 1572864 | tf_op jit(solution)/shard_map/reduce_scatter | solution.py:63
  380.2 256.7 %copy-start.24 = (bf16[1,256,2048]{2,1,0:T(8,128)(2,1)S(1)}, bf16[1,256,2048]{2,1,0:T(8,128)(2,1)}, u32[]{:S(2)}) copy-start(bf16[1,256,2048]{2,1,0:T(8,128)(2,1)} %all-gather.32.cloned.1.call-done) | copy-start | bytes 3145732
  829.9 80.0 %reduce-scatter.34.cloned.1.call-start = ((), (), s32[]{:S(2)}) async-start(), calls=%async_computation.37 | async-start | bytes 1572864 | tf_op jit(solution)/shard_map/reduce_scatter | solution.py:63
  891.8 41.1 %reduce-scatter.24.cloned.1.call-start = ((), (), s32[]{:S(2)}) async-start(), calls=%async_computation.31 | async-start | bytes 1572864 | tf_op jit(solution)/shard_map/reduce_scatter | solution.py:63
  891.9 18.0 copy-start.6
  891.9 18.0 copy-start.8
  904.2 53.5 %all-gather.46.cloned.1.call-start = ((), (), s32[]{:S(2)}) async-start(), calls=%async_computation.33 | async-start | bytes 1572864 | tf_op jit(solution)/shard_map/all_gather | solution.py:59
  912.6 49.0 %copy-start.67 = (f32[128]{0:T(128)}, f32[128]{0:T(128)S(1)}, u32[]{:S(2)}) copy-start(f32[128]{0:T(128)S(1)} %broadcast_multiply_fusion.7) | copy-start | bytes 1540
  912.6 49.0 %copy-start.65 = (f32[128]{0:T(128)}, f32[128]{0:T(128)S(1)}, u32[]{:S(2)}) copy-start(f32[128]{0:T(128)S(1)} %broadcast_multiply_fusion.5) | copy-start | bytes 1540
  936.3 45.0 %all-gather.48.cloned.1.call-start = ((), (), s32[]{:S(2)}) async-start(), calls=%async_computation.38 | async-start | bytes 1572864 | tf_op jit(solution)/shard_map/all_gather | solution.py:59
  937.0 24.8 %copy-start.45 = (bf16[1,1024,4,1,128]{1,4,3,2,0:T(8,128)(2,1)S(1)}, bf16[1,1024,4,1,128]{1,4,3,2,0:T(8,128)(2,1)}, u32[]{:S(2)}) copy-start(bf16[1,1024,4,1,128]{1,4,3,2,0:T(8,128)(2,1)} %all-gather.50.cloned.1.call-done) | copy-start | bytes 3145732
  937.1 76.8 %reduce-scatter.28.cloned.1.call-start = ((), (), s32[]{:S(2)}) async-start(), calls=%async_computation.34 | async-start | bytes 1310720 | tf_op jit(solution)/shard_map/reduce_scatter | solution.py:276
  974.5 65.4 %reduce-scatter.30.cloned.1.call-start = ((), (), s32[]{:S(2)}) async-start(), calls=%async_computation.35 | async-start | bytes 1310720 | tf_op jit(solution)/shard_map/reduce_scatter | solution.py:279
  980.5 87.6 %reduce-scatter.36.cloned.1.call-start = ((), (), s32[]{:S(2)}) async-start(), calls=%async_computation.39 | async-start | bytes 1310720 | tf_op jit(solution)/shard_map/reduce_scatter | solution.py:276
  997.9 98.7 %reduce-scatter.38.cloned.1.call-start = ((), (), s32[]{:S(2)}) async-start(), calls=%async_computation.40 | async-start | bytes 1310720 | tf_op jit(solution)/shard_map/reduce_scatter | solution.py:279
  1008.0 256.7 %reduce-scatter.32.cloned.1.call-start = ((), (), s32[]{:S(2)}) async-start(), calls=%async_computation.36 | async-start | bytes 1572864 | tf_op jit(solution)/shard_map/reduce_scatter | solution.py:63
  1047.9 216.8 %reduce-scatter.40.cloned.1.call-start = ((), (), s32[]{:S(2)}) async-start(), calls=%async_computation.41 | async-start | bytes 1572864 | tf_op jit(solution)/shard_map/reduce_scatter | solution.py:63
  1104.6 225.0 %reduce-scatter.20.cloned.1.call-start = ((), (), s32[]{:S(2)}) async-start(), calls=%async_computation.26 | async-start | bytes 1572864 | tf_op jit(solution)/shard_map/reduce_scatter | solution.py:63
  1116.7 218.3 %reduce-scatter.44.cloned.1.call-start = ((), (), s32[]{:S(2)}) async-start(), calls=%async_computation.47 | async-start | bytes 8912896 | tf_op jit(solution)/shard_map/reduce_scatter | solution.py:310
  1123.9 333.3 %reduce-scatter.42.cloned.1.call-start = ((), (), s32[]{:S(2)}) async-start(), calls=%async_computation.46 | async-start | bytes 17825792 | tf_op jit(solution)/shard_map/reduce_scatter | solution.py:308
  1137.4 656.5 %reduce-scatter.46.cloned.1.call-start = ((), (), s32[]{:S(2)}) async-start(), calls=%async_computation.48 | async-start | bytes 35651584 | tf_op jit(solution)/shard_map/reduce_scatter | solution.py:311
  1179.3 951.0 %reduce-scatter.48.cloned.1.call-start = ((), (), s32[]{:S(2)}) async-start(), calls=%async_computation.49 | async-start | bytes 35651584 | tf_op jit(solution)/shard_map/reduce_scatter | solution.py:312
  1179.6 16.8 copy-start.37
  1221.2 16.5 copy-start.43
  1221.2 1245.7 %reduce-scatter.50.cloned.1.call-start = ((), (), s32[]{:S(2)}) async-start(), calls=%async_computation.50 | async-start | bytes 35651584 | tf_op jit(solution)/shard_map/reduce_scatter | solution.py:313
  1262.8 66.9 %copy-start.9 = (bf16[1,128,2048]{2,1,0:T(8,128)(2,1)S(1)}, bf16[1,128,2048]{2,1,0:T(8,128)(2,1)}, u32[]{:S(2)}) copy-start(bf16[1,128,2048]{2,1,0:T(8,128)(2,1)} %reduce-scatter.18.cloned.1.call-done) | copy-start | bytes 1572868
  1262.8 66.9 %copy-start.11 = (bf16[2,1,128,2048]{3,2,1,0:T(8,128)(2,1)S(1)}, bf16[2,1,128,2048]{3,2,1,0:T(8,128)(2,1)}, u32[]{:S(2)}) copy-start(bf16[2,1,128,2048]{3,2,1,0:T(8,128)(2,1)} %param.12) | copy-start | bytes 3145732
  1262.8 66.9 %copy-start.50 = (f32[16,1,128]{2,1,0:T(1,128)S(1)}, f32[16,1,128]{2,1,0:T(1,128)}, u32[]{:S(2)}) copy-start(f32[16,1,128]{2,1,0:T(1,128)} %copy-done.49) | copy-start | bytes 24580
  1262.8 66.9 %copy-start.59 = (f32[128]{0:T(128)S(1)}, f32[128]{0:T(128)}, u32[]{:S(2)}) copy-start(f32[128]{0:T(128)} %copy-done.58) | copy-start | bytes 1540
  1262.8 66.9 %copy-start.68 = (f32[128]{0:T(128)S(1)}, f32[128]{0:T(128)}, u32[]{:S(2)}) copy-start(f32[128]{0:T(128)} %copy-done.67) | copy-start | bytes 1540
  1264.6 68.5 %copy-start.7 = (bf16[1,128,2048]{2,1,0:T(8,128)(2,1)S(1)}, bf16[1,128,2048]{2,1,0:T(8,128)(2,1)}, u32[]{:S(2)}) copy-start(bf16[1,128,2048]{2,1,0:T(8,128)(2,1)} %reduce-scatter.22.cloned.1.call-done) | copy-start | bytes 1572868
  1264.7 68.5 %copy-start.57 = (f32[128]{0:T(128)S(1)}, f32[128]{0:T(128)}, u32[]{:S(2)}) copy-start(f32[128]{0:T(128)} %copy-done.56) | copy-start | bytes 1540
  1264.7 68.5 %copy-start.66 = (f32[128]{0:T(128)S(1)}, f32[128]{0:T(128)}, u32[]{:S(2)}) copy-start(f32[128]{0:T(128)} %copy-done.65) | copy-start | bytes 1540
  (46 other events, 208.6 us)
Sparse Core Ops, SparseCore 0:
  10.2 77.4 all-gather.25
  89.9 19.1 all-gather.23
  111.2 21.2 all-gather.39
  134.5 28.8 all-gather.27
  165.4 28.4 all-gather.49
  195.9 53.2 all-gather.29
  251.3 26.6 all-gather.41
  280.1 28.4 all-gather.51
  311.4 19.9 reduce-scatter.17
  334.2 20.3 reduce-scatter.21
  358.9 21.3 all-gather.31
  382.3 127.3 all-gather.33
  511.8 125.0 all-gather.35
  638.9 19.0 all-gather.53
  659.9 130.7 all-gather.37
  792.7 19.0 all-gather.43
  813.7 21.2 all-gather.55
  837.8 20.3 reduce-scatter.25
  892.0 17.8 reduce-scatter.33
  912.5 20.3 reduce-scatter.23
  936.4 21.3 all-gather.45
  960.0 21.2 all-gather.47
  984.3 26.9 reduce-scatter.27
  1014.0 25.7 reduce-scatter.29
  1042.3 25.7 reduce-scatter.35
  1070.8 25.7 reduce-scatter.37
  1099.4 19.1 reduce-scatter.31
  1121.4 20.3 reduce-scatter.39
  1144.1 20.3 reduce-scatter.19
  1168.9 104.9 reduce-scatter.43
  1278.6 178.6 reduce-scatter.41
  1462.1 331.7 reduce-scatter.45
  1798.6 331.7 reduce-scatter.47
  2135.2 331.7 reduce-scatter.49
where the time goes:
time: 2480 us; the launch traced here: 2470 us
  waiting for transfers between devices  1870 us (75%)
  matrix products  382 us (15%)
  blocking collectives  123 us (5%)
  other arithmetic  44.5 us (2%)
  local copies, waits for them, and re-layouts  34.5 us (1%)
    reduce_scatter x1, waiting for transfers between devices, body(): lax.psum_scatter(grad_gate_w, ('fsdp', 'ctx'), scatter_dimension=0, tiled...  337 us
    reduce_scatter x1, waiting for transfers between devices, body(): lax.psum_scatter(grad_down_w, ('fsdp', 'ctx'), scatter_dimension=1, tiled...  337 us
    reduce_scatter x1, waiting for transfers between devices, body(): lax.psum_scatter(grad_up_w, ('fsdp', 'ctx'), scatter_dimension=0, tiled=T...  336 us
    all_gather x1, waiting for transfers between devices, fetch_weights(): lax.all_gather(w_down, ('fsdp', 'ctx'), axis=1, tiled=True)  133 us
    all_gather x1, waiting for transfers between devices, fetch_weights(): lax.all_gather(w_gate, ('fsdp', 'ctx'), axis=0, tiled=True)  129 us
    reduce_scatter x1, waiting for transfers between devices, body(): lax.psum_scatter(grad_qkv_w, ('fsdp', 'ctx'), scatter_dimension=0, tiled=...  122 us
    all_gather x1, waiting for transfers between devices, fetch_weights(): lax.all_gather(w_up, ('fsdp', 'ctx'), axis=0, tiled=True)  115 us
    all_gather x8, waiting for transfers between devices, spread_rows(): return lax.all_gather(local_rows, 'tp', axis=1, tiled=True)  72.3 us
  transfers between devices with their start and end apart: 34, of which 25 were waited for; matrix products, arithmetic and copies ran while one was open for 18% of the time, Pallas kernels for 0%

commit v1 on v0

v1 whole, which is shorter than its diff:
```python
import functools

import jax
import jax.numpy as jnp
from jax import lax
from jax.sharding import PartitionSpec as P
from jax.experimental import pallas as pl
from jax.experimental.pallas import tpu as pltpu

HEADS = 16
KV_HEADS = 8
HEAD_DIM = 128


EPS = 1e-05
THETA = 1000000.0
MASKED = -1e30


def rope_tables(position_ids):
    half_dim = HEAD_DIM // 2
    inverse = THETA ** (-(jnp.arange(half_dim, dtype=jnp.float32) * 2.0 / HEAD_DIM))
    angles = position_ids.astype(jnp.float32)[..., None] * inverse
    angles = jnp.concatenate([angles, angles], axis=-1)
    return (jnp.cos(angles), jnp.sin(angles))


def turned(values):
    half_dim = values.shape[-1] // 2
    return jnp.concatenate([-values[..., half_dim:], values[..., :half_dim]], axis=-1)


def turned_back(values):
    half_dim = values.shape[-1] // 2
    return jnp.concatenate([values[..., half_dim:], -values[..., :half_dim]], axis=-1)


def norm_rows(stream, gain_row):
    factor = lax.rsqrt(jnp.mean(stream * stream, axis=-1, keepdims=True) + EPS)
    normed = stream * factor
    return (normed, factor, (normed * gain_row).astype(jnp.bfloat16))


def groups_of(fsdp, inner):
    near = [[high * inner + low for low in range(inner)] for high in range(fsdp // inner)]
    far = [[high * inner + low for high in range(fsdp // inner)] for low in range(inner)]
    return near, far


def general_body(
    hidden_in, cotangent, block_ids, positions, attn_gain, wqkv, wo, ffn_gain, w_gate, w_up, w_down
):
    fsdp, ctx, tp = lax.axis_size("fsdp"), lax.axis_size("ctx"), lax.axis_size("tp")
    inner = KV_HEADS // tp
    outer = fsdp // inner
    near, far = groups_of(fsdp, inner)
    micro, _, rows, width = hidden_in.shape
    score_scale = HEAD_DIM ** (-0.5)
    f_at, c_at = lax.axis_index("fsdp"), lax.axis_index("ctx")
    swap = [
        ((high * inner + low) * ctx + c, (high * inner + c) * ctx + low)
        for high in range(outer)
        for low in range(inner)
        for c in range(ctx)
    ]

    def rehome(array):
        return lax.ppermute(array, ("fsdp", "ctx"), swap)

    def trade(pieces):
        return lax.all_to_all(pieces, "fsdp", 0, 0, axis_index_groups=near)

    def spread(block):
        both = lax.all_gather(block, "tp")
        return lax.all_gather(both, "fsdp", axis_index_groups=near)

    def fold(parts):
        half = lax.psum_scatter(
            parts.astype(jnp.bfloat16), "fsdp", scatter_dimension=0, axis_index_groups=near
        )
        return lax.psum_scatter(half, "tp", scatter_dimension=0).astype(jnp.float32)

    def gather_levels(pieces):
        up = lax.all_gather(pieces, "ctx")
        if outer == 1:
            return up[None]
        return lax.all_gather(up, "fsdp", axis_index_groups=far)

    def scatter_levels(pieces):
        if outer == 1:
            pieces = pieces[0]
        else:
            pieces = lax.psum_scatter(pieces, "fsdp", scatter_dimension=0, axis_index_groups=far)
        return lax.psum_scatter(pieces, "ctx", scatter_dimension=0)

    def fetch_columns(shard):
        block, cols = shard.shape
        pieces = trade(shard.reshape(block, inner, cols // inner).transpose(1, 0, 2))
        whole = gather_levels(pieces).transpose(0, 2, 1, 3, 4)
        return whole.reshape(-1, cols // inner)

    def fetch_rows(shard):
        length, block = shard.shape
        pieces = trade(shard.reshape(inner, length // inner, block))
        whole = gather_levels(pieces).transpose(3, 0, 2, 1, 4)
        return whole.reshape(length // inner, -1)

    def return_columns(grad):
        total, cols = grad.shape
        grad = grad.astype(jnp.bfloat16).reshape(outer, inner, ctx, -1, cols)
        mine = trade(scatter_levels(grad.transpose(0, 2, 1, 3, 4)))
        return mine.transpose(1, 0, 2).reshape(mine.shape[1], -1).astype(jnp.float32)

    def return_rows(grad):
        length, total = grad.shape
        grad = grad.astype(jnp.bfloat16).reshape(length, outer, inner, ctx, -1)
        mine = trade(scatter_levels(grad.transpose(1, 3, 2, 0, 4)))
        return mine.reshape(inner * length, -1).astype(jnp.float32)

    def dot(left, right, dims):
        return lax.dot_general(left, right, (dims, ((), ())), preferred_element_type=jnp.float32)

    gains = lax.all_gather(jnp.stack([attn_gain, ffn_gain]), ("fsdp", "ctx"))
    gain_attn = gains[:, 0].reshape(-1).astype(jnp.float32)
    gain_ffn = gains[:, 1].reshape(-1).astype(jnp.float32)
    span = positions.shape[2]
    ids_here = lax.dynamic_slice_in_dim(block_ids[:, 0], c_at * span, span, 1)
    marks = lax.all_gather(jnp.stack([positions[:, 0], ids_here]), ("fsdp", "ctx"))
    my_seq = f_at // inner * inner + c_at
    marks = lax.dynamic_slice_in_dim(marks, my_seq * ctx, ctx, 0)
    marks = marks.transpose(1, 2, 0, 3).reshape(2, micro, ctx * span)
    pos, ids = marks[0], marks[1]

    weight_qkv = fetch_columns(wqkv)
    weight_out = fetch_rows(wo)
    weight_gate = fetch_columns(w_gate)
    weight_up = fetch_columns(w_up)
    weight_down = fetch_rows(w_down)

    stream = rehome(hidden_in).reshape(micro * rows, width).astype(jnp.float32)
    grad_out_low = rehome(cotangent).reshape(micro * rows, width)
    grad_out = grad_out_low.astype(jnp.float32)

    def to_heads(flat):
        split = flat.reshape(inner * tp, micro, rows, -1, HEAD_DIM).transpose(1, 0, 2, 3, 4)
        return split.reshape(micro, inner * tp * rows, -1, HEAD_DIM)

    def from_heads(heads):
        split = heads.reshape(micro, inner * tp, rows, -1).transpose(1, 0, 2, 3)
        return split.reshape(inner * tp * micro * rows, -1)

    normed_one, factor_one, attn_rows = norm_rows(stream, gain_attn)
    attn_in = spread(attn_rows).reshape(-1, width)
    projected = to_heads(dot(attn_in, weight_qkv, ((1,), (0,))))
    group = HEADS // KV_HEADS
    cos_table, sin_table = rope_tables(pos)
    cos_heads, sin_heads = cos_table[:, :, None], sin_table[:, :, None]
    turning = projected[:, :, : group + 1]
    turning = (turning * cos_heads + turned(turning) * sin_heads).astype(jnp.bfloat16)
    queries, keys = turning[:, :, :group], turning[:, :, group]
    values = projected[:, :, group + 1].astype(jnp.bfloat16)
    allowed = (ids[:, None, :] <= ids[:, :, None])[:, None]
    raw = jnp.einsum("blge,bme->bglm", queries, keys, preferred_element_type=jnp.float32)
    scores = jnp.where(allowed, raw * score_scale, MASKED)
    row_max = jnp.max(scores, axis=-1, keepdims=True)
    exponent = jnp.exp(scores - row_max)
    prob = exponent / jnp.sum(exponent, axis=-1, keepdims=True)
    prob_low = prob.astype(jnp.bfloat16)
    mixed = jnp.einsum("bglm,bme->blge", prob_low, values, preferred_element_type=jnp.float32)
    mixed = from_heads(mixed.astype(jnp.bfloat16))
    out_part = dot(mixed, weight_out, ((1,), (0,)))
    stream_mid = stream + fold(out_part.reshape(inner, tp, -1, width))
    normed_two, factor_two, ffn_rows = norm_rows(stream_mid, gain_ffn)
    ffn_in = spread(ffn_rows).reshape(-1, width)
    dy = spread(grad_out_low).reshape(-1, width)

    gate_pre = dot(ffn_in, weight_gate, ((1,), (0,)))
    up_pre = dot(ffn_in, weight_up, ((1,), (0,)))
    gate_sig = jax.nn.sigmoid(gate_pre)
    gate_act = gate_pre * gate_sig
    hidden = (gate_act * up_pre).astype(jnp.bfloat16)
    grad_hidden = dot(dy, weight_down, ((1,), (1,)))
    grad_gate_pre = (
        grad_hidden * up_pre * gate_sig * (1.0 + gate_pre * (1.0 - gate_sig))
    ).astype(jnp.bfloat16)
    grad_up_pre = (grad_hidden * gate_act).astype(jnp.bfloat16)
    grad_ffn_part = dot(grad_gate_pre, weight_gate, ((1,), (1,))) + dot(
        grad_up_pre, weight_up, ((1,), (1,))
    )
    grad_ffn_in = fold(grad_ffn_part.reshape(inner, tp, -1, width))
    down_part = dot(hidden, weight_down, ((1,), (0,)))
    stream_out = stream_mid + fold(down_part.reshape(inner, tp, -1, width))
    grad_down = return_rows(dot(hidden, dy, ((0,), (0,))))
    grad_gate = return_columns(dot(ffn_in, grad_gate_pre, ((0,), (0,))))
    grad_up = return_columns(dot(ffn_in, grad_up_pre, ((0,), (0,))))

    def back_rows(grad, normed, factor, gain_row):
        grad_normed = grad * gain_row
        inner_mean = jnp.mean(grad_normed * normed, axis=-1, keepdims=True)
        return factor * (grad_normed - normed * inner_mean), jnp.sum(grad * normed, axis=0)

    mid_norm, gain_ffn_part = back_rows(grad_ffn_in, normed_two, factor_two, gain_ffn)
    grad_mid = grad_out + mid_norm
    grad_mid_low = spread(grad_mid.astype(jnp.bfloat16)).reshape(-1, width)
    grad_mixed = to_heads(dot(grad_mid_low, weight_out, ((1,), (1,))).astype(jnp.bfloat16))
    grad_wo = return_rows(dot(mixed, grad_mid_low, ((0,), (0,))))
    grad_prob = jnp.einsum("blge,bme->bglm", grad_mixed, values, preferred_element_type=jnp.float32)
    inner_prob = jnp.sum(grad_prob * prob, axis=-1, keepdims=True)
    grad_scores = (score_scale * prob * (grad_prob - inner_prob)).astype(jnp.bfloat16)
    grad_queries = jnp.einsum(
        "bglm,bme->blge", grad_scores, keys, preferred_element_type=jnp.float32
    )
    grad_keys = jnp.einsum(
        "bglm,blge->bme", grad_scores, queries, preferred_element_type=jnp.float32
    )
    grad_values = jnp.einsum(
        "bglm,blge->bme", prob_low, grad_mixed, preferred_element_type=jnp.float32
    )
    grad_turning = jnp.concatenate([grad_queries, grad_keys[:, :, None]], axis=2)
    grad_turning = grad_turning * cos_heads + turned_back(grad_turning * sin_heads)
    grad_projected = jnp.concatenate([grad_turning, grad_values[:, :, None]], axis=2)
    grad_projected = from_heads(grad_projected.astype(jnp.bfloat16))
    grad_attn_in = fold(
        dot(grad_projected, weight_qkv, ((1,), (1,))).reshape(inner, tp, -1, width)
    )
    grad_wqkv = return_columns(dot(attn_in, grad_projected, ((0,), (0,))))
    in_norm, gain_attn_part = back_rows(grad_attn_in, normed_one, factor_one, gain_attn)
    grad_in = (grad_mid + in_norm).astype(jnp.bfloat16)

    gain_parts = jnp.stack([gain_attn_part, gain_ffn_part], axis=1).reshape(fsdp * ctx, -1, 2)
    gain_sums = lax.psum_scatter(gain_parts, ("fsdp", "ctx"), scatter_dimension=0)
    gain_sums = lax.psum(gain_sums, "tp")

    def home(array):
        return rehome(array.reshape(micro, 1, rows, width))

    return (
        home(stream_out.astype(jnp.bfloat16)),
        home(grad_in),
        gain_sums[:, 0],
        grad_wqkv,
        grad_wo,
        gain_sums[:, 1],
        grad_gate,
        grad_up,
        grad_down,
    )


MESH = pl.DeviceIdType.MESH
ROWS = 128
LANES = 128
NARROW = jnp.bfloat16
WIDE = jnp.float32
HALF = HEAD_DIM // 2
SCALE = HEAD_DIM ** (-0.5)
ANYWHERE = pl.BlockSpec(memory_space=pl.ANY)


class Place:
    def __init__(self):
        f, c, t = lax.axis_index("fsdp"), lax.axis_index("ctx"), lax.axis_index("tp")
        self.f, self.c, self.t = f, c, t
        fs, fy = f + 1 - 2 * (f % 2), (f + 2) % 4
        fd = (fs + 2) % 4
        self.fs, self.fy, self.fd = fs, fy, fd
        self.c1, self.c2 = c + 1 - 2 * (c % 2), (c + 2) % 4
        self.c3 = (self.c1 + 2) % 4
        self.side, self.core, self.row = (f, c, 1 - t), (fs, c, t), (fy, c, t)
        self.cross = (fd, c, t)
        self.z1, self.z2 = (f, self.c1, t), (f, self.c2, t)
        self.swap = (c, f, t)
        self.b, self.b_side = f * 2 + t, f * 2 + 1 - t
        self.b_row, self.b_far = fy * 2 + t, fy * 2 + 1 - t
        self.b_core, self.b_core_side = fs * 2 + t, fs * 2 + 1 - t
        self.b_core_row, self.b_core_far = fd * 2 + t, fd * 2 + 1 - t


class Sent:
    def __init__(self, copy, landing):
        self.copy, self.landing = copy, landing

    def arrive(self):
        self.landing.wait_recv()

    def leave(self):
        self.copy.wait_send()


class Post:
    def __init__(self, send_sems, recv_sems, local_sems):
        self.sems = send_sems, recv_sems
        self.local_sems = local_sems
        self.n, self.n_local = 0, 0
        self.out, self.kept = [], []

    def make(self, source, target, device, lands):
        sems = dict(
            send_sem=self.sems[0].at[self.n],
            recv_sem=self.sems[1].at[self.n],
            device_id=device,
            device_id_type=MESH,
        )
        self.n += 1
        copy = pltpu.make_async_remote_copy(src_ref=source, dst_ref=target, **sems)
        landing = pltpu.make_async_remote_copy(src_ref=lands, dst_ref=lands, **sems)
        return Sent(copy, landing)

    def send(self, source, target, device, lands):
        sent = self.make(source, target, device, lands)
        sent.copy.start()
        self.out.append(sent)
        return sent

    def keep(self, source, target):
        copy = pltpu.make_async_copy(source, target, self.local_sems.at[self.n_local])
        self.n_local += 1
        copy.start()
        self.kept.append(copy)
        return copy

    def close(self):
        for sent in self.out:
            sent.leave()
        for copy in self.kept:
            copy.wait()
        self.out, self.kept = [], []


def meet(devices):
    bar = pltpu.get_barrier_semaphore()
    for device in devices:
        pl.semaphore_signal(bar, inc=1, device_id=device, device_id_type=MESH)
    pl.semaphore_wait(bar, len(devices))


class Spread:
    def __init__(self, post, at, out):
        self.post, self.at, self.out = post, at, out
        self.sent = {}

    def slot(self, block, half):
        return self.out.at[block, pl.ds(half * ROWS, ROWS)]

    def own(self, half, source):
        at, mine = self.at, self.slot(self.at.b, half)
        self.sent["side", half] = self.post.send(source, mine, at.side, self.slot(at.b_side, half))
        self.sent["row", half] = self.post.send(source, mine, at.row, self.slot(at.b_row, half))
        self.sent["core", half] = self.post.send(source, mine, at.core, self.slot(at.b_core, half))
        self.post.keep(source, mine)

    def pass_on(self, name, half, block, lands):
        here = self.slot(block, half)
        self.sent[name, half] = self.post.send(
            here, here, self.at.core, self.slot(lands, half)
        )

    def relay(self, half):
        at = self.at
        first = ("side", "row") if half == 0 else ("row", "side")
        for name in first:
            self.sent[name, half].arrive()
            block = at.b_side if name == "side" else at.b_row
            here = self.slot(block, half)
            if half == 0 and name == "side":
                self.sent["far", 0] = self.post.send(here, here, at.row, self.slot(at.b_far, 0))
            if half == 1 and name == "row":
                self.sent["far", 1] = self.post.send(here, here, at.side, self.slot(at.b_far, 1))
            lands = at.b_core_side if name == "side" else at.b_core_row
            self.pass_on("core_" + name, half, block, lands)

    def corner(self):
        for half in range(2):
            self.sent["far", half].arrive()
            self.pass_on("core_far", half, self.at.b_far, self.at.b_core_far)

    def finish(self):
        for name in ("core", "core_side", "core_row", "core_far"):
            for half in range(2):
                self.sent[name, half].arrive()


SPREAD_COPIES, SPREAD_KEPT = 14, 2


class Fold:
    copies = 10

    def __init__(self, post, at, part, scratch):
        self.post, self.at, self.part = post, at, part
        self.got, self.give, self.far, self.side, self.row, self.gx, self.gy, self.held = scratch

    @staticmethod
    def scratch(width):
        return [
            pltpu.VMEM((4, 2 * ROWS, width), NARROW),
            pltpu.VMEM((4, 2 * ROWS, width), NARROW),
            pltpu.VMEM((2, ROWS, width), NARROW),
            pltpu.VMEM((2, ROWS, width), NARROW),
            pltpu.VMEM((2, ROWS, width), NARROW),
            pltpu.VMEM((3, ROWS, width), NARROW),
            pltpu.VMEM((3, ROWS, width), NARROW),
            pltpu.VMEM((4, ROWS, width), WIDE),
        ]

    def to_core(self, slot, block):
        self.give[slot] = self.part(block).astype(NARROW)
        return self.post.send(self.give.at[slot], self.got.at[slot], self.at.core, self.got.at[slot])

    def first(self):
        at, post = self.at, self.post
        sent = self.to_core(3, at.b_core_far)
        value = self.part(at.b_far)
        sent.arrive()
        value = (value + self.got[3].astype(WIDE)).astype(NARROW)
        self.far[0] = value[:ROWS]
        self.far[1] = value[ROWS:]
        self.far_x = post.send(self.far.at[0], self.gx.at[0], at.side, self.gx.at[0])
        self.far_y = post.send(self.far.at[1], self.gy.at[0], at.row, self.gy.at[0])
        sent = self.to_core(1, at.b_core_side)
        value = self.part(at.b_side)
        sent.arrive()
        value = value + self.got[1].astype(WIDE)
        self.side[0] = value[:ROWS].astype(NARROW)
        self.held[2] = value[ROWS:]
        self.side_x = post.send(self.side.at[0], self.gx.at[1], at.side, self.gx.at[1])
        sent = self.to_core(2, at.b_core_row)
        value = self.part(at.b_row)
        sent.arrive()
        value = value + self.got[2].astype(WIDE)
        self.row[1] = value[ROWS:].astype(NARROW)
        self.held[3] = value[:ROWS]
        self.row_y = post.send(self.row.at[1], self.gy.at[1], at.row, self.gy.at[1])
        sent = self.to_core(0, at.b_core)
        value = self.part(at.b)
        sent.arrive()
        value = value + self.got[0].astype(WIDE)
        self.held[0] = value[:ROWS]
        self.held[1] = value[ROWS:]

    def second(self):
        at, post = self.at, self.post
        self.far_y.arrive()
        self.side[1] = (self.held[2] + self.gy[0].astype(WIDE)).astype(NARROW)
        self.side_b = post.send(self.side.at[1], self.gx.at[2], at.side, self.gx.at[2])
        self.far_x.arrive()
        self.row[0] = (self.held[3] + self.gx[0].astype(WIDE)).astype(NARROW)
        self.row_a = post.send(self.row.at[0], self.gy.at[2], at.row, self.gy.at[2])

    def third(self):
        self.side_x.arrive()
        self.row_y.arrive()
        self.held[0] = self.held[0] + self.gx[1].astype(WIDE)
        self.held[1] = self.held[1] + self.gy[1].astype(WIDE)
        self.row_a.arrive()
        self.held[0] = self.held[0] + self.gy[2].astype(WIDE)
        self.side_b.arrive()
        self.held[1] = self.held[1] + self.gx[2].astype(WIDE)


class Climb:
    copies, kept = 3, 1

    def __init__(self, post, at, level, out):
        self.post, self.at, self.out = post, at, out
        mine = out.at[:, at.c]
        self.far = post.send(level, mine, at.z2, out.at[:, at.c2])
        self.close = post.send(level, mine, at.z1, out.at[:, at.c1])
        post.keep(level, mine)

    def forward(self):
        at = self.at
        self.far.arrive()
        there = self.out.at[:, at.c2]
        self.last = self.post.send(there, there, at.z1, self.out.at[:, at.c3])

    def finish(self):
        self.close.arrive()
        self.last.arrive()


def call(kernel, name, outs, args, scratch, copies, kept, collective_id):
    sems = [
        pltpu.SemaphoreType.DMA((copies,)),
        pltpu.SemaphoreType.DMA((copies,)),
        pltpu.SemaphoreType.DMA((kept,)),
    ]
    n_in, n_out = len(args), len(outs)

    def inner(*refs):
        post = Post(*refs[len(refs) - 3 :])
        kernel(
            post, Place(), refs[:n_in], refs[n_in : n_in + n_out], refs[n_in + n_out : len(refs) - 3]
        )
        post.close()
        assert post.n <= copies and post.n_local <= kept, (post.n, post.n_local)

    return pl.pallas_call(
        inner,
        out_shape=outs,
        in_specs=[ANYWHERE] * n_in,
        out_specs=[ANYWHERE] * n_out,
        scratch_shapes=scratch + sems,
        compiler_params=pltpu.CompilerParams(
            collective_id=collective_id, has_side_effects=True, vmem_limit_bytes=62 << 20
        ),
        name=name,
    )(*args)


def shape(*dims, dtype=NARROW):
    return jax.ShapeDtypeStruct(dims, dtype)


def gain_row(gains_ref, which):
    return jnp.concatenate([gains_ref[i, which : which + 1, :] for i in range(16)], axis=1)


def normed_rows(values):
    factor = lax.rsqrt(jnp.mean(values * values, axis=-1, keepdims=True) + EPS)
    return values * factor, factor


def start_kernel(post, at, ins, outs, scratch):
    hidden, cot, table, marks, gains, wqkv, wo, w_gate, w_up, w_down = ins
    x_own, cot_own, attn_in, tables, all_marks, all_gains, qkv_all, out_all, gate_lvl, up_lvl, down_lvl = outs
    rows_in, rows_out, gain_buf = scratch
    f, c = at.f, at.c
    bar = pltpu.get_barrier_semaphore()
    partners = (at.side, at.core, at.row, at.cross, at.z1, at.z2)
    for device in partners:
        pl.semaphore_signal(bar, inc=1, device_id=device, device_id_type=MESH)

    @pl.when(f != c)
    def _():
        pl.semaphore_signal(bar, inc=1, device_id=at.swap, device_id_type=MESH)
        pl.semaphore_wait(bar, len(partners) + 1)

    @pl.when(f == c)
    def _():
        pl.semaphore_wait(bar, len(partners))

    moves = []

    def swap(source, target, lands):
        sent = post.make(source, target, at.swap, lands)
        local = pltpu.make_async_copy(source, target, post.local_sems.at[post.n_local])
        post.n_local += 1

        @pl.when(f != c)
        def _():
            sent.copy.start()

        @pl.when(f == c)
        def _():
            local.start()

        moves.append(sent)

        def arrive():
            @pl.when(f != c)
            def _():
                sent.landing.wait_recv()

            @pl.when(f == c)
            def _():
                local.wait()

        return arrive

    halves = [pl.ds(half * ROWS, ROWS) for half in range(2)]
    table_moved = swap(table, tables.at[c], tables.at[f])
    marks_moved = swap(marks, all_marks.at[c], all_marks.at[f])
    x_moved = [swap(hidden.at[half], rows_in.at[half], rows_in.at[half]) for half in halves]

    mine = gain_buf.at[f, c]
    post.keep(gains, mine).wait()
    post.kept.pop()
    gain_step = post.send(mine, mine, at.core, gain_buf.at[at.fs, c])
    heads = wqkv.shape[1] // 4
    span = wo.shape[0] // 4
    first = []
    for device, k, src in (
        (at.row, at.fy, at.fy),
        (at.cross, at.fd, at.fd),
        (at.core, at.fs, at.fs),
    ):
        lane = pl.ds(pl.multiple_of(k * heads, LANES), heads)
        first.append(post.send(wqkv.at[:, lane], qkv_all.at[f, c], device, qkv_all.at[src, c]))
        row = pl.ds(pl.multiple_of(k * span, LANES), span)
        first.append(post.send(wo.at[row], out_all.at[f, c], device, out_all.at[src, c]))
    lane = pl.ds(pl.multiple_of(f * heads, LANES), heads)
    post.keep(wqkv.at[:, lane], qkv_all.at[f, c]).wait()
    row = pl.ds(pl.multiple_of(f * span, LANES), span)
    post.keep(wo.at[row], out_all.at[f, c]).wait()
    post.kept = post.kept[:-2]

    gain_step.arrive()
    pair = gain_buf.at[pl.ds(f // 2 * 2, 2), c]
    gain_step = post.send(pair, pair, at.row, gain_buf.at[pl.ds(at.fy // 2 * 2, 2), c])

    for sent in first:
        sent.arrive()
    levels = []
    for out in (qkv_all, out_all):
        here, there = out.at[:, c], out.at[:, at.c2]
        far = post.send(here, here, at.z2, there)
        close = post.send(here, here, at.z1, out.at[:, at.c1])
        levels.append((far, close, there, out))

    gain_step.arrive()
    gain_step = post.send(gain_buf.at[:, c], gain_buf.at[:, c], at.z1, gain_buf.at[:, at.c1])
    gain_step.arrive()
    pair = gain_buf.at[:, pl.ds(c // 2 * 2, 2)]
    gain_step = post.send(pair, pair, at.z2, gain_buf.at[:, pl.ds(at.c2 // 2 * 2, 2)])
    gain_step.arrive()
    gain = jnp.concatenate(
        [gain_buf[i // 4, i % 4, 0:1, :] for i in range(16)], axis=1
    )
    post.keep(gain_buf, all_gains)

    spread = Spread(post, at, attn_in)
    for half in range(2):
        x_moved[half]()
        normed, _ = normed_rows(rows_in[halves[half]].astype(WIDE))
        rows_out[halves[half]] = (normed * gain).astype(NARROW)
        spread.own(half, rows_out.at[halves[half]])
        post.keep(rows_in.at[halves[half]], x_own.at[halves[half]])

    table_moved()
    marks_moved()
    small = []
    for buf in (tables, all_marks):
        here = buf.at[f]
        small.append((buf, post.send(here, here, at.core, buf.at[at.fs])))
    cot_moved = [swap(cot.at[half], cot_own.at[half], cot_own.at[half]) for half in halves]
    smaller = []
    for buf, sent in small:
        sent.arrive()
        pair = buf.at[pl.ds(f // 2 * 2, 2)]
        smaller.append(post.send(pair, pair, at.row, buf.at[pl.ds(at.fy // 2 * 2, 2)]))

    spread.relay(0)

    part = w_gate.shape[1] // 4
    chunk = part // 4
    later = []
    for device, k, src in (
        (at.row, at.fy, at.fy),
        (at.cross, at.fd, at.fd),
        (at.core, at.fs, at.fs),
        (None, f, f),
    ):
        for j in range(4):
            lane = pl.ds(pl.multiple_of(k * part + j * chunk, LANES), chunk)
            for source, target in (
                (w_gate.at[:, lane], gate_lvl),
                (w_up.at[:, lane], up_lvl),
                (w_down.at[lane], down_lvl),
            ):
                if device is None:
                    post.keep(source, target.at[j, f])
                else:
                    later.append(post.send(source, target.at[j, f], device, target.at[j, src]))

    spread.relay(1)
    forwards = []
    for far, close, there, out in levels:
        far.arrive()
        forwards.append((post.send(there, there, at.z1, out.at[:, at.c3]), close))
    spread.corner()
    for last, close in forwards:
        last.arrive()
        close.arrive()
    spread.finish()
    for sent in smaller + later:
        sent.arrive()
    for arrive in cot_moved:
        arrive()

    @pl.when(f != c)
    def _():
        for sent in moves:
            sent.copy.wait_send()


def rope(values, cos_full, sin_full):
    return values * cos_full + pltpu.roll(values, HALF, 1) * sin_full


def rope_back(values, cos_full, sin_full):
    return values * cos_full - pltpu.roll(values, HALF, 1) * sin_full


def rope_full(table):
    turned_table = pltpu.roll(table, HALF, 1)
    low = lax.broadcasted_iota(jnp.int32, table.shape, 1) < HALF
    return jnp.where(low, table, turned_table), jnp.where(low, -turned_table, table)


def mm(left, right, dims=((1,), (0,))):
    return lax.dot_general(left, right, (dims, ((), ())), preferred_element_type=WIDE)


TILE = 256


def softmax_tile(query, key, id_col, id_row):
    raw = mm(query, key, ((1,), (1,))) * SCALE
    raw = jnp.where(id_row <= id_col, raw, MASKED)
    top = jnp.max(raw, axis=-1, keepdims=True)
    exponent = jnp.exp(raw - top)
    return exponent * (1.0 / jnp.sum(exponent, axis=-1, keepdims=True))


def id_rows(marks, m, tiles):
    return jnp.concatenate([marks[i, m : m + 1, :] for i in range(tiles)], axis=1)


def attend_kernel(jobs, post, at, ins, outs, scratch):
    attn_in, qkv_all, tables_in, marks_in, cot_own = ins[:5]
    levels = jobs(ins[5:])
    queries, keys, values, mixed, dy, *climbed = outs
    rows, weight, tables, marks, q_buf, k_buf, v_buf, mix_buf = scratch
    meet((at.side, at.core, at.row, at.z1, at.z2))
    local = [
        post.keep(tables_in, tables),
        post.keep(marks_in, marks),
        post.keep(qkv_all, weight),
        post.keep(attn_in.at[:, pl.ds(0, ROWS)], rows.at[0]),
        post.keep(attn_in.at[:, pl.ds(ROWS, ROWS)], rows.at[1]),
    ]
    spread = Spread(post, at, dy)
    for half in range(2):
        spread.own(half, cot_own.at[pl.ds(half * ROWS, ROWS)])
    climbs = [Climb(post, at, level, out) for level, out in zip(levels, climbed)]
    for copy in local:
        copy.wait()
        post.kept.remove(copy)
    width = rows.shape[-1]
    columns = weight.shape[-1]
    for m in range(2):
        for i in range(4):
            here = rows[m, 2 * i : 2 * i + 2].reshape(TILE, width)
            projected = mm(here, weight[...].reshape(width, columns))
            cos_full, sin_full = rope_full(tables[i, m])
            place = pl.ds(i * TILE, TILE)
            for g in range(2):
                lane = slice(g * HEAD_DIM, (g + 1) * HEAD_DIM)
                q_buf[m, place, lane] = rope(projected[:, lane], cos_full, sin_full).astype(NARROW)
            k_buf[m, place] = rope(projected[:, 256:384], cos_full, sin_full).astype(NARROW)
            v_buf[m, place] = projected[:, 384:512].astype(NARROW)
    spread.relay(0)
    for m in range(2):
        for i in range(4):
            n = min(i + 2, 4) * TILE
            id_col = marks[i].T[:, m : m + 1]
            id_row = id_rows(marks, m, n // TILE)
            for g in range(2):
                lane = slice(g * HEAD_DIM, (g + 1) * HEAD_DIM)
                prob = softmax_tile(
                    q_buf[m, i * TILE : (i + 1) * TILE, lane], k_buf[m, :n], id_col, id_row
                )
                value = mm(prob.astype(NARROW), v_buf[m, :n]).astype(NARROW)
                for h in range(2):
                    mix_buf[2 * i + h, m * ROWS : (m + 1) * ROWS, lane] = value[
                        h * ROWS : (h + 1) * ROWS
                    ]
        if m == 0:
            spread.relay(1)
            for climb in climbs:
                climb.forward()
    for source, target in ((q_buf, queries), (k_buf, keys), (v_buf, values), (mix_buf, mixed)):
        post.keep(source, target)
    spread.corner()
    spread.finish()
    for climb in climbs:
        climb.finish()


def middle_kernel(jobs, post, at, ins, outs, scratch):
    mixed, out_all, x_own, gains_in = ins[:4]
    levels = jobs(ins[4:])
    mid_own, ffn_in, *climbed = outs
    mix_buf, weight, x_buf, gains, rows_out, *fold_scratch = scratch
    meet((at.side, at.core, at.row, at.z1, at.z2))
    local = [
        post.keep(out_all.at[i // 4, i % 4], weight.at[:, pl.ds(i * LANES, LANES)])
        for i in range(16)
    ]
    local += [post.keep(mixed, mix_buf), post.keep(x_own, x_buf), post.keep(gains_in, gains)]
    for copy in local:
        copy.wait()
        post.kept.remove(copy)
    climbs = [Climb(post, at, level, out) for level, out in zip(levels, climbed)]

    def part(block):
        return mm(mix_buf[block], weight[...])

    fold = Fold(post, at, part, fold_scratch)
    fold.first()
    fold.second()
    fold.third()
    gain = jnp.concatenate([gains[i // 4, i % 4, 1:2, :] for i in range(16)], axis=1)
    spread = Spread(post, at, ffn_in)
    for half in range(2):
        rows = pl.ds(half * ROWS, ROWS)
        value = fold.held[half] + x_buf[rows].astype(WIDE)
        fold.held[half] = value
        normed, _ = normed_rows(value)
        rows_out[half] = (normed * gain).astype(NARROW)
        spread.own(half, rows_out.at[half])
        post.keep(fold.held.at[half], mid_own.at[rows])
    spread.relay(0)
    for climb in climbs:
        climb.forward()
    spread.relay(1)
    spread.corner()
    spread.finish()
    for climb in climbs:
        climb.finish()


class Jobs:
    def __init__(self, *wanted):
        self.wanted = wanted

    def __call__(self, level_refs):
        return [level_refs[a].at[j] for a, j in self.wanted]

    def shapes(self, levels):
        return [
            jax.ShapeDtypeStruct((4, 4) + levels[a].shape[2:], NARROW) for a, j in self.wanted
        ]


def small_arrays(block_ids, positions, attn_gain, ffn_gain):
    micro, _, span = positions.shape
    cos_table, sin_table = rope_tables(positions[:, 0])
    table = jnp.concatenate([cos_table[..., :HALF], sin_table[..., :HALF]], axis=-1)
    ids = lax.dynamic_slice_in_dim(block_ids[:, 0], lax.axis_index("ctx") * span, span, 1)
    marks = jnp.zeros((8, span), WIDE).at[:micro].set(ids.astype(WIDE))
    gains = jnp.zeros((8, LANES), WIDE).at[0].set(attn_gain.astype(WIDE))
    return table, marks, gains.at[1].set(ffn_gain.astype(WIDE))


def rest_by_compiler(
    x_own, cot_own, attn_in, tables, all_marks, all_gains, qkv_all, out_all,
    queries, keys, values, mixed, dy, mid_own, ffn_in, weight_gate, weight_up, weight_down,
):
    fsdp, ctx, tp = lax.axis_size("fsdp"), lax.axis_size("ctx"), lax.axis_size("tp")
    inner = KV_HEADS // tp
    outer = fsdp // inner
    near, far = groups_of(fsdp, inner)
    micro, rows, width = 2, 128, x_own.shape[-1]
    score_scale = SCALE
    swap = [
        ((high * inner + low) * ctx + c, (high * inner + c) * ctx + low)
        for high in range(outer)
        for low in range(inner)
        for c in range(ctx)
    ]

    def rehome(array):
        return lax.ppermute(array, ("fsdp", "ctx"), swap)

    def trade(pieces):
        return lax.all_to_all(pieces, "fsdp", 0, 0, axis_index_groups=near)

    def spread(block):
        both = lax.all_gather(block, "tp")
        return lax.all_gather(both, "fsdp", axis_index_groups=near)

    def fold(parts):
        half = lax.psum_scatter(
            parts.astype(jnp.bfloat16), "fsdp", scatter_dimension=0, axis_index_groups=near
        )
        return lax.psum_scatter(half, "tp", scatter_dimension=0).astype(jnp.float32)

    def scatter_levels(pieces):
        if outer == 1:
            pieces = pieces[0]
        else:
            pieces = lax.psum_scatter(pieces, "fsdp", scatter_dimension=0, axis_index_groups=far)
        return lax.psum_scatter(pieces, "ctx", scatter_dimension=0)

    def return_columns(grad):
        total, cols = grad.shape
        grad = grad.astype(jnp.bfloat16).reshape(outer, inner, ctx, -1, cols)
        mine = trade(scatter_levels(grad.transpose(0, 2, 1, 3, 4)))
        return mine.transpose(1, 0, 2).reshape(mine.shape[1], -1).astype(jnp.float32)

    def return_rows(grad):
        length, total = grad.shape
        grad = grad.astype(jnp.bfloat16).reshape(length, outer, inner, ctx, -1)
        mine = trade(scatter_levels(grad.transpose(1, 3, 2, 0, 4)))
        return mine.reshape(inner * length, -1).astype(jnp.float32)

    def dot(left, right, dims):
        return lax.dot_general(left, right, (dims, ((), ())), preferred_element_type=jnp.float32)

    gain_attn = all_gains[:, :, 0].reshape(-1)
    gain_ffn = all_gains[:, :, 1].reshape(-1)
    ids = all_marks[:, :2].transpose(1, 0, 2).reshape(2, 1024)
    tabs = tables.transpose(1, 0, 2, 3).reshape(2, 1024, 128)
    cos_table = jnp.concatenate([tabs[..., :64]] * 2, axis=-1)
    sin_table = jnp.concatenate([tabs[..., 64:]] * 2, axis=-1)
    cos_heads, sin_heads = cos_table[:, :, None], sin_table[:, :, None]
    weight_qkv = qkv_all.reshape(width, 512)
    weight_out = out_all.transpose(2, 0, 1, 3).reshape(256, width)
    grad_out = cot_own.astype(jnp.float32)
    stream_mid = mid_own
    attn_in = attn_in.reshape(-1, width)
    mixed = mixed.reshape(-1, 256)
    dy = dy.reshape(-1, width)
    ffn_in = ffn_in.reshape(-1, width)
    queries = queries.reshape(2, 1024, 2, 128)
    normed_one, factor_one, _ = norm_rows(x_own.astype(jnp.float32), gain_attn)
    normed_two, factor_two, _ = norm_rows(stream_mid, gain_ffn)
    allowed = (ids[:, None, :] <= ids[:, :, None])[:, None]
    raw = jnp.einsum("blge,bme->bglm", queries, keys, preferred_element_type=jnp.float32)
    scores = jnp.where(allowed, raw * score_scale, MASKED)
    row_max = jnp.max(scores, axis=-1, keepdims=True)
    exponent = jnp.exp(scores - row_max)
    prob = exponent / jnp.sum(exponent, axis=-1, keepdims=True)
    prob_low = prob.astype(jnp.bfloat16)

    def to_heads(flat):
        split = flat.reshape(inner * tp, micro, rows, -1, HEAD_DIM).transpose(1, 0, 2, 3, 4)
        return split.reshape(micro, inner * tp * rows, -1, HEAD_DIM)

    def from_heads(heads):
        split = heads.reshape(micro, inner * tp, rows, -1).transpose(1, 0, 2, 3)
        return split.reshape(inner * tp * micro * rows, -1)

    gate_pre = dot(ffn_in, weight_gate, ((1,), (0,)))
    up_pre = dot(ffn_in, weight_up, ((1,), (0,)))
    gate_sig = jax.nn.sigmoid(gate_pre)
    gate_act = gate_pre * gate_sig
    hidden = (gate_act * up_pre).astype(jnp.bfloat16)
    grad_hidden = dot(dy, weight_down, ((1,), (1,)))
    grad_gate_pre = (
        grad_hidden * up_pre * gate_sig * (1.0 + gate_pre * (1.0 - gate_sig))
    ).astype(jnp.bfloat16)
    grad_up_pre = (grad_hidden * gate_act).astype(jnp.bfloat16)
    grad_ffn_part = dot(grad_gate_pre, weight_gate, ((1,), (1,))) + dot(
        grad_up_pre, weight_up, ((1,), (1,))
    )
    grad_ffn_in = fold(grad_ffn_part.reshape(inner, tp, -1, width))
    down_part = dot(hidden, weight_down, ((1,), (0,)))
    stream_out = stream_mid + fold(down_part.reshape(inner, tp, -1, width))
    grad_down = return_rows(dot(hidden, dy, ((0,), (0,))))
    grad_gate = return_columns(dot(ffn_in, grad_gate_pre, ((0,), (0,))))
    grad_up = return_columns(dot(ffn_in, grad_up_pre, ((0,), (0,))))

    def back_rows(grad, normed, factor, gain_row):
        grad_normed = grad * gain_row
        inner_mean = jnp.mean(grad_normed * normed, axis=-1, keepdims=True)
        return factor * (grad_normed - normed * inner_mean), jnp.sum(grad * normed, axis=0)

    mid_norm, gain_ffn_part = back_rows(grad_ffn_in, normed_two, factor_two, gain_ffn)
    grad_mid = grad_out + mid_norm
    grad_mid_low = spread(grad_mid.astype(jnp.bfloat16)).reshape(-1, width)
    grad_mixed = to_heads(dot(grad_mid_low, weight_out, ((1,), (1,))).astype(jnp.bfloat16))
    grad_wo = return_rows(dot(mixed, grad_mid_low, ((0,), (0,))))
    grad_prob = jnp.einsum("blge,bme->bglm", grad_mixed, values, preferred_element_type=jnp.float32)
    inner_prob = jnp.sum(grad_prob * prob, axis=-1, keepdims=True)
    grad_scores = (score_scale * prob * (grad_prob - inner_prob)).astype(jnp.bfloat16)
    grad_queries = jnp.einsum(
        "bglm,bme->blge", grad_scores, keys, preferred_element_type=jnp.float32
    )
    grad_keys = jnp.einsum(
        "bglm,blge->bme", grad_scores, queries, preferred_element_type=jnp.float32
    )
    grad_values = jnp.einsum(
        "bglm,blge->bme", prob_low, grad_mixed, preferred_element_type=jnp.float32
    )
    grad_turning = jnp.concatenate([grad_queries, grad_keys[:, :, None]], axis=2)
    grad_turning = grad_turning * cos_heads + turned_back(grad_turning * sin_heads)
    grad_projected = jnp.concatenate([grad_turning, grad_values[:, :, None]], axis=2)
    grad_projected = from_heads(grad_projected.astype(jnp.bfloat16))
    grad_attn_in = fold(
        dot(grad_projected, weight_qkv, ((1,), (1,))).reshape(inner, tp, -1, width)
    )
    grad_wqkv = return_columns(dot(attn_in, grad_projected, ((0,), (0,))))
    in_norm, gain_attn_part = back_rows(grad_attn_in, normed_one, factor_one, gain_attn)
    grad_in = (grad_mid + in_norm).astype(jnp.bfloat16)

    gain_parts = jnp.stack([gain_attn_part, gain_ffn_part], axis=1).reshape(fsdp * ctx, -1, 2)
    gain_sums = lax.psum_scatter(gain_parts, ("fsdp", "ctx"), scatter_dimension=0)
    gain_sums = lax.psum(gain_sums, "tp")

    def home(array):
        return rehome(array.reshape(micro, 1, rows, width))

    return (
        home(stream_out.astype(jnp.bfloat16)),
        home(grad_in),
        gain_sums[:, 0],
        grad_wqkv,
        grad_wo,
        gain_sums[:, 1],
        grad_gate,
        grad_up,
        grad_down,
    )


def near_body(
    hidden_in, cotangent, block_ids, positions, attn_gain, wqkv, wo, ffn_gain, w_gate, w_up, w_down
):
    micro, _, rows, width = hidden_in.shape
    own = micro * rows
    ff = w_gate.shape[1]
    chunk = ff // 16
    table, marks, gains = small_arrays(block_ids, positions, attn_gain, ffn_gain)
    (
        x_own, cot_own, attn_in, tables, all_marks, all_gains, qkv_all, out_all, gate_lvl, up_lvl, down_lvl,
    ) = call(
        start_kernel,
        "start",
        [
            shape(own, width), shape(own, width), shape(8, own, width),
            shape(4, *table.shape, dtype=WIDE), shape(4, *marks.shape, dtype=WIDE),
            shape(4, 4, *gains.shape, dtype=WIDE),
            shape(4, 4, LANES, wqkv.shape[1] // 4), shape(4, 4, wo.shape[0] // 4, LANES),
            shape(4, 4, LANES, chunk), shape(4, 4, LANES, chunk), shape(4, 4, chunk, LANES),
        ],
        (
            hidden_in.reshape(own, width), cotangent.reshape(own, width), table, marks, gains,
            wqkv, wo, w_gate, w_up, w_down,
        ),
        [pltpu.VMEM((own, width), NARROW), pltpu.VMEM((own, width), NARROW), pltpu.VMEM((4, 4, 8, LANES), WIDE)],
        80, 32, 1,
    )
    levels = (gate_lvl, up_lvl, down_lvl)
    jobs_a = Jobs((0, 0), (1, 0))
    jobs_b = Jobs((2, 0), (0, 1), (1, 1), (2, 1), (0, 2), (1, 2), (2, 2), (0, 3), (1, 3), (2, 3))
    queries, keys, values, mixed, dy, *climb_a = call(
        functools.partial(attend_kernel, jobs_a),
        "attend",
        [
            shape(2, 1024, 256), shape(2, 1024, 128), shape(2, 1024, 128), shape(8, own, 256),
            shape(8, own, width), *jobs_a.shapes(levels),
        ],
        (attn_in, qkv_all, tables, all_marks, cot_own, *levels),
        [
            pltpu.VMEM((2, 8, ROWS, width), NARROW), pltpu.VMEM(qkv_all.shape, NARROW),
            pltpu.VMEM(tables.shape, WIDE), pltpu.VMEM(all_marks.shape, WIDE),
            pltpu.VMEM((2, 1024, 256), NARROW), pltpu.VMEM((2, 1024, 128), NARROW),
            pltpu.VMEM((2, 1024, 128), NARROW), pltpu.VMEM((8, own, 256), NARROW),
        ],
        40, 24, 2,
    )
    mid_own, ffn_in, *climb_b = call(
        functools.partial(middle_kernel, jobs_b),
        "middle",
        [shape(own, width, dtype=WIDE), shape(8, own, width), *jobs_b.shapes(levels)],
        (mixed, out_all, x_own, all_gains, *levels),
        [
            pltpu.VMEM((8, own, 256), NARROW), pltpu.VMEM((256, width), NARROW),
            pltpu.VMEM((own, width), NARROW), pltpu.VMEM((4, 4, 8, LANES), WIDE),
            pltpu.VMEM((2, ROWS, width), NARROW), *Fold.scratch(width),
        ],
        60, 40, 3,
    )
    have = dict(zip(jobs_a.wanted + jobs_b.wanted, climb_a + climb_b))
    weight_gate = jnp.concatenate([have[0, j].reshape(width, chunk) for j in range(4)], axis=1)
    weight_up = jnp.concatenate([have[1, j].reshape(width, chunk) for j in range(4)], axis=1)
    weight_down = jnp.concatenate(
        [have[2, j].transpose(2, 0, 1, 3).reshape(chunk, width) for j in range(4)], axis=0
    )
    return rest_by_compiler(
        x_own, cot_own, attn_in, tables, all_marks, all_gains, qkv_all, out_all,
        queries, keys, values, mixed, dy, mid_own, ffn_in, weight_gate, weight_up, weight_down,
    )


def body(*shards):
    inner = KV_HEADS // lax.axis_size("tp")
    near = (lax.axis_size("fsdp"), lax.axis_size("ctx"), lax.axis_size("tp"), inner)
    return (near_body if near == (4, 4, 2, 4) else general_body)(*shards)


def solution(mesh):
    return jax.shard_map(
        body,
        mesh=mesh,
        in_specs=(
            P(None, "fsdp", ("ctx", "tp"), None),
            P(None, "fsdp", ("ctx", "tp"), None),
            P(None, "fsdp", None),
            P(None, "fsdp", "ctx"),
            P(("fsdp", "ctx")),
            P(("fsdp", "ctx"), "tp"),
            P("tp", ("fsdp", "ctx")),
            P(("fsdp", "ctx")),
            P(("fsdp", "ctx"), "tp"),
            P(("fsdp", "ctx"), "tp"),
            P("tp", ("fsdp", "ctx")),
        ),
        out_specs=(
            P(None, "fsdp", ("ctx", "tp"), None),
            P(None, "fsdp", ("ctx", "tp"), None),
            P(("fsdp", "ctx")),
            P(("fsdp", "ctx"), "tp"),
            P("tp", ("fsdp", "ctx")),
            P(("fsdp", "ctx")),
            P(("fsdp", "ctx"), "tp"),
            P(("fsdp", "ctx"), "tp"),
            P("tp", ("fsdp", "ctx")),
        ),
        check_vma=False,
    )
```

time: 2480 us -> 1680 us (0.68)
  waiting for transfers between devices: 1870 us -> 752 us
  Pallas kernels: 0 us -> 440 us
  matrix products: 382 us -> 211 us
  starting transfers between devices: 3.18 us -> 41.6 us
  local copies, waits for them, and re-layouts: 34.5 us -> 65.6 us
    reduce_scatter x17 -> x8, waiting for transfers between devices: 1230 us -> 294 us  [the longest x3 126 us: fold(): lax.psum_scatter(parts.astype(jnp.bfloat16), 'fsdp', scatter_dimension=0,...]
    all_gather x17 -> x2, waiting for transfers between devices: 631 us -> 73.1 us  [the longest x1 39.8 us: spread(): return lax.all_gather(both, 'fsdp', axis_index_groups=near)]
    pallas_call x0 -> x3, Pallas kernels: none -> 440 us  [call(): pl.pallas_call(inner, out_shape=outs, in_specs=[ANYWHERE] * n_in, out_spe...]
    unnamed x34 -> x12, waiting for transfers between devices: 5.78 us -> 359 us
    dot_general x42 -> x17, matrix products: 382 us -> 199 us  [the longest x13 171 us: dot(): lax.dot_general(left, right, (dims, ((), ())), preferred_element_type=jnp...]
    all_gather x2 -> x0, blocking collectives: 60 us -> none  [the longest x1 30.6 us: fetch_weights(): lax.all_gather(attn_gain, ('fsdp', 'ctx'), axis=0, tiled=True)]
    unnamed x1, blocking collectives: 58 us -> 98.1 us
    all_to_all x0 -> x5, starting transfers between devices: none -> 35.5 us  [trade(): return lax.all_to_all(pieces, 'fsdp', 0, 0, axis_index_groups=near)]
  transfers between devices with their start and end apart: 34 -> 18, of which waited for: 25 -> 12; matrix products, arithmetic and copies ran while one was open for 18% -> 9% of each run, Pallas kernels for 0% -> 0%
where the time goes in v1:
time: 1680 us; the launch traced here: 1670 us
  waiting for transfers between devices  752 us (45%)
  Pallas kernels  440 us (26%)
  matrix products  211 us (13%)
  blocking collectives  102 us (6%)
  local copies, waits for them, and re-layouts  65.6 us (4%)
  starting transfers between devices  41.6 us (2%)
  other arithmetic  40.7 us (2%)
    pallas_call x3, Pallas kernels, call(): pl.pallas_call(inner, out_shape=outs, in_specs=[ANYWHERE] * n_in, out_spe...  440 us
    unnamed x12, waiting for transfers between devices  359 us
    dot_general x13, matrix products, dot(): lax.dot_general(left, right, (dims, ((), ())), preferred_element_type=jnp...  171 us
    reduce_scatter x3, waiting for transfers between devices, fold(): lax.psum_scatter(parts.astype(jnp.bfloat16), 'fsdp', scatter_dimension=0,...  126 us
    unnamed x1, blocking collectives  98.1 us
    reduce_scatter x2, waiting for transfers between devices, scatter_levels(): return lax.psum_scatter(pieces, 'ctx', scatter_dimension=0)  91.7 us
    reduce_scatter x3, waiting for transfers between devices, fold(): return lax.psum_scatter(half, 'tp', scatter_dimension=0).astype(jnp.float32)  76.3 us
    all_gather x1, waiting for transfers between devices, spread(): return lax.all_gather(both, 'fsdp', axis_index_groups=near)  39.8 us
  transfers between devices with their start and end apart: 18, of which 12 were waited for; matrix products, arithmetic and copies ran while one was open for 9% of the time, Pallas kernels for 0%

profile of v1, /device:TPU:1, one launch (start us, length us, event | category | flops | bytes accessed | tf_op | source)
XLA Modules:
  0.0 1666.3 jit_solution(4380209430461989032)
XLA Ops:
  9.4 1.9 maximum_cosine_fusion
  13.4 211.8 %start.1 = (bf16[256,2048]{1,0:T(8,128)(2,1)}, bf16[256,2048]{1,0:T(8,128)(2,1)}, bf16[8,256,2048]{2,1,0:T(8,128)(2,1)}, f32[4,2,256,128]{3,2,1,0:T(8,128)}, f32...) custom-call(bf16[256,2048]{1,0:T(8,128)(2,1)} %bitcast.299, ...), custom_call_target="tpu_custom_call" | custom-call | tf_op jit(solution)/shard_map/start/pallas_call | solution.py:498
  225.2 52.6 %attend.1 = (bf16[2,1024,256]{2,1,0:T(8,128)(2,1)}, bf16[2,1024,128]{2,1,0:T(8,128)(2,1)}, bf16[2,1024,128]{2,1,0:T(8,128)(2,1)}, bf16[8,256,256]{2,1,0:T(8,128)...) custom-call(bf16[8,256,2048]{2,1,0:T(8,128)(2,1)} %get-tuple-element.75.ref, ...), custom_call_target="tpu_custom_call" | custom-call | tf_op jit(solution)/shard_map/attend/pallas_call | solution.py:498
  277.8 175.2 %middle.1 = (f32[256,2048]{1,0:T(8,128)}, bf16[8,256,2048]{2,1,0:T(8,128)(2,1)}, bf16[4,4,256,128]{3,2,1,0:T(8,128)(2,1)}, bf16[4,4,128,256]{3,2,1,0:T(8,128)(2,...) custom-call(bf16[8,256,256]{2,1,0:T(8,128)(2,1)} %get-tuple-element., ...), custom_call_target="tpu_custom_call" | custom-call | tf_op jit(solution)/shard_map/middle/pallas_call | solution.py:498
  454.6 1.9 copy.83
  456.4 1.9 copy.84
  458.3 2.6 copy.85
  461.0 14.6 fusion.43
  475.6 13.1 fusion.41
  488.7 22.0 %multiply_convert_fusion = (bf16[2048,1024]{1,0:T(8,128)(2,1)}, bf16[2048,1024]{1,0:T(8,128)(2,1)}, bf16[2048,1024]{1,0:T(8,128)(2,1)}) fusion(f32[2048,1024]{1,0:T(8,128)} %fusion.43, f32[2048,1024]{1,0:T(8,128)} %fusion.41, bf16[2048,2048]{1,0:T(8,128)(2,1)} %bitcast.316, bf16[256,2048]{0,1:T(8,128)(2,1)} %bitcast.289, ...), kind=kOutput, calls=%fused_computation.15 | convolution fusion | flops 8638169088 | bytes 41943040 | tf_op jit(solution)/shard_map/dot_general | solution.py:900
  510.7 15.5 fusion.42
  526.2 16.3 add_convert_fusion
  542.6 71.0 %reduce-scatter.22.cloned.1.call-done = bf16[1,2,256,2048]{3,2,1,0:T(8,128)(2,1)} async-done(((bf16[4,2,256,2048]{3,2,1,0:T(8,128)(2,1)}), bf16[1,2,256,2048]{3,2,1,0:T(8,128)(2,1)}) %reduce-scatter.22.cloned.1.call-update) | async-done | bytes 2097168 | tf_op jit(solution)/shard_map/reduce_scatter | solution.py:875
  615.4 32.3 %reduce-scatter.24.cloned.1.call-done = bf16[1,256,2048]{2,1,0:T(8,128)(2,1)} async-done(((bf16[2,256,2048]{2,1,0:T(8,128)(2,1)}), bf16[1,256,2048]{2,1,0:T(8,128)(2,1)}) %reduce-scatter.24.cloned.1.call-update) | async-done | bytes 1048592 | tf_op jit(solution)/shard_map/reduce_scatter | solution.py:878
  647.7 2.6 fusion.27
  650.9 2.9 fusion.65
  653.9 33.2 %all-gather.5.cloned.1.call-done = bf16[512,2048]{1,0:T(8,128)(2,1)} async-done(((bf16[256,2048]{1,0:T(8,128)(2,1)}), bf16[512,2048]{1,0:T(8,128)(2,1)}) %all-gather.5.cloned.1.call-update) | async-done | bytes 2097168 | tf_op jit(solution)/shard_map/all_gather | solution.py:871
  688.0 2.6 copy.88
  693.8 2.3 broadcast_compare_fusion
  696.1 11.3 fusion.69
  707.5 39.8 %all-gather.7.cloned.1.call-done = bf16[8,256,2048]{2,1,0:T(8,128)(2,1)} async-done(((bf16[2,256,2048]{2,1,0:T(8,128)(2,1)}), bf16[8,256,2048]{2,1,0:T(8,128)(2,1)}) %all-gather.7.cloned.1.call-update) | async-done | bytes 8388624 | tf_op jit(solution)/shard_map/all_gather | solution.py:872
  747.3 6.9 convolution_convert_fusion.7
  754.2 2.3 reshape.301
  756.5 2.4 copy.89
  759.0 9.7 fusion.37
  768.7 14.4 fusion.1
  783.0 12.0 fusion.3
  795.0 2.9 convolution_bitcast_fusion.1
  801.8 2.8 copy.98
  804.6 10.1 convolution_convert_fusion.1
  816.5 13.6 convolution_convert_fusion
  830.1 14.5 convolution_convert_fusion.2
  844.6 7.8 reshape.313
  852.5 5.3 copy.135
  857.8 14.1 convolution_convert_fusion.3
  872.0 5.8 convolution_convert_fusion.6
  879.9 14.3 convolution_convert_fusion.4
  894.2 10.4 convolution_convert_fusion.5
  905.3 55.2 %reduce-scatter.18.cloned.1.call-done = bf16[1,2,256,2048]{3,2,1,0:T(8,128)(2,1)} async-done(((bf16[4,2,256,2048]{3,2,1,0:T(8,128)(2,1)}), bf16[1,2,256,2048]{3,2,1,0:T(8,128)(2,1)}) %reduce-scatter.18.cloned.1.call-update) | async-done | bytes 2097168 | tf_op jit(solution)/shard_map/reduce_scatter | solution.py:875
  960.5 79.1 %reduce-scatter.32.cloned.1.call-done = bf16[1,4,1024,128]{3,2,1,0:T(8,128)(2,1)} async-done(((bf16[4,4,1024,128]{3,2,1,0:T(8,128)(2,1)}), bf16[1,4,1024,128]{3,2,1,0:T(8,128)(2,1)}) %reduce-scatter.32.cloned.1.call-update) | async-done | bytes 1048592 | tf_op jit(solution)/shard_map/reduce_scatter | solution.py:885
  1039.6 4.1 all-to-all-start.4
  1045.2 12.2 all-to-all-done.4
  1057.4 12.6 reduce-scatter.30.cloned.1.call-done
  1070.1 4.2 all-to-all-start.1
  1074.3 357.9 %all-reduce.9.cloned.1.call-done = (bf16[4,4,128,512]{3,2,0,1:T(8,128)(2,1)}, bf16[4,4,128,1024]{3,2,0,1:T(8,128)(2,1)}, bf16[4,4,128,1024]{3,2,0,1:T(8,128)(2,1)}) async-done(((bf16[4,4,128,512]{3,2,0,1:T(8,128)(2,1)}, bf16[4,4,128,1024]{3,2,0,1:T(8,128)(2,1)}, bf16[4,4,128,1024]{3,2,0,1:T(8,128)(2,1)}), (bf16[4,4,128,512]{3,2,0,1:T(8,128)(2,1)}, bf16[4,4,128,1024]{3,2,0,1:T(8,128)(2,1)}, ...) | async-done | bytes 10485776
  1434.9 1.9 constant_dynamic-slice_fusion
  1438.2 4.8 all-to-all-start
  1443.0 3.1 constant_dynamic-slice_fusion.1
  1446.1 2.3 copy.102
  1448.3 16.7 %reduce-scatter.28.cloned.1.call-done = bf16[1,256,2048]{2,1,0:T(8,128)(2,1)} async-done(((bf16[2,256,2048]{2,1,0:T(8,128)(2,1)}), bf16[1,256,2048]{2,1,0:T(8,128)(2,1)}) %reduce-scatter.28.cloned.1.call-update) | async-done | bytes 1048592 | tf_op jit(solution)/shard_map/reduce_scatter | solution.py:878
  1465.1 2.1 fusion.26
  1467.2 4.9 all-to-all-start.3
  1472.0 27.3 %reduce-scatter.20.cloned.1.call-done = bf16[1,256,2048]{2,1,0:T(8,128)(2,1)} async-done(((bf16[2,256,2048]{2,1,0:T(8,128)(2,1)}), bf16[1,256,2048]{2,1,0:T(8,128)(2,1)}) %reduce-scatter.20.cloned.1.call-update) | async-done | bytes 1048592 | tf_op jit(solution)/shard_map/reduce_scatter | solution.py:878
  1499.3 4.8 fusion.23
  1504.1 3.6 collective-permute-start
  1507.8 1.9 collective-permute-start.1
  1509.7 17.5 %all-to-all-start.2 = ((bf16[4,128,1024]{1,2,0:T(8,128)(2,1)}), bf16[4,128,1024]{1,2,0:T(8,128)(2,1)S(1)}, u32[]{:S(2)}, u32[]{:S(2)}) async-start(bf16[4,128,1024]{1,2,0:T(8,128)(2,1)} %bitcast.269), calls=%async_computation.9 | async-start | bytes 2097152 | tf_op jit(solution)/shard_map/all_to_all | solution.py:868
  1527.3 2.7 bitcast_convert_fusion
  1534.6 1.8 copy.107
  1536.4 13.5 all-to-all-done.2
  1551.8 98.1 %all-reduce.2 = f32[16,128,2]{1,2,0:T(2,128)S(1)} all-reduce(f32[16,128,2]{1,2,0:T(2,128)S(1)} %pad_maximum_fusion.15), channel_id=10, replica_groups=mesh['fsdp'=4,'ctx'=4,'tp'=2] {'fsdp','ctx'}, use_global_device_ids=true, to_apply=%region_15.16.clone | all-reduce | flops 4096 | bytes 32768
  1650.6 3.8 psum.7
  1654.9 2.3 copy.144
  1657.3 2.3 copy.145
  (148 shorter events, 34.1 us)
Async XLA Ops:
  7.2 0.7 copy-start
  7.2 606.3 %reduce-scatter.22.cloned.1.call-start = ((), (), s32[]{:S(2)}) async-start(), calls=%async_computation.15 | async-start | bytes 10485760 | tf_op jit(solution)/shard_map/reduce_scatter | solution.py:875
  12.8 0.6 copy-start.24
  454.5 34.2 %copy-start.10 = (bf16[256,4,4,128]{0,3,2,1:T(8,128)(2,1)}, bf16[256,4,4,128]{0,3,2,1:T(8,128)(2,1)S(1)}, u32[]{:S(2)}) copy-start(bf16[256,4,4,128]{0,3,2,1:T(8,128)(2,1)S(1)} %copy.82) | copy-start | bytes 3145732
  456.4 32.3 %copy-start.12 = (bf16[256,4,4,128]{0,3,2,1:T(8,128)(2,1)}, bf16[256,4,4,128]{0,3,2,1:T(8,128)(2,1)S(1)}, u32[]{:S(2)}) copy-start(bf16[256,4,4,128]{0,3,2,1:T(8,128)(2,1)S(1)} %copy.83) | copy-start | bytes 3145732
  458.3 30.4 %copy-start.14 = (bf16[256,4,4,128]{0,3,2,1:T(8,128)(2,1)}, bf16[256,4,4,128]{0,3,2,1:T(8,128)(2,1)S(1)}, u32[]{:S(2)}) copy-start(bf16[256,4,4,128]{0,3,2,1:T(8,128)(2,1)S(1)} %copy.84) | copy-start | bytes 3145732
  461.0 14.6 copy-start.27
  461.0 14.6 copy-start.29
  461.0 14.6 copy-start.31
  461.0 14.6 copy-start.33
  510.7 15.5 copy-start.28
  510.7 15.5 copy-start.30
  510.7 15.5 copy-start.32
  542.5 71.1 %copy-start.2 = (f32[256,2048]{1,0:T(8,128)S(1)}, f32[256,2048]{1,0:T(8,128)}, u32[]{:S(2)}) copy-start(f32[256,2048]{1,0:T(8,128)} %get-tuple-element.87) | copy-start | bytes 6291460
  542.5 108.4 %copy-start.5 = (bf16[256,2048]{1,0:T(8,128)(2,1)S(1)}, bf16[256,2048]{1,0:T(8,128)(2,1)}, u32[]{:S(2)}) copy-start(bf16[256,2048]{1,0:T(8,128)(2,1)} %get-tuple-element.79.refs_4_) | copy-start | bytes 3145732
  542.5 105.2 %reduce-scatter.24.cloned.1.call-start = ((), (), s32[]{:S(2)}) async-start(), calls=%async_computation.16 | async-start | bytes 3145728 | tf_op jit(solution)/shard_map/reduce_scatter | solution.py:878
  613.6 73.6 %all-gather.5.cloned.1.call-start = ((), (), s32[]{:S(2)}) async-start(), calls=%async_computation.21 | async-start | bytes 3145728 | tf_op jit(solution)/shard_map/all_gather | solution.py:871
  613.8 40.0 %copy-start.22 = (f32[256]{0:T(256)}, f32[256]{0:T(256)S(1)}, u32[]{:S(2)}) copy-start(f32[256]{0:T(256)S(1)} %add_rsqrt_fusion.1) | copy-start | bytes 3076
  615.4 38.5 %copy-start.18 = (f32[4,4,1,128]{3,2,1,0:T(1,128)}, f32[4,4,1,128]{3,2,1,0:T(1,128)S(1)}, u32[]{:S(2)}) copy-start(f32[4,4,1,128]{3,2,1,0:T(1,128)S(1)} %get-tuple-element.133) | copy-start | bytes 24580
  650.3 0.6 copy-start.25
  653.8 36.8 %copy-start.8 = (f32[4,2,256,128]{3,2,1,0:T(8,128)S(1)}, f32[4,2,256,128]{3,2,1,0:T(8,128)}, u32[]{:S(2)}) copy-start(f32[4,2,256,128]{3,2,1,0:T(8,128)} %get-tuple-element.77.refs_2_) | copy-start | bytes 3145732
  653.9 93.4 %all-gather.7.cloned.1.call-start = ((), (), s32[]{:S(2)}) async-start(), calls=%async_computation.22 | async-start | bytes 10485760 | tf_op jit(solution)/shard_map/all_gather | solution.py:872
  687.2 217.6 %reduce-scatter.26.cloned.1.call-start = ((), (), s32[]{:S(2)}) async-start(), calls=%async_computation.17 | async-start | bytes 10485760 | tf_op jit(solution)/shard_map/reduce_scatter | solution.py:875
  795.0 2.9 copy-start.17
  800.0 1.0 copy-start.16
  814.6 1.2 copy-start.11
  814.6 1.5 copy-start.13
  814.6 1.9 copy-start.15
  814.7 145.8 %reduce-scatter.18.cloned.1.call-start = ((), (), s32[]{:S(2)}) async-start(), calls=%async_computation.13 | async-start | bytes 10485760 | tf_op jit(solution)/shard_map/reduce_scatter | solution.py:875
  830.1 209.5 %reduce-scatter.32.cloned.1.call-start = ((), (), s32[]{:S(2)}) async-start(), calls=%async_computation.20 | async-start | bytes 5242880 | tf_op jit(solution)/shard_map/reduce_scatter | solution.py:885
  857.8 14.2 copy-start.6
  857.8 212.3 %reduce-scatter.30.cloned.1.call-start = ((), (), s32[]{:S(2)}) async-start(), calls=%async_computation.19 | async-start | bytes 1310720 | tf_op jit(solution)/shard_map/reduce_scatter | solution.py:885
  879.8 14.4 copy-start.9
  879.8 552.4 %all-reduce.9.cloned.1.call-start = ((), (), s32[]{:S(2)}) async-start(), calls=%async_computation.23 | async-start | bytes 20971520
  904.6 139.1 %copy-start.35 = (u32[32]{0:T(128)S(1)}, u32[32]{0:T(128)}, u32[]{:S(2)}) copy-start(u32[32]{0:T(128)} %constant.132) | copy-start | bytes 388
  904.7 139.7 %copy-start.34 = (u32[32]{0:T(128)S(1)}, u32[32]{0:T(128)}, u32[]{:S(2)}) copy-start(u32[32]{0:T(128)} %constant.128) | copy-start | bytes 388
  904.7 140.2 %copy-start.4 = (bf16[256,2048]{1,0:T(8,128)(2,1)S(1)}, bf16[256,2048]{1,0:T(8,128)(2,1)}, u32[]{:S(2)}) copy-start(bf16[256,2048]{1,0:T(8,128)(2,1)} %get-tuple-element.85.refs_2_) | copy-start | bytes 3145732
  904.7 560.4 %reduce-scatter.28.cloned.1.call-start = ((), (), s32[]{:S(2)}) async-start(), calls=%async_computation.18 | async-start | bytes 3145728 | tf_op jit(solution)/shard_map/reduce_scatter | solution.py:878
  905.3 594.0 %reduce-scatter.20.cloned.1.call-start = ((), (), s32[]{:S(2)}) async-start(), calls=%async_computation.14 | async-start | bytes 3145728 | tf_op jit(solution)/shard_map/reduce_scatter | solution.py:878
  1039.6 17.8 %all-to-all-start.4 = ((bf16[4,1024,128]{2,1,0:T(8,128)(2,1)}), bf16[4,1024,128]{2,1,0:T(8,128)(2,1)S(1)}, u32[]{:S(2)}, u32[]{:S(2)}) async-start(bf16[4,1024,128]{2,1,0:T(8,128)(2,1)} %bitcast.291), calls=%async_computation.12 | async-start | bytes 2097152 | tf_op jit(solution)/shard_map/all_to_all | solution.py:868
  1057.4 385.6 %copy-start.7 = (bf16[4,1024,128]{2,1,0:T(8,128)(2,1)}, bf16[4,1024,128]{2,1,0:T(8,128)(2,1)S(1)}, u32[]{:S(2)}) copy-start(bf16[4,1024,128]{2,1,0:T(8,128)(2,1)S(1)} %all-to-all-done.4) | copy-start | bytes 3145732
  1070.1 368.1 %all-to-all-start.1 = ((bf16[4,256,128]{2,1,0:T(8,128)(2,1)}), bf16[4,256,128]{2,1,0:T(8,128)(2,1)S(1)}, u32[]{:S(2)}, u32[]{:S(2)}) async-start(bf16[4,256,128]{2,1,0:T(8,128)(2,1)} %bitcast.301), calls=%async_computation.8 | async-start | bytes 524288 | tf_op jit(solution)/shard_map/all_to_all | solution.py:868
  1436.9 28.2 %copy-start.20 = (f32[4,4,1,128]{3,2,1,0:T(1,128)S(1)}, f32[4,4,1,128]{3,2,1,0:T(1,128)}, u32[]{:S(2)}) copy-start(f32[4,4,1,128]{3,2,1,0:T(1,128)} %get-tuple-element.132) | copy-start | bytes 24580
  1438.2 29.0 %all-to-all-start = ((bf16[4,128,512]{1,2,0:T(8,128)(2,1)}), bf16[4,128,512]{1,2,0:T(8,128)(2,1)}, u32[]{:S(2)}, u32[]{:S(2)}) async-start(bf16[4,128,512]{1,2,0:T(8,128)(2,1)} %bitcast.282), calls=%async_computation.6 | async-start | bytes 1048576 | tf_op jit(solution)/shard_map/all_to_all | solution.py:868
  1443.0 56.3 %copy-start.3 = (f32[256,2048]{1,0:T(8,128)S(1)}, f32[256,2048]{1,0:T(8,128)}, u32[]{:S(2)}) copy-start(f32[256,2048]{1,0:T(8,128)} %get-tuple-element.87) | copy-start | bytes 6291460
  1443.0 56.3 %copy-start.19 = (f32[4,4,1,128]{3,2,1,0:T(1,128)S(1)}, f32[4,4,1,128]{3,2,1,0:T(1,128)}, u32[]{:S(2)}) copy-start(f32[4,4,1,128]{3,2,1,0:T(1,128)} %copy-done.18) | copy-start | bytes 24580
  1443.0 56.3 %copy-start.23 = (f32[256]{0:T(256)S(1)}, f32[256]{0:T(256)}, u32[]{:S(2)}) copy-start(f32[256]{0:T(256)} %copy-done.22) | copy-start | bytes 3076
  1443.0 56.3 %copy-start.26 = (f32[256]{0:T(256)S(1)}, f32[256]{0:T(256)}, u32[]{:S(2)}) copy-start(f32[256]{0:T(256)} %copy-done.25) | copy-start | bytes 3076
  1467.2 42.6 %all-to-all-start.3 = ((bf16[4,128,1024]{1,2,0:T(8,128)(2,1)}), bf16[4,128,1024]{1,2,0:T(8,128)(2,1)}, u32[]{:S(2)}, u32[]{:S(2)}) async-start(bf16[4,128,1024]{1,2,0:T(8,128)(2,1)} %bitcast.270), calls=%async_computation.10 | async-start | bytes 2097152 | tf_op jit(solution)/shard_map/all_to_all | solution.py:868
  1504.1 150.8 %collective-permute-start = (bf16[2,1,128,2048]{3,2,1,0:T(8,128)(2,1)}, bf16[2,1,128,2048]{3,2,1,0:T(8,128)(2,1)}, u32[]{:S(2)}, u32[]{:S(2)}) collective-permute-start(bf16[2,1,128,2048]{3,2,1,0:T(8,128)(2,1)} %bitcast.26), channel_id=1, source_target_pairs={{0,0},{2,8},{4,16},{6,24},{8,2},{10,10},{12,18},{14,26},{16,4},{18... | collective-permute-start | bytes 3145736 | tf_op jit(solution)/shard_map/ppermute | solution.py:865
  1507.8 147.2 %collective-permute-start.1 = (bf16[2,1,128,2048]{3,2,1,0:T(8,128)(2,1)}, bf16[2,1,128,2048]{3,2,1,0:T(8,128)(2,1)}, u32[]{:S(2)}, u32[]{:S(2)}) collective-permute-start(bf16[2,1,128,2048]{3,2,1,0:T(8,128)(2,1)} %bitcast.65), channel_id=1, source_target_pairs={{0,0},{2,8},{4,16},{6,24},{8,2},{10,10},{12,18},{14,26},{16,4},{18... | collective-permute-start | bytes 3145736 | tf_op jit(solution)/shard_map/ppermute | solution.py:865
  1509.7 40.1 %all-to-all-start.2 = ((bf16[4,128,1024]{1,2,0:T(8,128)(2,1)}), bf16[4,128,1024]{1,2,0:T(8,128)(2,1)S(1)}, u32[]{:S(2)}, u32[]{:S(2)}) async-start(bf16[4,128,1024]{1,2,0:T(8,128)(2,1)} %bitcast.269), calls=%async_computation.9 | async-start | bytes 2097152 | tf_op jit(solution)/shard_map/all_to_all | solution.py:868
  1536.4 15.4 copy-start.21
  1550.0 109.6 %copy-start.1 = (s32[2,1,1024]{2,1,0:T(1,128)S(1)}, s32[2,1,1024]{2,1,0:T(1,128)}, u32[]{:S(2)}) copy-start(s32[2,1,1024]{2,1,0:T(1,128)} %param.19) | copy-start | bytes 24580
Sparse Core Ops, SparseCore 0:
  542.6 70.8 reduce-scatter.21
  615.9 31.8 reduce-scatter.23
  654.0 33.1 all-gather.4
  688.6 58.7 all-gather.6
  814.8 71.2 reduce-scatter.25
  888.7 71.6 reduce-scatter.17
  962.8 76.7 reduce-scatter.31
  1042.6 27.4 reduce-scatter.29
  1073.5 358.6 all-reduce.8
  1434.3 30.7 reduce-scatter.27
  1467.4 31.8 reduce-scatter.19

commit v2 on v1

--- a/solution.py
+++ b/solution.py
@@ -269,7 +269,8 @@
         self.side, self.core, self.row = (f, c, 1 - t), (fs, c, t), (fy, c, t)
         self.cross = (fd, c, t)
         self.z1, self.z2 = (f, self.c1, t), (f, self.c2, t)
-        self.swap = (c, f, t)
+        self.fr, self.cr = f % 2 * 2 + f // 2, c % 2 * 2 + c // 2
+        self.swap = (self.cr, self.fr, t)
         self.b, self.b_side = f * 2 + t, f * 2 + 1 - t
         self.b_row, self.b_far = fy * 2 + t, fy * 2 + 1 - t
         self.b_core, self.b_core_side = fs * 2 + t, fs * 2 + 1 - t
@@ -318,6 +319,11 @@
         copy.start()
         self.kept.append(copy)
         return copy
+
+    def settle(self, copies):
+        for copy in copies:
+            copy.wait()
+        self.kept = [kept for kept in self.kept if not any(kept is copy for copy in copies)]
 
     def close(self):
         for sent in self.out:
@@ -466,7 +472,7 @@
         mine = out.at[:, at.c]
         self.far = post.send(level, mine, at.z2, out.at[:, at.c2])
         self.close = post.send(level, mine, at.z1, out.at[:, at.c1])
-        post.keep(level, mine)
+        self.own = post.keep(level, mine)
 
     def forward(self):
         at = self.at
@@ -477,6 +483,7 @@
     def finish(self):
         self.close.arrive()
         self.last.arrive()
+        self.post.settle([self.own])
 
 
 def call(kernel, name, outs, args, scratch, copies, kept, collective_id):
@@ -521,111 +528,123 @@
     return values * factor, factor
 
 
+class Swap:
+    def __init__(self, post, at):
+        self.post, self.at, self.moves = post, at, []
+
+    def __call__(self, source, target, lands):
+        post, at = self.post, self.at
+        sent = post.make(source, target, at.swap, lands)
+        local = pltpu.make_async_copy(source, target, post.local_sems.at[post.n_local])
+        post.n_local += 1
+
+        @pl.when(at.f != at.cr)
+        def _():
+            sent.copy.start()
+
+        @pl.when(at.f == at.cr)
+        def _():
+            local.start()
+
+        self.moves.append(sent)
+
+        def arrive():
+            @pl.when(at.f != at.cr)
+            def _():
+                sent.landing.wait_recv()
+
+            @pl.when(at.f == at.cr)
+            def _():
+                local.wait()
+
+        return arrive
+
+    def finish(self):
+        @pl.when(self.at.f != self.at.cr)
+        def _():
+            for sent in self.moves:
+                sent.copy.wait_send()
+
+
+def meet_swap(at):
+    bar = pltpu.get_barrier_semaphore()
+    partners = (at.side, at.core, at.row, at.cross, at.z1, at.z2)
+    for device in partners:
+        pl.semaphore_signal(bar, inc=1, device_id=device, device_id_type=MESH)
+
+    @pl.when(at.f != at.cr)
+    def _():
+        pl.semaphore_signal(bar, inc=1, device_id=at.swap, device_id_type=MESH)
+        pl.semaphore_wait(bar, len(partners) + 1)
+
+    @pl.when(at.f == at.cr)
+    def _():
+        pl.semaphore_wait(bar, len(partners))
+
+
+HALVES = [pl.ds(half * ROWS, ROWS) for half in range(2)]
+
+
 def start_kernel(post, at, ins, outs, scratch):
     hidden, cot, table, marks, gains, wqkv, wo, w_gate, w_up, w_down = ins
     x_own, cot_own, attn_in, tables, all_marks, all_gains, qkv_all, out_all, gate_lvl, up_lvl, down_lvl = outs
     rows_in, rows_out, gain_buf = scratch
     f, c = at.f, at.c
-    bar = pltpu.get_barrier_semaphore()
-    partners = (at.side, at.core, at.row, at.cross, at.z1, at.z2)
-    for device in partners:
-        pl.semaphore_signal(bar, inc=1, device_id=device, device_id_type=MESH)
-
-    @pl.when(f != c)
-    def _():
-        pl.semaphore_signal(bar, inc=1, device_id=at.swap, device_id_type=MESH)
-        pl.semaphore_wait(bar, len(partners) + 1)
-
-    @pl.when(f == c)
-    def _():
-        pl.semaphore_wait(bar, len(partners))
-
-    moves = []
-
-    def swap(source, target, lands):
-        sent = post.make(source, target, at.swap, lands)
-        local = pltpu.make_async_copy(source, target, post.local_sems.at[post.n_local])
-        post.n_local += 1
-
-        @pl.when(f != c)
-        def _():
-            sent.copy.start()
-
-        @pl.when(f == c)
-        def _():
-            local.start()
-
-        moves.append(sent)
-
-        def arrive():
-            @pl.when(f != c)
-            def _():
-                sent.landing.wait_recv()
-
-            @pl.when(f == c)
-            def _():
-                local.wait()
-
-        return arrive
-
-    halves = [pl.ds(half * ROWS, ROWS) for half in range(2)]
-    table_moved = swap(table, tables.at[c], tables.at[f])
-    marks_moved = swap(marks, all_marks.at[c], all_marks.at[f])
-    x_moved = [swap(hidden.at[half], rows_in.at[half], rows_in.at[half]) for half in halves]
-
-    mine = gain_buf.at[f, c]
-    post.keep(gains, mine).wait()
-    post.kept.pop()
-    gain_step = post.send(mine, mine, at.core, gain_buf.at[at.fs, c])
+    meet_swap(at)
+    swap = Swap(post, at)
+    x_moved = [swap(hidden.at[half], rows_in.at[half], rows_in.at[half]) for half in HALVES]
     heads = wqkv.shape[1] // 4
     span = wo.shape[0] // 4
     first = []
-    for device, k, src in (
-        (at.row, at.fy, at.fy),
-        (at.cross, at.fd, at.fd),
-        (at.core, at.fs, at.fs),
-    ):
+    for device, k in ((at.row, at.fy), (at.cross, at.fd), (at.core, at.fs)):
         lane = pl.ds(pl.multiple_of(k * heads, LANES), heads)
-        first.append(post.send(wqkv.at[:, lane], qkv_all.at[f, c], device, qkv_all.at[src, c]))
+        first.append(post.send(wqkv.at[:, lane], qkv_all.at[f, c], device, qkv_all.at[k, c]))
         row = pl.ds(pl.multiple_of(k * span, LANES), span)
-        first.append(post.send(wo.at[row], out_all.at[f, c], device, out_all.at[src, c]))
+        first.append(post.send(wo.at[row], out_all.at[f, c], device, out_all.at[k, c]))
     lane = pl.ds(pl.multiple_of(f * heads, LANES), heads)
-    post.keep(wqkv.at[:, lane], qkv_all.at[f, c]).wait()
+    own = [post.keep(wqkv.at[:, lane], qkv_all.at[f, c])]
     row = pl.ds(pl.multiple_of(f * span, LANES), span)
-    post.keep(wo.at[row], out_all.at[f, c]).wait()
-    post.kept = post.kept[:-2]
-
-    gain_step.arrive()
+    own.append(post.keep(wo.at[row], out_all.at[f, c]))
+    table_moved = swap(table, tables.at[at.cr], tables.at[f])
+    marks_moved = swap(marks, all_marks.at[at.cr], all_marks.at[f])
+
+    mine = gain_buf.at[f, c]
+    post.settle([post.keep(gains, mine)])
+    step = post.send(mine, mine, at.core, gain_buf.at[at.fs, c])
+    step.arrive()
     pair = gain_buf.at[pl.ds(f // 2 * 2, 2), c]
-    gain_step = post.send(pair, pair, at.row, gain_buf.at[pl.ds(at.fy // 2 * 2, 2), c])
-
+    step = post.send(pair, pair, at.row, gain_buf.at[pl.ds(at.fy // 2 * 2, 2), c])
+    step.arrive()
+    step = post.send(gain_buf.at[:, c], gain_buf.at[:, c], at.z1, gain_buf.at[:, at.c1])
+    step.arrive()
+    pair = gain_buf.at[:, pl.ds(c // 2 * 2, 2)]
+    step = post.send(pair, pair, at.z2, gain_buf.at[:, pl.ds(at.c2 // 2 * 2, 2)])
+    step.arrive()
+    gain = jnp.concatenate([gain_buf[i // 4, i % 4, 0:1, :] for i in range(16)], axis=1)
+    post.keep(gain_buf, all_gains)
+
+    post.settle(own)
     for sent in first:
         sent.arrive()
+
+    spread = Spread(post, at, attn_in)
     levels = []
-    for out in (qkv_all, out_all):
-        here, there = out.at[:, c], out.at[:, at.c2]
-        far = post.send(here, here, at.z2, there)
-        close = post.send(here, here, at.z1, out.at[:, at.c1])
-        levels.append((far, close, there, out))
-
-    gain_step.arrive()
-    gain_step = post.send(gain_buf.at[:, c], gain_buf.at[:, c], at.z1, gain_buf.at[:, at.c1])
-    gain_step.arrive()
-    pair = gain_buf.at[:, pl.ds(c // 2 * 2, 2)]
-    gain_step = post.send(pair, pair, at.z2, gain_buf.at[:, pl.ds(at.c2 // 2 * 2, 2)])
-    gain_step.arrive()
-    gain = jnp.concatenate(
-        [gain_buf[i // 4, i % 4, 0:1, :] for i in range(16)], axis=1
-    )
-    post.keep(gain_buf, all_gains)
-
-    spread = Spread(post, at, attn_in)
+
+    def climb():
+        for out in (qkv_all, out_all):
+            here, there = out.at[:, c], out.at[:, at.c2]
+            far = post.send(here, here, at.z2, there)
+            close = post.send(here, here, at.z1, out.at[:, at.c1])
+            levels.append((far, close, there, out))
+
     for half in range(2):
         x_moved[half]()
-        normed, _ = normed_rows(rows_in[halves[half]].astype(WIDE))
-        rows_out[halves[half]] = (normed * gain).astype(NARROW)
-        spread.own(half, rows_out.at[halves[half]])
-        post.keep(rows_in.at[halves[half]], x_own.at[halves[half]])
+        if half == 1:
+            climb()
+        normed, _ = normed_rows(rows_in[HALVES[half]].astype(WIDE))
+        rows_out[HALVES[half]] = (normed * gain).astype(NARROW)
+        spread.own(half, rows_out.at[HALVES[half]])
+        post.keep(rows_in.at[HALVES[half]], x_own.at[HALVES[half]])
 
     table_moved()
     marks_moved()
@@ -633,7 +652,6 @@
     for buf in (tables, all_marks):
         here = buf.at[f]
         small.append((buf, post.send(here, here, at.core, buf.at[at.fs])))
-    cot_moved = [swap(cot.at[half], cot_own.at[half], cot_own.at[half]) for half in halves]
     smaller = []
     for buf, sent in small:
         sent.arrive()
@@ -641,16 +659,12 @@
         smaller.append(post.send(pair, pair, at.row, buf.at[pl.ds(at.fy // 2 * 2, 2)]))
 
     spread.relay(0)
+    spread.relay(1)
 
     part = w_gate.shape[1] // 4
     chunk = part // 4
     later = []
-    for device, k, src in (
-        (at.row, at.fy, at.fy),
-        (at.cross, at.fd, at.fd),
-        (at.core, at.fs, at.fs),
-        (None, f, f),
-    ):
+    for device, k in ((at.row, at.fy), (at.cross, at.fd), (at.core, at.fs), (None, f)):
         for j in range(4):
             lane = pl.ds(pl.multiple_of(k * part + j * chunk, LANES), chunk)
             for source, target in (
@@ -661,13 +675,13 @@
                 if device is None:
                     post.keep(source, target.at[j, f])
                 else:
-                    later.append(post.send(source, target.at[j, f], device, target.at[j, src]))
-
-    spread.relay(1)
+                    later.append(post.send(source, target.at[j, f], device, target.at[j, k]))
+
     forwards = []
     for far, close, there, out in levels:
         far.arrive()
         forwards.append((post.send(there, there, at.z1, out.at[:, at.c3]), close))
+    cot_moved = [swap(cot.at[half], cot_own.at[half], cot_own.at[half]) for half in HALVES]
     spread.corner()
     for last, close in forwards:
         last.arrive()
@@ -677,11 +691,7 @@
         sent.arrive()
     for arrive in cot_moved:
         arrive()
-
-    @pl.when(f != c)
-    def _():
-        for sent in moves:
-            sent.copy.wait_send()
+    swap.finish()
 
 
 def rope(values, cos_full, sin_full):
@@ -703,6 +713,7 @@
 
 
 TILE = 256
+QUARTER = (0, 2, 1, 3)
 
 
 def softmax_tile(query, key, id_col, id_row):
@@ -714,7 +725,7 @@
 
 
 def id_rows(marks, m, tiles):
-    return jnp.concatenate([marks[i, m : m + 1, :] for i in range(tiles)], axis=1)
+    return jnp.concatenate([marks[QUARTER[i], m : m + 1, :] for i in range(tiles)], axis=1)
 
 
 def attend_kernel(jobs, post, at, ins, outs, scratch):
@@ -734,16 +745,15 @@
     for half in range(2):
         spread.own(half, cot_own.at[pl.ds(half * ROWS, ROWS)])
     climbs = [Climb(post, at, level, out) for level, out in zip(levels, climbed)]
-    for copy in local:
-        copy.wait()
-        post.kept.remove(copy)
+    post.settle(local)
     width = rows.shape[-1]
     columns = weight.shape[-1]
     for m in range(2):
         for i in range(4):
-            here = rows[m, 2 * i : 2 * i + 2].reshape(TILE, width)
+            q = QUARTER[i]
+            here = rows[m, 2 * q : 2 * q + 2].reshape(TILE, width)
             projected = mm(here, weight[...].reshape(width, columns))
-            cos_full, sin_full = rope_full(tables[i, m])
+            cos_full, sin_full = rope_full(tables[q, m])
             place = pl.ds(i * TILE, TILE)
             for g in range(2):
                 lane = slice(g * HEAD_DIM, (g + 1) * HEAD_DIM)
@@ -754,7 +764,8 @@
     for m in range(2):
         for i in range(4):
             n = min(i + 2, 4) * TILE
-            id_col = marks[i].T[:, m : m + 1]
+            q = QUARTER[i]
+            id_col = marks[q].T[:, m : m + 1]
             id_row = id_rows(marks, m, n // TILE)
             for g in range(2):
                 lane = slice(g * HEAD_DIM, (g + 1) * HEAD_DIM)
@@ -763,7 +774,7 @@
                 )
                 value = mm(prob.astype(NARROW), v_buf[m, :n]).astype(NARROW)
                 for h in range(2):
-                    mix_buf[2 * i + h, m * ROWS : (m + 1) * ROWS, lane] = value[
+                    mix_buf[2 * q + h, m * ROWS : (m + 1) * ROWS, lane] = value[
                         h * ROWS : (h + 1) * ROWS
                     ]
         if m == 0:
@@ -789,9 +800,7 @@
         for i in range(16)
     ]
     local += [post.keep(mixed, mix_buf), post.keep(x_own, x_buf), post.keep(gains_in, gains)]
-    for copy in local:
-        copy.wait()
-        post.kept.remove(copy)
+    post.settle(local)
     climbs = [Climb(post, at, level, out) for level, out in zip(levels, climbed)]
 
     def part(block):
@@ -844,166 +853,365 @@
     return table, marks, gains.at[1].set(ffn_gain.astype(WIDE))
 
 
-def rest_by_compiler(
-    x_own, cot_own, attn_in, tables, all_marks, all_gains, qkv_all, out_all,
-    queries, keys, values, mixed, dy, mid_own, ffn_in, weight_gate, weight_up, weight_down,
-):
-    fsdp, ctx, tp = lax.axis_size("fsdp"), lax.axis_size("ctx"), lax.axis_size("tp")
-    inner = KV_HEADS // tp
-    outer = fsdp // inner
-    near, far = groups_of(fsdp, inner)
-    micro, rows, width = 2, 128, x_own.shape[-1]
-    score_scale = SCALE
-    swap = [
-        ((high * inner + low) * ctx + c, (high * inner + c) * ctx + low)
-        for high in range(outer)
-        for low in range(inner)
-        for c in range(ctx)
+def ffn_kernel(jobs, post, at, ins, outs, scratch):
+    ffn_in, dy = ins[:2]
+    ready = ins[2:8]
+    levels = jobs(ins[8:])
+    hidden, grads_pre, parts, *climbed = outs
+    x_buf, dy_buf, gate_buf, up_buf, down_buf, act, act_t, staged = scratch
+    meet((at.z1, at.z2))
+    climbs = [Climb(post, at, level, out) for level, out in zip(levels, climbed)]
+    local = [post.keep(ffn_in, x_buf), post.keep(dy, dy_buf)]
+    weights = list(ready) + list(climbed)
+
+    def load(j):
+        slot = j % 2
+        gate, up, down = weights[3 * j : 3 * j + 3]
+        copies = [post.keep(gate, gate_buf.at[slot]), post.keep(up, up_buf.at[slot])]
+        for i in range(16):
+            copies.append(
+                post.keep(down.at[i // 4, i % 4], down_buf.at[slot, :, pl.ds(i * LANES, LANES)])
+            )
+        return copies
+
+    loading = load(0)
+    post.settle(local)
+    width = x_buf.shape[-1]
+    saved = []
+    for j in range(4):
+        slot = j % 2
+        if loading is None:
+            for climb in climbs[3 * (j - 2) : 3 * (j - 1)]:
+                climb.finish()
+            loading = load(j)
+        post.settle(loading)
+        loading = load(1) if j == 0 else None
+        post.settle(saved)
+
+        def rows(i, carry):
+            x, grad = x_buf[i], dy_buf[i]
+            gate = mm(x, gate_buf[slot].reshape(width, -1))
+            up = mm(x, up_buf[slot].reshape(width, -1))
+            grad_hidden = mm(grad, down_buf[slot], ((1,), (1,)))
+            sig = 1.0 / (1.0 + jnp.exp(-gate))
+            silu = gate * sig
+            values = (
+                grad_hidden * up * sig * (1.0 + gate * (1.0 - sig)),
+                grad_hidden * silu,
+                silu * up,
+            )
+            place = pl.ds(pl.multiple_of(i * TILE, TILE), TILE)
+            for k in range(3):
+                act[k, i] = values[k].astype(NARROW)
+                act_t[k, :, place] = values[k].T.astype(NARROW)
+            return carry
+
+        lax.fori_loop(0, 8, rows, 0)
+        chunk = act.shape[-1]
+        lane = pl.ds(j * chunk, chunk)
+        saved = [
+            post.keep(act.at[0], grads_pre.at[:, :, lane]),
+            post.keep(act.at[1], grads_pre.at[:, :, pl.ds((4 + j) * chunk, chunk)]),
+            post.keep(act.at[2], hidden.at[:, :, lane]),
+        ]
+        if j < 2:
+            for climb in climbs[3 * j : 3 * j + 3]:
+                climb.forward()
+
+        def sums(n, carry):
+            place = pl.ds(pl.multiple_of(n * TILE, TILE), TILE)
+            x = x_buf[:, :, place].reshape(8 * TILE, TILE)
+            grad = dy_buf[:, :, place].reshape(8 * TILE, TILE)
+            for k in range(3):
+                value = mm(act_t[k], grad if k == 2 else x).astype(NARROW)
+                staged[k, 2 * n] = value[:, :LANES]
+                staged[k, 2 * n + 1] = value[:, LANES:]
+            return carry
+
+        lax.fori_loop(0, 8, sums, 0)
+        for k in range(3):
+            for fl in range(4):
+                saved.append(post.keep(staged.at[k, pl.ds(4 * fl, 4)], parts.at[3 * j + k, fl]))
+
+
+class Descend:
+    def __init__(self, post, at, pieces, got):
+        self.near = post.send(pieces.at[:, at.c1], got.at[0], at.z1, got.at[0])
+        self.next = post.send(pieces.at[:, at.c3], got.at[1], at.z1, got.at[1])
+
+    def finish(self):
+        self.near.arrive()
+        self.next.arrive()
+
+
+def norm_back_rows(grad, values, gain):
+    normed, factor = normed_rows(values)
+    scaled = grad * gain
+    inner_mean = jnp.mean(scaled * normed, axis=-1, keepdims=True)
+    return factor * (scaled - normed * inner_mean), jnp.sum(grad * normed, axis=0, keepdims=True)
+
+
+def back_kernel(first, count, post, at, ins, outs, scratch):
+    grads_pre, mid_own, cot_own, gains_in, parts, *weights = ins
+    grad_mid_own, grad_mid, gain_part, got = outs
+    pre_buf, weight, mid_buf, cot_buf, gains, rows_out, gain_out, *fold_scratch = scratch
+    meet((at.side, at.core, at.row, at.z1, at.z2))
+    downs = [Descend(post, at, parts.at[first + q], got.at[q]) for q in range(count)]
+    chunk = pre_buf.shape[-1] // 8
+    local = [post.keep(grads_pre, pre_buf)]
+    for a in range(2):
+        for j in range(4):
+            place = pl.ds((4 * a + j) * chunk, chunk)
+            local.append(post.keep(weights[4 * a + j], weight.at[:, :, :, place]))
+    local += [post.keep(mid_own, mid_buf), post.keep(cot_own, cot_buf), post.keep(gains_in, gains)]
+    post.settle(local)
+    width = mid_buf.shape[-1]
+
+    def part(block):
+        return mm(pre_buf[block], weight[...].reshape(width, -1), ((1,), (1,)))
+
+    fold = Fold(post, at, part, fold_scratch)
+    fold.first()
+    fold.second()
+    fold.third()
+    gain = jnp.concatenate([gains[i // 4, i % 4, 1:2, :] for i in range(16)], axis=1)
+    spread = Spread(post, at, grad_mid)
+    total = jnp.zeros((1, width), WIDE)
+    for half in range(2):
+        rows = HALVES[half]
+        back, piece = norm_back_rows(fold.held[half], mid_buf[rows], gain)
+        total = total + piece
+        value = cot_buf[rows].astype(WIDE) + back
+        fold.held[half] = value
+        rows_out[half] = value.astype(NARROW)
+        spread.own(half, rows_out.at[half])
+        post.keep(fold.held.at[half], grad_mid_own.at[rows])
+    gain_out[...] = jnp.broadcast_to(total, gain_out.shape)
+    post.keep(gain_out, gain_part)
+    spread.relay(0)
+    spread.relay(1)
+    spread.corner()
+    spread.finish()
+    for down in downs:
+        down.finish()
+
+
+def attend_back_kernel(first, count, post, at, ins, outs, scratch):
+    (
+        grad_mid, queries, keys, values, marks_in, tables_in, out_all, mixed, attn_in, hidden, mid_own, parts, *downs_in
+    ) = ins
+    grad_proj, parts_attn, hidden_out, got = outs
+    (
+        gm_buf, q_buf, k_buf, v_buf, marks, tables, weight, mix_buf, hid_buf, down_buf, gp_buf, gk_buf, gv_buf,
+        mix_t, gp_t, column, staged, mid_buf, out_buf, *fold_scratch
+    ) = scratch
+    meet((at.side, at.core, at.row, at.z1, at.z2))
+    steps = [Descend(post, at, parts.at[first + q], got.at[q]) for q in range(count)]
+
+    chunk = hid_buf.shape[-1] // 4
+    early = [post.keep(hidden, hid_buf)]
+    for j in range(4):
+        for i in range(16):
+            target = down_buf.at[pl.ds(j * chunk, chunk), pl.ds(i * LANES, LANES)]
+            early.append(post.keep(downs_in[j].at[i // 4, i % 4], target))
+    late = [
+        post.keep(source, target)
+        for source, target in (
+            (grad_mid, gm_buf), (queries, q_buf), (keys, k_buf), (values, v_buf), (marks_in, marks),
+            (tables_in, tables), (mixed, mix_buf), (mid_own, mid_buf),
+        )
     ]
-
-    def rehome(array):
-        return lax.ppermute(array, ("fsdp", "ctx"), swap)
-
-    def trade(pieces):
-        return lax.all_to_all(pieces, "fsdp", 0, 0, axis_index_groups=near)
-
-    def spread(block):
-        both = lax.all_gather(block, "tp")
-        return lax.all_gather(both, "fsdp", axis_index_groups=near)
-
-    def fold(parts):
-        half = lax.psum_scatter(
-            parts.astype(jnp.bfloat16), "fsdp", scatter_dimension=0, axis_index_groups=near
-        )
-        return lax.psum_scatter(half, "tp", scatter_dimension=0).astype(jnp.float32)
-
-    def scatter_levels(pieces):
-        if outer == 1:
-            pieces = pieces[0]
-        else:
-            pieces = lax.psum_scatter(pieces, "fsdp", scatter_dimension=0, axis_index_groups=far)
-        return lax.psum_scatter(pieces, "ctx", scatter_dimension=0)
-
-    def return_columns(grad):
-        total, cols = grad.shape
-        grad = grad.astype(jnp.bfloat16).reshape(outer, inner, ctx, -1, cols)
-        mine = trade(scatter_levels(grad.transpose(0, 2, 1, 3, 4)))
-        return mine.transpose(1, 0, 2).reshape(mine.shape[1], -1).astype(jnp.float32)
-
-    def return_rows(grad):
-        length, total = grad.shape
-        grad = grad.astype(jnp.bfloat16).reshape(length, outer, inner, ctx, -1)
-        mine = trade(scatter_levels(grad.transpose(1, 3, 2, 0, 4)))
-        return mine.reshape(inner * length, -1).astype(jnp.float32)
-
-    def dot(left, right, dims):
-        return lax.dot_general(left, right, (dims, ((), ())), preferred_element_type=jnp.float32)
-
-    gain_attn = all_gains[:, :, 0].reshape(-1)
-    gain_ffn = all_gains[:, :, 1].reshape(-1)
-    ids = all_marks[:, :2].transpose(1, 0, 2).reshape(2, 1024)
-    tabs = tables.transpose(1, 0, 2, 3).reshape(2, 1024, 128)
-    cos_table = jnp.concatenate([tabs[..., :64]] * 2, axis=-1)
-    sin_table = jnp.concatenate([tabs[..., 64:]] * 2, axis=-1)
-    cos_heads, sin_heads = cos_table[:, :, None], sin_table[:, :, None]
-    weight_qkv = qkv_all.reshape(width, 512)
-    weight_out = out_all.transpose(2, 0, 1, 3).reshape(256, width)
-    grad_out = cot_own.astype(jnp.float32)
-    stream_mid = mid_own
-    attn_in = attn_in.reshape(-1, width)
-    mixed = mixed.reshape(-1, 256)
-    dy = dy.reshape(-1, width)
-    ffn_in = ffn_in.reshape(-1, width)
-    queries = queries.reshape(2, 1024, 2, 128)
-    normed_one, factor_one, _ = norm_rows(x_own.astype(jnp.float32), gain_attn)
-    normed_two, factor_two, _ = norm_rows(stream_mid, gain_ffn)
-    allowed = (ids[:, None, :] <= ids[:, :, None])[:, None]
-    raw = jnp.einsum("blge,bme->bglm", queries, keys, preferred_element_type=jnp.float32)
-    scores = jnp.where(allowed, raw * score_scale, MASKED)
-    row_max = jnp.max(scores, axis=-1, keepdims=True)
-    exponent = jnp.exp(scores - row_max)
-    prob = exponent / jnp.sum(exponent, axis=-1, keepdims=True)
-    prob_low = prob.astype(jnp.bfloat16)
-
-    def to_heads(flat):
-        split = flat.reshape(inner * tp, micro, rows, -1, HEAD_DIM).transpose(1, 0, 2, 3, 4)
-        return split.reshape(micro, inner * tp * rows, -1, HEAD_DIM)
-
-    def from_heads(heads):
-        split = heads.reshape(micro, inner * tp, rows, -1).transpose(1, 0, 2, 3)
-        return split.reshape(inner * tp * micro * rows, -1)
-
-    gate_pre = dot(ffn_in, weight_gate, ((1,), (0,)))
-    up_pre = dot(ffn_in, weight_up, ((1,), (0,)))
-    gate_sig = jax.nn.sigmoid(gate_pre)
-    gate_act = gate_pre * gate_sig
-    hidden = (gate_act * up_pre).astype(jnp.bfloat16)
-    grad_hidden = dot(dy, weight_down, ((1,), (1,)))
-    grad_gate_pre = (
-        grad_hidden * up_pre * gate_sig * (1.0 + gate_pre * (1.0 - gate_sig))
-    ).astype(jnp.bfloat16)
-    grad_up_pre = (grad_hidden * gate_act).astype(jnp.bfloat16)
-    grad_ffn_part = dot(grad_gate_pre, weight_gate, ((1,), (1,))) + dot(
-        grad_up_pre, weight_up, ((1,), (1,))
-    )
-    grad_ffn_in = fold(grad_ffn_part.reshape(inner, tp, -1, width))
-    down_part = dot(hidden, weight_down, ((1,), (0,)))
-    stream_out = stream_mid + fold(down_part.reshape(inner, tp, -1, width))
-    grad_down = return_rows(dot(hidden, dy, ((0,), (0,))))
-    grad_gate = return_columns(dot(ffn_in, grad_gate_pre, ((0,), (0,))))
-    grad_up = return_columns(dot(ffn_in, grad_up_pre, ((0,), (0,))))
-
-    def back_rows(grad, normed, factor, gain_row):
-        grad_normed = grad * gain_row
-        inner_mean = jnp.mean(grad_normed * normed, axis=-1, keepdims=True)
-        return factor * (grad_normed - normed * inner_mean), jnp.sum(grad * normed, axis=0)
-
-    mid_norm, gain_ffn_part = back_rows(grad_ffn_in, normed_two, factor_two, gain_ffn)
-    grad_mid = grad_out + mid_norm
-    grad_mid_low = spread(grad_mid.astype(jnp.bfloat16)).reshape(-1, width)
-    grad_mixed = to_heads(dot(grad_mid_low, weight_out, ((1,), (1,))).astype(jnp.bfloat16))
-    grad_wo = return_rows(dot(mixed, grad_mid_low, ((0,), (0,))))
-    grad_prob = jnp.einsum("blge,bme->bglm", grad_mixed, values, preferred_element_type=jnp.float32)
-    inner_prob = jnp.sum(grad_prob * prob, axis=-1, keepdims=True)
-    grad_scores = (score_scale * prob * (grad_prob - inner_prob)).astype(jnp.bfloat16)
-    grad_queries = jnp.einsum(
-        "bglm,bme->blge", grad_scores, keys, preferred_element_type=jnp.float32
-    )
-    grad_keys = jnp.einsum(
-        "bglm,blge->bme", grad_scores, queries, preferred_element_type=jnp.float32
-    )
-    grad_values = jnp.einsum(
-        "bglm,blge->bme", prob_low, grad_mixed, preferred_element_type=jnp.float32
-    )
-    grad_turning = jnp.concatenate([grad_queries, grad_keys[:, :, None]], axis=2)
-    grad_turning = grad_turning * cos_heads + turned_back(grad_turning * sin_heads)
-    grad_projected = jnp.concatenate([grad_turning, grad_values[:, :, None]], axis=2)
-    grad_projected = from_heads(grad_projected.astype(jnp.bfloat16))
-    grad_attn_in = fold(
-        dot(grad_projected, weight_qkv, ((1,), (1,))).reshape(inner, tp, -1, width)
-    )
-    grad_wqkv = return_columns(dot(attn_in, grad_projected, ((0,), (0,))))
-    in_norm, gain_attn_part = back_rows(grad_attn_in, normed_one, factor_one, gain_attn)
-    grad_in = (grad_mid + in_norm).astype(jnp.bfloat16)
-
-    gain_parts = jnp.stack([gain_attn_part, gain_ffn_part], axis=1).reshape(fsdp * ctx, -1, 2)
-    gain_sums = lax.psum_scatter(gain_parts, ("fsdp", "ctx"), scatter_dimension=0)
-    gain_sums = lax.psum(gain_sums, "tp")
-
-    def home(array):
-        return rehome(array.reshape(micro, 1, rows, width))
-
-    return (
-        home(stream_out.astype(jnp.bfloat16)),
-        home(grad_in),
-        gain_sums[:, 0],
-        grad_wqkv,
-        grad_wo,
-        gain_sums[:, 1],
-        grad_gate,
-        grad_up,
-        grad_down,
-    )
+    late += [
+        post.keep(out_all.at[i // 4, i % 4], weight.at[:, pl.ds(i * LANES, LANES)])
+        for i in range(16)
+    ]
+    post.settle(early)
+    fold = Fold(post, at, lambda block: mm(hid_buf[block], down_buf[...]), fold_scratch)
+    fold.first()
+    post.settle(late)
+
+    def fetch(n):
+        place = pl.ds(n * TILE, TILE)
+        return post.keep(attn_in.at[:, :, place], column.at[n % 2])
+
+    fetched = fetch(0)
+    width = gm_buf.shape[-1]
+    for m in range(2):
+        for i in range(4):
+            q = QUARTER[i]
+            n = min(i + 2, 4) * TILE
+            place = slice(i * TILE, (i + 1) * TILE)
+            id_col = marks[q].T[:, m : m + 1]
+            id_row = id_rows(marks, m, n // TILE)
+            cos_full, sin_full = rope_full(tables[q, m])
+            rows = gm_buf[2 * q : 2 * q + 2, m * ROWS : (m + 1) * ROWS].reshape(TILE, width)
+            grad_mixed = mm(rows, weight[...], ((1,), (1,))).astype(NARROW)
+            for g in range(2):
+                lane = slice(g * HEAD_DIM, (g + 1) * HEAD_DIM)
+                query = q_buf[m, place, lane]
+                prob = softmax_tile(query, k_buf[m, :n], id_col, id_row)
+                grad = grad_mixed[:, lane]
+                grad_prob = mm(grad, v_buf[m, :n], ((1,), (1,)))
+                inner = jnp.sum(grad_prob * prob, axis=-1, keepdims=True)
+                grad_scores = (SCALE * prob * (grad_prob - inner)).astype(NARROW)
+                grad_query = mm(grad_scores, k_buf[m, :n])
+                grad_key = mm(grad_scores, query, ((0,), (0,)))
+                grad_value = mm(prob.astype(NARROW), grad, ((0,), (0,)))
+                if i == 0 and g == 0:
+                    gk_buf[:n], gv_buf[:n] = grad_key, grad_value
+                    gk_buf[n:], gv_buf[n:] = (jnp.zeros_like(gk_buf[n:]),) * 2
+                else:
+                    gk_buf[:n] = gk_buf[:n] + grad_key
+                    gv_buf[:n] = gv_buf[:n] + grad_value
+                done = rope_back(grad_query, cos_full, sin_full).astype(NARROW)
+                for h in range(2):
+                    gp_buf[2 * q + h, m * ROWS : (m + 1) * ROWS, lane] = done[h * ROWS : (h + 1) * ROWS]
+        for i in range(4):
+            q = QUARTER[i]
+            place = slice(i * TILE, (i + 1) * TILE)
+            cos_full, sin_full = rope_full(tables[q, m])
+            done = (
+                rope_back(gk_buf[place], cos_full, sin_full).astype(NARROW),
+                gv_buf[place].astype(NARROW),
+            )
+            for k in range(2):
+                lane = slice((2 + k) * HEAD_DIM, (3 + k) * HEAD_DIM)
+                for h in range(2):
+                    gp_buf[2 * q + h, m * ROWS : (m + 1) * ROWS, lane] = done[k][h * ROWS : (h + 1) * ROWS]
+        if m == 0:
+            fold.second()
+    post.keep(gp_buf, grad_proj)
+    fold.third()
+    for half in range(2):
+        out_buf[HALVES[half]] = (fold.held[half] + mid_buf[HALVES[half]]).astype(NARROW)
+    post.keep(out_buf, hidden_out)
+    for i in range(8):
+        place = slice(i * TILE, (i + 1) * TILE)
+        mix_t[:, place] = mix_buf[i].astype(WIDE).T.astype(NARROW)
+        gp_t[:, place] = gp_buf[i].astype(WIDE).T.astype(NARROW)
+    span = mix_t.shape[0]
+    for n in range(8):
+        post.settle([fetched])
+        if n < 7:
+            fetched = fetch(n + 1)
+        place = slice(n * TILE, (n + 1) * TILE)
+        value = mm(mix_t[...], gm_buf[:, :, place].reshape(8 * TILE, TILE)).astype(NARROW)
+        other = mm(gp_t[...], column[n % 2].reshape(8 * TILE, TILE)).astype(NARROW)
+        for h in range(2):
+            block = 2 * n + h
+            lane = slice(h * LANES, (h + 1) * LANES)
+            staged[block // 4, block % 4, :span] = value[:, lane]
+            staged[block // 4, block % 4, span:] = other[:, lane]
+    post.keep(staged, parts_attn)
+    for step in steps:
+        step.finish()
+
+
+def end_kernel(post, at, ins, outs, scratch):
+    (
+        grad_proj, qkv_all, x_own, gains_in, grad_mid_own, hidden_out, gain_ffn_part, parts, got_a, got_b, parts_attn
+    ) = ins
+    out_home, grad_home, gain_sums, ffn_sums, attn_sums = outs
+    (
+        gp_buf, weight, x_buf, gains, mid_buf, rows_out, gain_buf, gain_got,
+        own_ffn, far_ffn, one_ffn, two_ffn, end_ffn, own_attn, far_attn, got_attn, end_attn, *fold_scratch
+    ) = scratch
+    f, c = at.f, at.c
+    meet_swap(at)
+    step_attn = Descend(post, at, parts_attn, got_attn)
+    swap = Swap(post, at)
+    moved = [swap(hidden_out.at[half], out_home.at[half], out_home.at[half]) for half in HALVES]
+
+    n_a = got_a.shape[0]
+    n_all = parts.shape[0]
+    a, b = pl.ds(0, n_a), pl.ds(n_a, n_all - n_a)
+    sums = [
+        post.keep(parts.at[:, :, at.c2], far_ffn),
+        post.keep(got_a.at[:, 1], two_ffn.at[a]),
+        post.keep(got_b.at[:, 1], two_ffn.at[b]),
+    ]
+    fold_in = [
+        post.keep(grad_proj, gp_buf), post.keep(qkv_all, weight), post.keep(x_own, x_buf),
+        post.keep(gains_in, gains), post.keep(grad_mid_own, mid_buf),
+        post.keep(gain_ffn_part, gain_buf),
+    ]
+    later = [
+        post.keep(parts.at[:, :, c], own_ffn),
+        post.keep(got_a.at[:, 0], one_ffn.at[a]),
+        post.keep(got_b.at[:, 0], one_ffn.at[b]),
+        post.keep(parts_attn.at[:, c], own_attn), post.keep(parts_attn.at[:, at.c2], far_attn),
+    ]
+    post.settle(sums)
+
+    def add(left, right):
+        return (left.astype(WIDE) + right.astype(WIDE)).astype(NARROW)
+
+    def add_far(q, carry):
+        far_ffn[q] = add(far_ffn[q], two_ffn[q])
+        return carry
+
+    lax.fori_loop(0, n_all, add_far, 0)
+    far_sent = post.send(far_ffn, end_ffn, at.z2, end_ffn)
+    post.settle(fold_in)
+    width = x_buf.shape[-1]
+
+    def part(block):
+        return mm(gp_buf[block], weight[...].reshape(width, -1), ((1,), (1,)))
+
+    fold = Fold(post, at, part, fold_scratch)
+    fold.first()
+    fold.second()
+    fold.third()
+    gain = jnp.concatenate([gains[i // 4, i % 4, 0:1, :] for i in range(16)], axis=1)
+    total = jnp.zeros((1, width), WIDE)
+    for half in range(2):
+        rows = HALVES[half]
+        back, piece = norm_back_rows(fold.held[half], x_buf[rows].astype(WIDE), gain)
+        total = total + piece
+        rows_out[rows] = (mid_buf[rows] + back).astype(NARROW)
+        moved.append(swap(rows_out.at[rows], grad_home.at[rows], grad_home.at[rows]))
+    gain_buf[0:1] = total
+    post.settle(later)
+    step_attn.finish()
+    for k in range(4):
+        far_attn[k] = add(far_attn[k], got_attn[1, k])
+    far_attn_sent = post.send(far_attn, end_attn, at.z2, end_attn)
+    for k, device in enumerate((at.core, at.row, at.side, at.z1, at.z2)):
+        gain_sent = post.send(gain_buf, gain_got.at[k], device, gain_got.at[k])
+        gain_sent.arrive()
+        gain_sent.leave()
+        post.out.pop()
+        gain_buf[...] = gain_buf[...] + gain_got[k]
+    place = pl.ds(pl.multiple_of((f * 4 + c) * LANES, LANES), LANES)
+    post.keep(gain_buf.at[:, place], gain_sums)
+
+    far_sent.arrive()
+
+    def add_own(q, carry):
+        value = own_ffn[q].astype(WIDE) + one_ffn[q].astype(WIDE) + end_ffn[q].astype(WIDE)
+        own_ffn[q] = value.astype(NARROW)
+        return carry
+
+    lax.fori_loop(0, n_all, add_own, 0)
+    trades = []
+    places = ((at.row, at.fy), (at.cross, at.fd), (at.core, at.fs))
+
+    def trade(mine, out):
+        post.keep(mine(f), out.at[f])
+        for device, k in places:
+            trades.append(post.send(mine(k), out.at[f], device, out.at[k]))
+
+    trade(lambda k: own_ffn.at[:, k], ffn_sums)
+    far_attn_sent.arrive()
+    for k in range(4):
+        value = own_attn[k].astype(WIDE) + got_attn[0, k].astype(WIDE) + end_attn[k].astype(WIDE)
+        own_attn[k] = value.astype(NARROW)
+    trade(lambda k: own_attn.at[k], attn_sums)
+    for sent in trades:
+        sent.arrive()
+    for arrive in moved:
+        arrive()
+    swap.finish()
 
 
 def near_body(
@@ -1035,7 +1243,8 @@
     )
     levels = (gate_lvl, up_lvl, down_lvl)
     jobs_a = Jobs((0, 0), (1, 0))
-    jobs_b = Jobs((2, 0), (0, 1), (1, 1), (2, 1), (0, 2), (1, 2), (2, 2), (0, 3), (1, 3), (2, 3))
+    jobs_b = Jobs((2, 0), (0, 1), (1, 1), (2, 1))
+    jobs_c = Jobs(*((a, j) for j in (2, 3) for a in range(3)))
     queries, keys, values, mixed, dy, *climb_a = call(
         functools.partial(attend_kernel, jobs_a),
         "attend",
@@ -1065,14 +1274,105 @@
         60, 40, 3,
     )
     have = dict(zip(jobs_a.wanted + jobs_b.wanted, climb_a + climb_b))
-    weight_gate = jnp.concatenate([have[0, j].reshape(width, chunk) for j in range(4)], axis=1)
-    weight_up = jnp.concatenate([have[1, j].reshape(width, chunk) for j in range(4)], axis=1)
-    weight_down = jnp.concatenate(
-        [have[2, j].transpose(2, 0, 1, 3).reshape(chunk, width) for j in range(4)], axis=0
+    hidden, grads_pre, parts, *climb_c = call(
+        functools.partial(ffn_kernel, jobs_c),
+        "ffn",
+        [
+            shape(8, own, ff // 4), shape(8, own, ff // 2), shape(12, 4, 4, chunk, LANES),
+            *jobs_c.shapes(levels),
+        ],
+        (ffn_in, dy, *(have[a, j] for j in range(2) for a in range(3)), *levels),
+        [
+            pltpu.VMEM((8, own, width), NARROW), pltpu.VMEM((8, own, width), NARROW),
+            pltpu.VMEM((2, 4, 4, LANES, chunk), NARROW), pltpu.VMEM((2, 4, 4, LANES, chunk), NARROW),
+            pltpu.VMEM((2, chunk, width), NARROW), pltpu.VMEM((3, 8, own, chunk), NARROW),
+            pltpu.VMEM((3, chunk, 8 * own), NARROW), pltpu.VMEM((3, 16, chunk, LANES), NARROW),
+        ],
+        24, 160, 4,
     )
-    return rest_by_compiler(
-        x_own, cot_own, attn_in, tables, all_marks, all_gains, qkv_all, out_all,
-        queries, keys, values, mixed, dy, mid_own, ffn_in, weight_gate, weight_up, weight_down,
+    have.update(zip(jobs_c.wanted, climb_c))
+    count_a = 7
+    fold_scratch = Fold.scratch(width)
+    grad_mid_own, grad_mid, gain_ffn_part, got_a = call(
+        functools.partial(back_kernel, 0, count_a),
+        "back",
+        [
+            shape(own, width, dtype=WIDE), shape(8, own, width), shape(8, width, dtype=WIDE),
+            shape(count_a, 2, 4, chunk, LANES),
+        ],
+        (
+            grads_pre, mid_own, cot_own, all_gains, parts,
+            *(have[a, j] for a in range(2) for j in range(4)),
+        ),
+        [
+            pltpu.VMEM((8, own, ff // 2), NARROW), pltpu.VMEM((4, 4, LANES, ff // 2), NARROW),
+            pltpu.VMEM((own, width), WIDE), pltpu.VMEM((own, width), NARROW),
+            pltpu.VMEM((4, 4, 8, LANES), WIDE), pltpu.VMEM((2, ROWS, width), NARROW),
+            pltpu.VMEM((8, width), WIDE), *fold_scratch,
+        ],
+        48, 32, 5,
+    )
+    grad_proj, parts_attn, hidden_out, got_b = call(
+        functools.partial(attend_back_kernel, count_a, 12 - count_a),
+        "attend_back",
+        [
+            shape(8, own, 512), shape(4, 4, 768, LANES), shape(own, width),
+            shape(12 - count_a, 2, 4, chunk, LANES),
+        ],
+        (
+            grad_mid, queries, keys, values, all_marks, tables, out_all, mixed, attn_in, hidden, mid_own, parts,
+            *(have[2, j] for j in range(4)),
+        ),
+        [
+            pltpu.VMEM((8, own, width), NARROW), pltpu.VMEM((2, 1024, 256), NARROW),
+            pltpu.VMEM((2, 1024, 128), NARROW), pltpu.VMEM((2, 1024, 128), NARROW),
+            pltpu.VMEM(all_marks.shape, WIDE), pltpu.VMEM(tables.shape, WIDE),
+            pltpu.VMEM((256, width), NARROW), pltpu.VMEM((8, own, 256), NARROW),
+            pltpu.VMEM((8, own, ff // 4), NARROW), pltpu.VMEM((ff // 4, width), NARROW),
+            pltpu.VMEM((8, own, 512), NARROW), pltpu.VMEM((1024, 128), WIDE),
+            pltpu.VMEM((1024, 128), WIDE), pltpu.VMEM((256, 8 * own), NARROW),
+            pltpu.VMEM((512, 8 * own), NARROW), pltpu.VMEM((2, 8, own, TILE), NARROW),
+            pltpu.VMEM((4, 4, 768, LANES), NARROW), pltpu.VMEM((own, width), WIDE),
+            pltpu.VMEM((own, width), NARROW), *fold_scratch,
+        ],
+        32, 128, 6,
+    )
+    out_home, grad_home, gain_sums, ffn_sums, attn_sums = call(
+        end_kernel,
+        "end",
+        [
+            shape(own, width), shape(own, width), shape(8, LANES, dtype=WIDE),
+            shape(4, 12, chunk, LANES), shape(4, 768, LANES),
+        ],
+        (
+            grad_proj, qkv_all, x_own, all_gains, grad_mid_own, hidden_out, gain_ffn_part, parts, got_a, got_b, parts_attn
+        ),
+        [
+            pltpu.VMEM((8, own, 512), NARROW), pltpu.VMEM(qkv_all.shape, NARROW),
+            pltpu.VMEM((own, width), NARROW), pltpu.VMEM((4, 4, 8, LANES), WIDE),
+            pltpu.VMEM((own, width), WIDE), pltpu.VMEM((own, width), NARROW),
+            pltpu.VMEM((8, width), WIDE), pltpu.VMEM((5, 8, width), WIDE),
+            *[pltpu.VMEM((12, 4, chunk, LANES), NARROW)] * 5,
+            pltpu.VMEM((4, 768, LANES), NARROW), pltpu.VMEM((4, 768, LANES), NARROW),
+            pltpu.VMEM((2, 4, 768, LANES), NARROW), pltpu.VMEM((4, 768, LANES), NARROW),
+            *fold_scratch,
+        ],
+        40, 40, 7,
+    )
+    grads = ffn_sums.reshape(4, 4, 3, chunk, LANES).transpose(2, 0, 1, 3, 4)
+    grads = grads.reshape(3, ff, LANES)
+    grad_qkv = attn_sums[:, 256:].reshape(-1, LANES)
+    grad_out = attn_sums[:, :256].reshape(-1, LANES)
+    return (
+        out_home.reshape(hidden_in.shape),
+        grad_home.reshape(hidden_in.shape),
+        gain_sums[0],
+        grad_qkv.T.astype(WIDE),
+        grad_out.astype(WIDE),
+        gain_sums[1],
+        grads[0].T.astype(WIDE),
+        grads[1].T.astype(WIDE),
+        grads[2].astype(WIDE),
     )
 
 

time: 1680 us -> 875 us (0.52)
  waiting for transfers between devices: 752 us -> 0 us
  Pallas kernels: 440 us -> 833 us
  matrix products: 211 us -> 0 us
  blocking collectives: 102 us -> 0 us
  local copies, waits for them, and re-layouts: 65.6 us -> 15.3 us
  starting transfers between devices: 41.6 us -> 0 us
  other arithmetic: 40.7 us -> 8.9 us
    pallas_call x3 -> x7, Pallas kernels: 440 us -> 833 us  [call(): pl.pallas_call(inner, out_shape=outs, in_specs=[ANYWHERE] * n_in, out_spe...]
    unnamed x12 -> x0, waiting for transfers between devices: 359 us -> none
    reduce_scatter x8 -> x0, waiting for transfers between devices: 294 us -> none  [the longest x3 126 us: fold(): lax.psum_scatter(parts.astype(jnp.bfloat16), 'fsdp', scatter_dimension=0,...]
    dot_general x17 -> x0, matrix products: 199 us -> none  [the longest x13 171 us: dot(): lax.dot_general(left, right, (dims, ((), ())), preferred_element_type=jnp...]
    unnamed x1 -> x0, blocking collectives: 98.1 us -> none
    all_gather x2 -> x0, waiting for transfers between devices: 73.1 us -> none  [the longest x1 39.8 us: spread(): return lax.all_gather(both, 'fsdp', axis_index_groups=near)]
    all_to_all x5 -> x0, starting transfers between devices: 35.5 us -> none  [trade(): return lax.all_to_all(pieces, 'fsdp', 0, 0, axis_index_groups=near)]
    all_to_all x5 -> x0, waiting for transfers between devices: 25.7 us -> none  [trade(): return lax.all_to_all(pieces, 'fsdp', 0, 0, axis_index_groups=near)]
  transfers between devices with their start and end apart: 18 -> 0, of which waited for: 12 -> 0; matrix products, arithmetic and copies ran while one was open for 9% -> 0% of each run, Pallas kernels for 0% -> 0%
where the time goes in v2:
time: 875 us; the launch traced here: 859 us
  Pallas kernels  833 us (95%)
  local copies, waits for them, and re-layouts  15.3 us (2%)
  other arithmetic  8.9 us (1%)
    pallas_call x7, Pallas kernels, call(): pl.pallas_call(inner, out_shape=outs, in_specs=[ANYWHERE] * n_in, out_spe...  833 us

profile of v2, /device:TPU:1, one launch (start us, length us, event | category | flops | bytes accessed | tf_op | source)
XLA Modules:
  0.0 858.9 jit_solution(8063531778736412892)
XLA Ops:
  0.6 0.0 copy-start
  0.7 0.7 bitcast_convert_fusion.5
  1.3 0.0 copy-done
  1.4 0.7 convert_element_type.57
  2.1 0.7 pad_convert_fusion
  2.7 0.0 copy-start.3
  2.7 0.6 scatter.14.refs_3_
  3.3 0.1 broadcast_multiply_fusion
  3.5 1.9 maximum_cosine_fusion
  5.4 0.8 pad_maximum_fusion.1.refs_2_
  6.2 0.0 copy-done.3
  6.2 146.7 %start.1 = (bf16[256,2048]{1,0:T(8,128)(2,1)}, bf16[256,2048]{1,0:T(8,128)(2,1)}, bf16[8,256,2048]{2,1,0:T(8,128)(2,1)}, f32[4,2,256,128]{3,2,1,0:T(8,128)}, f32...) custom-call(bf16[256,2048]{1,0:T(8,128)(2,1)} %bitcast.48, ...), custom_call_target="tpu_custom_call" | custom-call | tf_op jit(solution)/shard_map/start/pallas_call | solution.py:505
  152.9 58.3 %attend.1 = (bf16[2,1024,256]{2,1,0:T(8,128)(2,1)}, bf16[2,1024,128]{2,1,0:T(8,128)(2,1)}, bf16[2,1024,128]{2,1,0:T(8,128)(2,1)}, bf16[8,256,256]{2,1,0:T(8,128)...) custom-call(bf16[8,256,2048]{2,1,0:T(8,128)(2,1)} %get-tuple-element.91.ref, ...), custom_call_target="tpu_custom_call" | custom-call | tf_op jit(solution)/shard_map/attend/pallas_call | solution.py:505
  211.2 85.2 %middle.1 = (f32[256,2048]{1,0:T(8,128)}, bf16[8,256,2048]{2,1,0:T(8,128)(2,1)}, bf16[4,4,256,128]{3,2,1,0:T(8,128)(2,1)}, bf16[4,4,128,256]{3,2,1,0:T(8,128)(2,...) custom-call(bf16[8,256,256]{2,1,0:T(8,128)(2,1)} %get-tuple-element.99.refs_0_.refs_7_, ...), custom_call_target="tpu_custom_call" | custom-call | tf_op jit(solution)/shard_map/middle/pallas_call | solution.py:505
  296.4 131.8 %ffn.1 = (bf16[8,256,1024]{2,1,0:T(8,128)(2,1)}, bf16[8,256,2048]{2,1,0:T(8,128)(2,1)}, bf16[12,4,4,256,128]{4,3,2,1,0:T(8,128)(2,1)}, bf16[4,4,128,256]{3,2,1,0...) custom-call(bf16[8,256,2048]{2,1,0:T(8,128)(2,1)} %get-tuple-element, ...), custom_call_target="tpu_custom_call" | custom-call | tf_op jit(solution)/shard_map/ffn/pallas_call | solution.py:505
  428.2 96.8 %back.1 = (f32[256,2048]{1,0:T(8,128)}, bf16[8,256,2048]{2,1,0:T(8,128)(2,1)}, f32[8,2048]{1,0:T(8,128)}, bf16[7,2,4,256,128]{4,3,2,1,0:T(8,128)(2,1)}) custom-call(bf16[8,256,2048]{2,1,0:T(8,128)(2,1)} %get-tuple-element.111.refs_0_, f32[256,2048]{1,0:T(8,128)} %get-tuple-element.112.refs_1_.refs_10_, bf16[256,2048]{1,0:T(8,128)(2,1)} %get-tuple-element.95.refs_4_.refs_2_, ...), custom_call_target="tpu_custom_call" | custom-call | tf_op jit(solution)/shard_map/back/pallas_call | solution.py:505
  525.1 67.1 %attend_back.1 = (bf16[8,256,512]{2,1,0:T(8,128)(2,1)}, bf16[4,4,768,128]{3,2,1,0:T(8,128)(2,1)}, bf16[256,2048]{1,0:T(8,128)(2,1)}, bf16[5,2,4,256,128]{4,3,2,1,0:T(8,128)(2,1)}) custom-call(bf16[8,256,2048]{2,1,0:T(8,128)(2,1)} %get-tuple-element.118.refs_0_, bf16[2,1024,256]{2,1,0:T(8,128)(2,1)} %get-tuple-element.119.refs_1_, ...), custom_call_target="tpu_custom_call" | custom-call | tf_op jit(solution)/shard_map/attend_back/pallas_call | solution.py:505
  592.2 247.6 %end.1 = (bf16[256,2048]{1,0:T(8,128)(2,1)}, bf16[256,2048]{1,0:T(8,128)(2,1)}, f32[8,128]{1,0:T(8,128)}, bf16[4,12,256,128]{3,2,1,0:T(8,128)(2,1)}, bf16[4,768,128]{2,1,0:T(8,128)(2,1)}) custom-call(bf16[8,256,512]{2,1,0:T(8,128)(2,1)} %get-tuple-element.125.refs_0_, bf16[4,4,128,512]{3,2,1,0:T(8,128)(2,1)} %get-tuple-element.92.refs_1_, ...), custom_call_target="tpu_custom_call" | custom-call | tf_op jit(solution)/shard_map/end/pallas_call | solution.py:505
  839.8 1.3 slice_bitcast_fusion
  841.0 1.0 slice.79
  842.0 1.1 slice.78
  843.1 0.8 bitcast_convert_fusion.4
  843.9 0.1 bitcast_convert_fusion.3
  844.0 1.3 copy.21
  845.3 3.1 fusion.2
  848.5 0.2 bitcast_convert_fusion.2
  848.7 1.8 copy.26
  850.5 2.9 bitcast_convert_fusion
  853.4 0.0 copy-start.2
  853.4 0.0 copy-start.1
  853.4 1.8 copy.27
  855.2 2.3 copy.38
  857.5 0.0 copy-done.2
  857.5 1.0 copy.39
  858.5 0.0 copy-done.1
  (5 shorter events, 0.0 us)
Async XLA Ops:
  0.6 0.7 copy-start
  2.7 3.5 copy-start.3
  853.4 4.1 copy-start.2
  853.4 5.1 copy-start.1

commit v3 on v2

--- a/solution.py
+++ b/solution.py
@@ -1,4 +1,5 @@
 import functools
+import math
 
 import jax
 import jax.numpy as jnp
@@ -269,8 +270,14 @@
         self.side, self.core, self.row = (f, c, 1 - t), (fs, c, t), (fy, c, t)
         self.cross = (fd, c, t)
         self.z1, self.z2 = (f, self.c1, t), (f, self.c2, t)
-        self.fr, self.cr = f % 2 * 2 + f // 2, c % 2 * 2 + c // 2
-        self.swap = (self.cr, self.fr, t)
+        self.is_end, self.is_mid = c * (3 - c) == 0, c * (3 - c) != 0
+        self.c_near, self.c_mate, self.c_outer = 1 + c // 3, 3 - c, 3 * c - 3
+        self.z3 = (f, 3 - c, t)
+        y, k, high, low = f // 2, f % 2, c // 2, c % 2
+        self.to_f, to_c = (low + y) % 2 * 2 + high, k * 2 + y
+        self.to = (self.to_f, to_c, t)
+        self.whence = (low * 2 + high, k * 2 + (y + low) % 2, t)
+        self.away = (self.to_f - f) * (self.to_f - f) + (to_c - c) * (to_c - c)
         self.b, self.b_side = f * 2 + t, f * 2 + 1 - t
         self.b_row, self.b_far = fy * 2 + t, fy * 2 + 1 - t
         self.b_core, self.b_core_side = fs * 2 + t, fs * 2 + 1 - t
@@ -294,6 +301,7 @@
         self.local_sems = local_sems
         self.n, self.n_local = 0, 0
         self.out, self.kept = [], []
+        self.gates = []
 
     def make(self, source, target, device, lands):
         sems = dict(
@@ -330,7 +338,45 @@
             sent.leave()
         for copy in self.kept:
             copy.wait()
-        self.out, self.kept = [], []
+        for gate in self.gates:
+            gate.leave()
+        self.out, self.kept, self.gates = [], [], []
+
+
+class Gate:
+    def __init__(self, post, sends, gets, what, lands):
+        self.post, self.sends, self.gets, self.what, self.lands = post, sends, gets, what, lands
+        self.n = post.n
+        post.n += 1
+
+    def copy(self, source, target, device):
+        return pltpu.make_async_remote_copy(
+            src_ref=source,
+            dst_ref=target,
+            send_sem=self.post.sems[0].at[self.n],
+            recv_sem=self.post.sems[1].at[self.n],
+            device_id=device,
+            device_id_type=MESH,
+        )
+
+    def start(self):
+        @pl.when(self.sends)
+        def _():
+            self.copy(*self.what()).start()
+
+        self.post.gates.append(self)
+        return self
+
+    def arrive(self):
+        @pl.when(self.gets)
+        def _():
+            there = self.lands()
+            self.copy(there, there, self.post.anyone).wait_recv()
+
+    def leave(self):
+        @pl.when(self.sends)
+        def _():
+            self.copy(*self.what()).wait_send()
 
 
 def meet(devices):
@@ -486,6 +532,114 @@
         self.post.settle([self.own])
 
 
+class LineClimb:
+    def __init__(self, post, at, level, out):
+        self.post = post
+        line = lambda c: (at.f, c, at.t)
+        slot = lambda c: out.at[:, c]
+        near, mate, outer = at.c_near, at.c_mate, at.c_outer
+        end, mid = at.is_end, at.is_mid
+        self.t0 = Gate(post, end, mid, lambda: (level, slot(at.c), line(near)), lambda: slot(outer))
+        self.t1 = Gate(post, mid, end, lambda: (level, slot(at.c), line(outer)), lambda: slot(near))
+        self.t2 = Gate(post, mid, mid, lambda: (level, slot(at.c), line(mate)), lambda: slot(mate))
+        self.t3 = Gate(
+            post, mid, mid, lambda: (slot(outer), slot(outer), line(mate)), lambda: slot(3 - outer)
+        )
+        self.t4 = Gate(
+            post, mid, end, lambda: (slot(mate), slot(mate), line(outer)), lambda: slot(3 - near)
+        )
+        self.t5 = Gate(
+            post, mid, end, lambda: (slot(3 - outer), slot(3 - outer), line(outer)), lambda: slot(3 - at.c)
+        )
+        for gate in (self.t0, self.t1, self.t2):
+            gate.start()
+        self.own = post.keep(level, slot(at.c))
+
+    def forward(self):
+        self.t2.arrive()
+        self.t4.start()
+        self.t0.arrive()
+        self.t3.start()
+
+    def last(self):
+        self.t3.arrive()
+        self.t5.start()
+
+    def finish(self):
+        for gate in (self.t1, self.t4, self.t5):
+            gate.arrive()
+        self.post.settle([self.own])
+
+
+class Ends:
+    def __init__(self, post, at, parts, first, got):
+        self.gates = [
+            Gate(
+                post, at.is_end, at.is_mid,
+                lambda q=q: (
+                    parts.at[first + q, :, pl.ds((3 - at.c) // 3, 3)], got.at[q], (at.f, at.c_near, at.t)
+                ),
+                lambda q=q: got.at[q],
+            ).start()
+            for q in range(got.shape[0])
+        ]
+
+    def finish(self):
+        for gate in self.gates:
+            gate.arrive()
+
+
+class Middle:
+    def __init__(self, post, at, step, parts, first, came, out, own, more):
+        self.post, self.at, self.out, self.own, self.more = post, at, out, own, more
+        self.step, self.n = step, out.shape[0]
+        self.sems = [post.local_sems.at[post.n_local + k] for k in range(2)]
+        post.n_local += 2
+        rows = pl.ds(first, self.n)
+
+        def sources():
+            if step == 1:
+                return (
+                    parts.at[rows, :, pl.ds(2 * (2 - at.c), 2)], came.at[:, :, pl.ds(2 - at.c, 2)]
+                )
+            return parts.at[rows, :, 3 * (at.c - 1)], came.at[:, :, at.c - 1]
+
+        self.sources = sources
+
+        @pl.when(at.is_mid)
+        def _():
+            for source, target, sem in zip(sources(), (own, more), self.sems):
+                pltpu.make_async_copy(source, target, sem).start()
+
+    def send(self):
+        at, own, more = self.at, self.own, self.more
+
+        @pl.when(at.is_mid)
+        def _():
+            for source, target, sem in zip(self.sources(), (own, more), self.sems):
+                pltpu.make_async_copy(source, target, sem).wait()
+
+            def add(q, carry):
+                own[q] = (own[q].astype(WIDE) + more[q].astype(WIDE)).astype(NARROW)
+                return carry
+
+            lax.fori_loop(0, self.n, add, 0)
+
+        c_to = at.c_mate if self.step == 1 else at.c_outer
+        self.gate = Gate(
+            self.post, at.is_mid, at.is_mid if self.step == 1 else at.is_end,
+            lambda: (own, self.out, (at.f, c_to, at.t)), lambda: self.out,
+        ).start()
+
+    def finish(self):
+        self.gate.arrive()
+
+
+def middle_scratch(step, n):
+    dims = (n, 4, 2, 256, LANES) if step == 1 else (n, 4, 256, LANES)
+    return [pltpu.VMEM(dims, NARROW)] * 2
+
+
 def call(kernel, name, outs, args, scratch, copies, kept, collective_id):
     sems = [
         pltpu.SemaphoreType.DMA((copies,)),
@@ -495,9 +649,10 @@
     n_in, n_out = len(args), len(outs)
 
     def inner(*refs):
-        post = Post(*refs[len(refs) - 3 :])
+        post, at = Post(*refs[len(refs) - 3 :]), Place()
+        post.anyone = at.z1
         kernel(
-            post, Place(), refs[:n_in], refs[n_in : n_in + n_out], refs[n_in + n_out : len(refs) - 3]
+            post, at, refs[:n_in], refs[n_in : n_in + n_out], refs[n_in + n_out : len(refs) - 3]
         )
         post.close()
         assert post.n <= copies and post.n_local <= kept, (post.n, post.n_local)
@@ -529,38 +684,39 @@
 
 
 class Swap:
-    def __init__(self, post, at):
+    def __init__(self, post, at, home=False):
         self.post, self.at, self.moves = post, at, []
+        self.device = at.whence if home else at.to
 
     def __call__(self, source, target, lands):
         post, at = self.post, self.at
-        sent = post.make(source, target, at.swap, lands)
+        sent = post.make(source, target, self.device, lands)
         local = pltpu.make_async_copy(source, target, post.local_sems.at[post.n_local])
         post.n_local += 1
 
-        @pl.when(at.f != at.cr)
+        @pl.when(at.away != 0)
         def _():
             sent.copy.start()
 
-        @pl.when(at.f == at.cr)
+        @pl.when(at.away == 0)
         def _():
             local.start()
 
         self.moves.append(sent)
 
         def arrive():
-            @pl.when(at.f != at.cr)
+            @pl.when(at.away != 0)
             def _():
                 sent.landing.wait_recv()
 
-            @pl.when(at.f == at.cr)
+            @pl.when(at.away == 0)
             def _():
                 local.wait()
 
         return arrive
 
     def finish(self):
-        @pl.when(self.at.f != self.at.cr)
+        @pl.when(self.at.away != 0)
         def _():
             for sent in self.moves:
                 sent.copy.wait_send()
@@ -568,26 +724,46 @@
 
 def meet_swap(at):
     bar = pltpu.get_barrier_semaphore()
-    partners = (at.side, at.core, at.row, at.cross, at.z1, at.z2)
+    partners = (at.side, at.core, at.row, at.cross, at.z1, at.z2, at.z3)
     for device in partners:
         pl.semaphore_signal(bar, inc=1, device_id=device, device_id_type=MESH)
 
-    @pl.when(at.f != at.cr)
+    @pl.when(at.away != 0)
     def _():
-        pl.semaphore_signal(bar, inc=1, device_id=at.swap, device_id_type=MESH)
-        pl.semaphore_wait(bar, len(partners) + 1)
-
-    @pl.when(at.f == at.cr)
+        for device in (at.to, at.whence):
+            pl.semaphore_signal(bar, inc=1, device_id=device, device_id_type=MESH)
+        pl.semaphore_wait(bar, len(partners) + 2)
+
+    @pl.when(at.away == 0)
     def _():
         pl.semaphore_wait(bar, len(partners))
 
 
+class Deal:
+    def __init__(self, post, at, shards, j, outs):
+        self.post, self.sent, self.kept = post, [], []
+        gate, up, down = shards
+        part = gate.shape[1] // 4
+        chunk = part // 4
+        for device, k in ((at.row, at.fy), (at.cross, at.fd), (at.core, at.fs), (None, at.f)):
+            lane = pl.ds(pl.multiple_of(k * part + j * chunk, LANES), chunk)
+            for source, out in zip((gate.at[:, lane], up.at[:, lane], down.at[lane]), outs):
+                if device is None:
+                    self.kept.append(post.keep(source, out.at[at.f]))
+                else:
+                    self.sent.append(post.send(source, out.at[at.f], device, out.at[k]))
+
+    def finish(self):
+        for sent in self.sent:
+            sent.arrive()
+
+
 HALVES = [pl.ds(half * ROWS, ROWS) for half in range(2)]
 
 
 def start_kernel(post, at, ins, outs, scratch):
-    hidden, cot, table, marks, gains, wqkv, wo, w_gate, w_up, w_down = ins
-    x_own, cot_own, attn_in, tables, all_marks, all_gains, qkv_all, out_all, gate_lvl, up_lvl, down_lvl = outs
+    hidden, cot, marks, gains, wqkv, wo, *shards = ins
+    x_own, cot_own, attn_in, all_marks, all_gains, qkv_all, out_all, *levels_out = outs
     rows_in, rows_out, gain_buf = scratch
     f, c = at.f, at.c
     meet_swap(at)
@@ -605,8 +781,7 @@
     own = [post.keep(wqkv.at[:, lane], qkv_all.at[f, c])]
     row = pl.ds(pl.multiple_of(f * span, LANES), span)
     own.append(post.keep(wo.at[row], out_all.at[f, c]))
-    table_moved = swap(table, tables.at[at.cr], tables.at[f])
-    marks_moved = swap(marks, all_marks.at[at.cr], all_marks.at[f])
+    marks_moved = swap(marks, all_marks.at[at.to_f], all_marks.at[f])
 
     mine = gain_buf.at[f, c]
     post.settle([post.keep(gains, mine)])
@@ -646,49 +821,28 @@
         spread.own(half, rows_out.at[HALVES[half]])
         post.keep(rows_in.at[HALVES[half]], x_own.at[HALVES[half]])
 
-    table_moved()
     marks_moved()
-    small = []
-    for buf in (tables, all_marks):
-        here = buf.at[f]
-        small.append((buf, post.send(here, here, at.core, buf.at[at.fs])))
-    smaller = []
-    for buf, sent in small:
-        sent.arrive()
-        pair = buf.at[pl.ds(f // 2 * 2, 2)]
-        smaller.append(post.send(pair, pair, at.row, buf.at[pl.ds(at.fy // 2 * 2, 2)]))
-
+    here = all_marks.at[f]
+    small = post.send(here, here, at.core, all_marks.at[at.fs])
     spread.relay(0)
+    small.arrive()
+    pair = all_marks.at[pl.ds(f // 2 * 2, 2)]
+    smaller = post.send(pair, pair, at.row, all_marks.at[pl.ds(at.fy // 2 * 2, 2)])
     spread.relay(1)
-
-    part = w_gate.shape[1] // 4
-    chunk = part // 4
-    later = []
-    for device, k in ((at.row, at.fy), (at.cross, at.fd), (at.core, at.fs), (None, f)):
-        for j in range(4):
-            lane = pl.ds(pl.multiple_of(k * part + j * chunk, LANES), chunk)
-            for source, target in (
-                (w_gate.at[:, lane], gate_lvl),
-                (w_up.at[:, lane], up_lvl),
-                (w_down.at[lane], down_lvl),
-            ):
-                if device is None:
-                    post.keep(source, target.at[j, f])
-                else:
-                    later.append(post.send(source, target.at[j, f], device, target.at[j, k]))
-
     forwards = []
     for far, close, there, out in levels:
         far.arrive()
         forwards.append((post.send(there, there, at.z1, out.at[:, at.c3]), close))
     cot_moved = [swap(cot.at[half], cot_own.at[half], cot_own.at[half]) for half in HALVES]
+    deals = [Deal(post, at, shards, j, levels_out[3 * j : 3 * j + 3]) for j in range(2)]
     spread.corner()
     for last, close in forwards:
         last.arrive()
         close.arrive()
     spread.finish()
-    for sent in smaller + later:
-        sent.arrive()
+    smaller.arrive()
+    for deal in deals:
+        deal.finish()
     for arrive in cot_moved:
         arrive()
     swap.finish()
@@ -702,10 +856,30 @@
     return values * cos_full - pltpu.roll(values, HALF, 1) * sin_full
 
 
-def rope_full(table):
+def rope_full(marks, m, inverse):
+    angle = marks.T[:, 2 + m : 3 + m] * inverse
+    low = lax.broadcasted_iota(jnp.int32, angle.shape, 1) < HALF
+    turns = jnp.floor(angle * (2.0 / math.pi) + 0.5)
+    rest = ((angle - turns * 1.5703125) - turns * 4.837512969970703125e-4) - turns * 7.54978995489188e-8
+    square = rest * rest
+    sine = rest + rest * square * (
+        -1.6666654611e-1 + square * (8.3321608736e-3 - square * 1.9515295891e-4)
+    )
+    cosine = 1.0 - 0.5 * square + square * square * (
+        4.166664568298827e-2 + square * (-1.388731625493765e-3 + square * 2.443315711809948e-5)
+    )
+    quadrant = turns + jnp.where(low, 1.0, 0.0)
+    half = jnp.floor(quadrant * 0.5)
+    odd = quadrant - 2.0 * half > 0.5
+    negative = half - 2.0 * jnp.floor(half * 0.5) > 0.5
+    table = jnp.where(odd, cosine, sine)
+    table = jnp.where(negative, -table, table)
     turned_table = pltpu.roll(table, HALF, 1)
-    low = lax.broadcasted_iota(jnp.int32, table.shape, 1) < HALF
     return jnp.where(low, table, turned_table), jnp.where(low, -turned_table, table)
+
+
+def quarter(at, i):
+    return (i + at.c) % 2 * 2 + i // 2
 
 
 def mm(left, right, dims=((1,), (0,))):
@@ -713,8 +887,6 @@
 
 
 TILE = 256
-QUARTER = (0, 2, 1, 3)
-
 
 def softmax_tile(query, key, id_col, id_row):
     raw = mm(query, key, ((1,), (1,))) * SCALE
@@ -724,18 +896,19 @@
     return exponent * (1.0 / jnp.sum(exponent, axis=-1, keepdims=True))
 
 
-def id_rows(marks, m, tiles):
-    return jnp.concatenate([marks[QUARTER[i], m : m + 1, :] for i in range(tiles)], axis=1)
-
-
-def attend_kernel(jobs, post, at, ins, outs, scratch):
-    attn_in, qkv_all, tables_in, marks_in, cot_own = ins[:5]
-    levels = jobs(ins[5:])
-    queries, keys, values, mixed, dy, *climbed = outs
-    rows, weight, tables, marks, q_buf, k_buf, v_buf, mix_buf = scratch
-    meet((at.side, at.core, at.row, at.z1, at.z2))
+def id_rows(at, marks, m, tiles):
+    return jnp.concatenate([marks[quarter(at, i), m : m + 1, :] for i in range(tiles)], axis=1)
+
+
+def attend_kernel(post, at, ins, outs, scratch):
+    attn_in, qkv_all, inverse_in, marks_in, cot_own, *shards = ins[:8]
+    levels = ins[8:]
+    queries, keys, values, mixed, dy, *more = outs
+    climbed, dealt = more[: len(levels)], more[len(levels) :]
+    rows, weight, inverse, marks, q_buf, k_buf, v_buf, mix_buf = scratch
+    meet((at.side, at.core, at.row, at.cross, at.z1, at.z2))
     local = [
-        post.keep(tables_in, tables),
+        post.keep(inverse_in, inverse),
         post.keep(marks_in, marks),
         post.keep(qkv_all, weight),
         post.keep(attn_in.at[:, pl.ds(0, ROWS)], rows.at[0]),
@@ -745,15 +918,16 @@
     for half in range(2):
         spread.own(half, cot_own.at[pl.ds(half * ROWS, ROWS)])
     climbs = [Climb(post, at, level, out) for level, out in zip(levels, climbed)]
+    deal = Deal(post, at, shards, 2, dealt)
     post.settle(local)
     width = rows.shape[-1]
     columns = weight.shape[-1]
     for m in range(2):
         for i in range(4):
-            q = QUARTER[i]
-            here = rows[m, 2 * q : 2 * q + 2].reshape(TILE, width)
+            q = quarter(at, i)
+            here = rows[m, pl.ds(2 * q, 2)].reshape(TILE, width)
             projected = mm(here, weight[...].reshape(width, columns))
-            cos_full, sin_full = rope_full(tables[q, m])
+            cos_full, sin_full = rope_full(marks[q], m, inverse[0:1])
             place = pl.ds(i * TILE, TILE)
             for g in range(2):
                 lane = slice(g * HEAD_DIM, (g + 1) * HEAD_DIM)
@@ -764,9 +938,9 @@
     for m in range(2):
         for i in range(4):
             n = min(i + 2, 4) * TILE
-            q = QUARTER[i]
+            q = quarter(at, i)
             id_col = marks[q].T[:, m : m + 1]
-            id_row = id_rows(marks, m, n // TILE)
+            id_row = id_rows(at, marks, m, n // TILE)
             for g in range(2):
                 lane = slice(g * HEAD_DIM, (g + 1) * HEAD_DIM)
                 prob = softmax_tile(
@@ -787,14 +961,16 @@
     spread.finish()
     for climb in climbs:
         climb.finish()
-
-
-def middle_kernel(jobs, post, at, ins, outs, scratch):
-    mixed, out_all, x_own, gains_in = ins[:4]
-    levels = jobs(ins[4:])
-    mid_own, ffn_in, *climbed = outs
+    deal.finish()
+
+
+def middle_kernel(post, at, ins, outs, scratch):
+    mixed, out_all, x_own, gains_in, *shards = ins[:7]
+    levels = ins[7:]
+    mid_own, ffn_in, *more = outs
+    climbed, dealt = more[: len(levels)], more[len(levels) :]
     mix_buf, weight, x_buf, gains, rows_out, *fold_scratch = scratch
-    meet((at.side, at.core, at.row, at.z1, at.z2))
+    meet((at.side, at.core, at.row, at.cross, at.z1, at.z2))
     local = [
         post.keep(out_all.at[i // 4, i % 4], weight.at[:, pl.ds(i * LANES, LANES)])
         for i in range(16)
@@ -809,6 +985,7 @@
     fold = Fold(post, at, part, fold_scratch)
     fold.first()
     fold.second()
+    deal = Deal(post, at, shards, 3, dealt)
     fold.third()
     gain = jnp.concatenate([gains[i // 4, i % 4, 1:2, :] for i in range(16)], axis=1)
     spread = Spread(post, at, ffn_in)
@@ -828,39 +1005,26 @@
     spread.finish()
     for climb in climbs:
         climb.finish()
-
-
-class Jobs:
-    def __init__(self, *wanted):
-        self.wanted = wanted
-
-    def __call__(self, level_refs):
-        return [level_refs[a].at[j] for a, j in self.wanted]
-
-    def shapes(self, levels):
-        return [
-            jax.ShapeDtypeStruct((4, 4) + levels[a].shape[2:], NARROW) for a, j in self.wanted
-        ]
+    deal.finish()
 
 
 def small_arrays(block_ids, positions, attn_gain, ffn_gain):
     micro, _, span = positions.shape
-    cos_table, sin_table = rope_tables(positions[:, 0])
-    table = jnp.concatenate([cos_table[..., :HALF], sin_table[..., :HALF]], axis=-1)
     ids = lax.dynamic_slice_in_dim(block_ids[:, 0], lax.axis_index("ctx") * span, span, 1)
-    marks = jnp.zeros((8, span), WIDE).at[:micro].set(ids.astype(WIDE))
-    gains = jnp.zeros((8, LANES), WIDE).at[0].set(attn_gain.astype(WIDE))
-    return table, marks, gains.at[1].set(ffn_gain.astype(WIDE))
-
-
-def ffn_kernel(jobs, post, at, ins, outs, scratch):
+    rows = jnp.concatenate([ids, positions[:, 0]]).astype(WIDE)
+    marks = jnp.pad(rows, ((0, 8 - 2 * micro), (0, 0)))
+    gains = jnp.pad(jnp.stack([attn_gain, ffn_gain]).astype(WIDE), ((0, 6), (0, 0)))
+    return marks, gains
+
+
+def ffn_kernel(post, at, ins, outs, scratch):
     ffn_in, dy = ins[:2]
-    ready = ins[2:8]
-    levels = jobs(ins[8:])
-    hidden, grads_pre, parts, *climbed = outs
-    x_buf, dy_buf, gate_buf, up_buf, down_buf, act, act_t, staged = scratch
-    meet((at.z1, at.z2))
-    climbs = [Climb(post, at, level, out) for level, out in zip(levels, climbed)]
+    ready = ins[2:9]
+    levels = ins[9:]
+    hidden, grads_pre, parts, ends_a, ends_b, mates, *climbed = outs
+    x_buf, dy_buf, gate_buf, up_buf, down_buf, act, act_t, staged, *sum_bufs = scratch
+    meet((at.z1, at.z3))
+    climbs = [LineClimb(post, at, level, out) for level, out in zip(levels, climbed)]
     local = [post.keep(ffn_in, x_buf), post.keep(dy, dy_buf)]
     weights = list(ready) + list(climbed)
 
@@ -877,11 +1041,11 @@
     loading = load(0)
     post.settle(local)
     width = x_buf.shape[-1]
-    saved = []
+    saved, sums_0 = [], []
     for j in range(4):
         slot = j % 2
         if loading is None:
-            for climb in climbs[3 * (j - 2) : 3 * (j - 1)]:
+            for climb in climbs[:2] if j == 2 else climbs[2:]:
                 climb.finish()
             loading = load(j)
         post.settle(loading)
@@ -893,7 +1057,7 @@
             gate = mm(x, gate_buf[slot].reshape(width, -1))
             up = mm(x, up_buf[slot].reshape(width, -1))
             grad_hidden = mm(grad, down_buf[slot], ((1,), (1,)))
-            sig = 1.0 / (1.0 + jnp.exp(-gate))
+            sig = jax.nn.sigmoid(gate)
             silu = gate * sig
             values = (
                 grad_hidden * up * sig * (1.0 + gate * (1.0 - sig)),
@@ -914,9 +1078,10 @@
             post.keep(act.at[1], grads_pre.at[:, :, pl.ds((4 + j) * chunk, chunk)]),
             post.keep(act.at[2], hidden.at[:, :, lane]),
         ]
-        if j < 2:
-            for climb in climbs[3 * j : 3 * j + 3]:
-                climb.forward()
+        for climb in climbs[:2] if j == 1 else climbs[2:] if j == 2 else ():
+            climb.last()
+        for climb in climbs[:2] if j == 0 else climbs[2:] if j == 1 else ():
+            climb.forward()
 
         def sums(n, carry):
             place = pl.ds(pl.multiple_of(n * TILE, TILE), TILE)
@@ -929,9 +1094,22 @@
             return carry
 
         lax.fori_loop(0, 8, sums, 0)
-        for k in range(3):
-            for fl in range(4):
-                saved.append(post.keep(staged.at[k, pl.ds(4 * fl, 4)], parts.at[3 * j + k, fl]))
+        stored = [
+            post.keep(staged.at[k, pl.ds(4 * fl, 4)], parts.at[3 * j + k, fl])
+            for k in range(3)
+            for fl in range(4)
+        ]
+        if j < 2:
+            post.settle(stored)
+            sums_0.append(Ends(post, at, parts, 3 * j, (ends_a, ends_b)[j]))
+        else:
+            saved += stored
+        if j == 2:
+            sums_0[0].finish()
+            sums_1 = Middle(post, at, 1, parts, 0, ends_a, mates, *sum_bufs)
+            sums_1.send()
+    sums_0[1].finish()
+    sums_1.finish()
 
 
 class Descend:
@@ -951,12 +1129,17 @@
     return factor * (scaled - normed * inner_mean), jnp.sum(grad * normed, axis=0, keepdims=True)
 
 
-def back_kernel(first, count, post, at, ins, outs, scratch):
-    grads_pre, mid_own, cot_own, gains_in, parts, *weights = ins
-    grad_mid_own, grad_mid, gain_part, got = outs
-    pre_buf, weight, mid_buf, cot_buf, gains, rows_out, gain_out, *fold_scratch = scratch
-    meet((at.side, at.core, at.row, at.z1, at.z2))
-    downs = [Descend(post, at, parts.at[first + q], got.at[q]) for q in range(count)]
+def back_kernel(post, at, ins, outs, scratch):
+    grads_pre, mid_own, cot_own, gains_in, parts, ends_b, mates_a, *weights = ins
+    grad_mid_own, grad_mid, gain_part, ends_c, mates_b, outer_a = outs
+    pre_buf, weight, mid_buf, cot_buf, gains, rows_out, gain_out = scratch[:7]
+    bufs_1, bufs_2, fold_scratch = scratch[7:9], scratch[9:11], scratch[11:]
+    meet((at.side, at.core, at.row, at.z1, at.z3))
+    downs = [
+        Middle(post, at, 1, parts, 3, ends_b, mates_b, *bufs_1),
+        Middle(post, at, 2, parts, 0, mates_a, outer_a, *bufs_2),
+        Ends(post, at, parts, 6, ends_c),
+    ]
     chunk = pre_buf.shape[-1] // 8
     local = [post.keep(grads_pre, pre_buf)]
     for a in range(2):
@@ -970,6 +1153,8 @@
     def part(block):
         return mm(pre_buf[block], weight[...].reshape(width, -1), ((1,), (1,)))
 
+    for down in downs[:2]:
+        down.send()
     fold = Fold(post, at, part, fold_scratch)
     fold.first()
     fold.second()
@@ -996,17 +1181,23 @@
         down.finish()
 
 
-def attend_back_kernel(first, count, post, at, ins, outs, scratch):
+def attend_back_kernel(post, at, ins, outs, scratch):
     (
-        grad_mid, queries, keys, values, marks_in, tables_in, out_all, mixed, attn_in, hidden, mid_own, parts, *downs_in
+        grad_mid, queries, keys, values, marks_in, inverse_in, out_all, mixed, attn_in, hidden, mid_own, parts,
+        ends_c, mates_b, *downs_in
     ) = ins
-    grad_proj, parts_attn, hidden_out, got = outs
+    grad_proj, parts_attn, hidden_out, ends_d, mates_c, outer_b = outs
     (
-        gm_buf, q_buf, k_buf, v_buf, marks, tables, weight, mix_buf, hid_buf, down_buf, gp_buf, gk_buf, gv_buf,
-        mix_t, gp_t, column, staged, mid_buf, out_buf, *fold_scratch
-    ) = scratch
-    meet((at.side, at.core, at.row, at.z1, at.z2))
-    steps = [Descend(post, at, parts.at[first + q], got.at[q]) for q in range(count)]
+        gm_buf, q_buf, k_buf, v_buf, marks, inverse, weight, mix_buf, hid_buf, down_buf, gp_buf, gk_buf, gv_buf,
+        staged, mid_buf, out_buf
+    ) = scratch[:16]
+    bufs_1, bufs_2, fold_scratch = scratch[16:18], scratch[18:20], scratch[20:]
+    meet((at.side, at.core, at.row, at.z1, at.z3))
+    steps = [
+        Middle(post, at, 1, parts, 6, ends_c, mates_c, *bufs_1),
+        Middle(post, at, 2, parts, 3, mates_b, outer_b, *bufs_2),
+        Ends(post, at, parts, 11, ends_d),
+    ]
 
     chunk = hid_buf.shape[-1] // 4
     early = [post.keep(hidden, hid_buf)]
@@ -1018,7 +1209,7 @@
         post.keep(source, target)
         for source, target in (
             (grad_mid, gm_buf), (queries, q_buf), (keys, k_buf), (values, v_buf), (marks_in, marks),
-            (tables_in, tables), (mixed, mix_buf), (mid_own, mid_buf),
+            (inverse_in, inverse), (mixed, mix_buf), (mid_own, mid_buf),
         )
     ]
     late += [
@@ -1026,25 +1217,31 @@
         for i in range(16)
     ]
     post.settle(early)
+    for step in steps[:2]:
+        step.send()
     fold = Fold(post, at, lambda block: mm(hid_buf[block], down_buf[...]), fold_scratch)
     fold.first()
     post.settle(late)
 
     def fetch(n):
         place = pl.ds(n * TILE, TILE)
-        return post.keep(attn_in.at[:, :, place], column.at[n % 2])
-
+        return post.keep(attn_in.at[:, :, place], column(n))
+
+    def column(n):
+        return hid_buf.at[:, :, pl.ds(n % 2 * TILE, TILE)]
+
+    mix_t, gp_t = down_buf.at[pl.ds(512, 256)], down_buf.at[pl.ds(0, 512)]
     fetched = fetch(0)
     width = gm_buf.shape[-1]
     for m in range(2):
         for i in range(4):
-            q = QUARTER[i]
+            q = quarter(at, i)
             n = min(i + 2, 4) * TILE
             place = slice(i * TILE, (i + 1) * TILE)
             id_col = marks[q].T[:, m : m + 1]
-            id_row = id_rows(marks, m, n // TILE)
-            cos_full, sin_full = rope_full(tables[q, m])
-            rows = gm_buf[2 * q : 2 * q + 2, m * ROWS : (m + 1) * ROWS].reshape(TILE, width)
+            id_row = id_rows(at, marks, m, n // TILE)
+            cos_full, sin_full = rope_full(marks[q], m, inverse[0:1])
+            rows = gm_buf[pl.ds(2 * q, 2), m * ROWS : (m + 1) * ROWS].reshape(TILE, width)
             grad_mixed = mm(rows, weight[...], ((1,), (1,))).astype(NARROW)
             for g in range(2):
                 lane = slice(g * HEAD_DIM, (g + 1) * HEAD_DIM)
@@ -1067,9 +1264,9 @@
                 for h in range(2):
                     gp_buf[2 * q + h, m * ROWS : (m + 1) * ROWS, lane] = done[h * ROWS : (h + 1) * ROWS]
         for i in range(4):
-            q = QUARTER[i]
+            q = quarter(at, i)
             place = slice(i * TILE, (i + 1) * TILE)
-            cos_full, sin_full = rope_full(tables[q, m])
+            cos_full, sin_full = rope_full(marks[q], m, inverse[0:1])
             done = (
                 rope_back(gk_buf[place], cos_full, sin_full).astype(NARROW),
                 gv_buf[place].astype(NARROW),
@@ -1096,7 +1293,7 @@
             fetched = fetch(n + 1)
         place = slice(n * TILE, (n + 1) * TILE)
         value = mm(mix_t[...], gm_buf[:, :, place].reshape(8 * TILE, TILE)).astype(NARROW)
-        other = mm(gp_t[...], column[n % 2].reshape(8 * TILE, TILE)).astype(NARROW)
+        other = mm(gp_t[...], column(n)[...].reshape(8 * TILE, TILE)).astype(NARROW)
         for h in range(2):
             block = 2 * n + h
             lane = slice(h * LANES, (h + 1) * LANES)
@@ -1109,27 +1306,24 @@
 
 def end_kernel(post, at, ins, outs, scratch):
     (
-        grad_proj, qkv_all, x_own, gains_in, grad_mid_own, hidden_out, gain_ffn_part, parts, got_a, got_b, parts_attn
+        grad_proj, qkv_all, x_own, gains_in, grad_mid_own, hidden_out, gain_ffn_part, parts, parts_attn,
+        ends_a, ends_b, ends_c, ends_d, mates_a, mates_b, mates_c, outer_a, outer_b
     ) = ins
-    out_home, grad_home, gain_sums, ffn_sums, attn_sums = outs
+    out_home, grad_home, gain_sums, mates_d, *home_sums = outs
     (
         gp_buf, weight, x_buf, gains, mid_buf, rows_out, gain_buf, gain_got,
-        own_ffn, far_ffn, one_ffn, two_ffn, end_ffn, own_attn, far_attn, got_attn, end_attn, *fold_scratch
-    ) = scratch
+        own_ffn, one_ffn, two_ffn, outer_c, outer_d, own_attn, far_attn, got_attn, end_attn
+    ) = scratch[:17]
+    bufs_1, bufs_2, bufs_3, fold_scratch = scratch[17:19], scratch[19:21], scratch[21:23], scratch[23:]
     f, c = at.f, at.c
     meet_swap(at)
     step_attn = Descend(post, at, parts_attn, got_attn)
-    swap = Swap(post, at)
+    steps = [
+        Middle(post, at, 1, parts, 11, ends_d, mates_d, *bufs_1),
+        Middle(post, at, 2, parts, 6, mates_c, outer_c, *bufs_2),
+    ]
+    swap = Swap(post, at, home=True)
     moved = [swap(hidden_out.at[half], out_home.at[half], out_home.at[half]) for half in HALVES]
-
-    n_a = got_a.shape[0]
-    n_all = parts.shape[0]
-    a, b = pl.ds(0, n_a), pl.ds(n_a, n_all - n_a)
-    sums = [
-        post.keep(parts.at[:, :, at.c2], far_ffn),
-        post.keep(got_a.at[:, 1], two_ffn.at[a]),
-        post.keep(got_b.at[:, 1], two_ffn.at[b]),
-    ]
     fold_in = [
         post.keep(grad_proj, gp_buf), post.keep(qkv_all, weight), post.keep(x_own, x_buf),
         post.keep(gains_in, gains), post.keep(grad_mid_own, mid_buf),
@@ -1137,21 +1331,43 @@
     ]
     later = [
         post.keep(parts.at[:, :, c], own_ffn),
-        post.keep(got_a.at[:, 0], one_ffn.at[a]),
-        post.keep(got_b.at[:, 0], one_ffn.at[b]),
         post.keep(parts_attn.at[:, c], own_attn), post.keep(parts_attn.at[:, at.c2], far_attn),
     ]
-    post.settle(sums)
+    sum_sems = [post.local_sems.at[post.n_local + k] for k in range(7)]
+    post.n_local += 7
+
+    def mid_loads():
+        pieces = [
+            (ends_a.at[:, :, 2 * (c - 1)], one_ffn.at[pl.ds(0, 3)]),
+            (ends_b.at[:, :, 2 * (c - 1)], one_ffn.at[pl.ds(3, 3)]),
+            (ends_c.at[:, :, 2 * (c - 1)], one_ffn.at[pl.ds(6, 5)]),
+            (ends_d.at[:, :, 2 * (c - 1)], one_ffn.at[pl.ds(11, 1)]),
+            (mates_a.at[:, :, 2 - c], two_ffn.at[pl.ds(0, 3)]),
+            (mates_b.at[:, :, 2 - c], two_ffn.at[pl.ds(3, 3)]),
+            (mates_c.at[:, :, 2 - c], two_ffn.at[pl.ds(6, 5)]),
+        ]
+        return [pltpu.make_async_copy(*piece, sem) for piece, sem in zip(pieces, sum_sems)]
+
+    def end_loads():
+        pieces = [(outer_a, two_ffn.at[pl.ds(0, 3)]), (outer_b, two_ffn.at[pl.ds(3, 3)])]
+        return [pltpu.make_async_copy(*piece, sem) for piece, sem in zip(pieces, sum_sems)]
+
+    @pl.when(at.is_mid)
+    def _():
+        for copy in mid_loads():
+            copy.start()
+
+    @pl.when(at.is_end)
+    def _():
+        for copy in end_loads():
+            copy.start()
+
+    for step in steps:
+        step.send()
 
     def add(left, right):
         return (left.astype(WIDE) + right.astype(WIDE)).astype(NARROW)
 
-    def add_far(q, carry):
-        far_ffn[q] = add(far_ffn[q], two_ffn[q])
-        return carry
-
-    lax.fori_loop(0, n_all, add_far, 0)
-    far_sent = post.send(far_ffn, end_ffn, at.z2, end_ffn)
     post.settle(fold_in)
     width = x_buf.shape[-1]
 
@@ -1172,10 +1388,13 @@
         moved.append(swap(rows_out.at[rows], grad_home.at[rows], grad_home.at[rows]))
     gain_buf[0:1] = total
     post.settle(later)
+    steps[0].finish()
+    steps.append(Middle(post, at, 2, parts, 11, mates_d, outer_d, *bufs_3))
     step_attn.finish()
     for k in range(4):
         far_attn[k] = add(far_attn[k], got_attn[1, k])
     far_attn_sent = post.send(far_attn, end_attn, at.z2, end_attn)
+    steps[2].send()
     for k, device in enumerate((at.core, at.row, at.side, at.z1, at.z2)):
         gain_sent = post.send(gain_buf, gain_got.at[k], device, gain_got.at[k])
         gain_sent.arrive()
@@ -1185,14 +1404,41 @@
     place = pl.ds(pl.multiple_of((f * 4 + c) * LANES, LANES), LANES)
     post.keep(gain_buf.at[:, place], gain_sums)
 
-    far_sent.arrive()
-
-    def add_own(q, carry):
-        value = own_ffn[q].astype(WIDE) + one_ffn[q].astype(WIDE) + end_ffn[q].astype(WIDE)
-        own_ffn[q] = value.astype(NARROW)
-        return carry
-
-    lax.fori_loop(0, n_all, add_own, 0)
+    @pl.when(at.is_mid)
+    def _():
+        copies = mid_loads()
+        for copy in copies:
+            copy.wait()
+        last = pltpu.make_async_copy(mates_d.at[:, :, 2 - c], two_ffn.at[pl.ds(11, 1)], sum_sems[0])
+        last.start()
+        last.wait()
+
+        def add_own(p, carry):
+            value = own_ffn[p].astype(WIDE) + one_ffn[p].astype(WIDE) + two_ffn[p].astype(WIDE)
+            own_ffn[p] = value.astype(NARROW)
+            return carry
+
+        lax.fori_loop(0, 12, add_own, 0)
+
+    for step in steps[1:]:
+        step.finish()
+
+    @pl.when(at.is_end)
+    def _():
+        for copy in end_loads():
+            copy.wait()
+
+        def add_own(first, other):
+            def body(q, carry):
+                own_ffn[first + q] = add(own_ffn[first + q], other[q])
+                return carry
+
+            return body
+
+        lax.fori_loop(0, 6, add_own(0, two_ffn), 0)
+        lax.fori_loop(0, 5, add_own(6, outer_c), 0)
+        lax.fori_loop(0, 1, add_own(11, outer_d), 0)
+
     trades = []
     places = ((at.row, at.fy), (at.cross, at.fd), (at.core, at.fs))
 
@@ -1201,17 +1447,37 @@
         for device, k in places:
             trades.append(post.send(mine(k), out.at[f], device, out.at[k]))
 
-    trade(lambda k: own_ffn.at[:, k], ffn_sums)
+    def trade_chunks(n):
+        for j in range(4):
+            post.keep(own_ffn.at[3 * j + n, f], home_sums[n].at[f, j])
+            for device, k in places:
+                trades.append(
+                    post.send(own_ffn.at[3 * j + n, k], home_sums[n].at[f, j], device, home_sums[n].at[k, j])
+                )
+
+    for n in range(3):
+        trade_chunks(n)
     far_attn_sent.arrive()
     for k in range(4):
         value = own_attn[k].astype(WIDE) + got_attn[0, k].astype(WIDE) + end_attn[k].astype(WIDE)
         own_attn[k] = value.astype(NARROW)
-    trade(lambda k: own_attn.at[k], attn_sums)
+    span = home_sums[3].shape[1]
+    trade(lambda k: own_attn.at[k, pl.ds(0, span)], home_sums[3])
+    trade(lambda k: own_attn.at[k, pl.ds(span, home_sums[4].shape[1])], home_sums[4])
     for sent in trades:
         sent.arrive()
     for arrive in moved:
         arrive()
     swap.finish()
+
+
+def home_kernel(gate, up, down, qkv, out, gate_out, up_out, down_out, qkv_out, out_out):
+    for source, target in ((gate, gate_out), (up, up_out), (qkv, qkv_out)):
+        for n in range(source.shape[0] // 512):
+            place = pl.ds(n * 512, 512)
+            target[:, place] = source[place, :].astype(WIDE).T
+    down_out[...] = down[...].astype(WIDE)
+    out_out[...] = out[...].astype(WIDE)
 
 
 def near_body(
@@ -1221,158 +1487,161 @@
     own = micro * rows
     ff = w_gate.shape[1]
     chunk = ff // 16
-    table, marks, gains = small_arrays(block_ids, positions, attn_gain, ffn_gain)
-    (
-        x_own, cot_own, attn_in, tables, all_marks, all_gains, qkv_all, out_all, gate_lvl, up_lvl, down_lvl,
-    ) = call(
+    shards = (w_gate, w_up, w_down)
+    marks, gains = small_arrays(block_ids, positions, attn_gain, ffn_gain)
+    inverse = THETA ** (-(jnp.arange(HALF, dtype=WIDE) * 2.0 / HEAD_DIM))
+    inverse = jnp.broadcast_to(jnp.concatenate([inverse, inverse]), (8, HEAD_DIM))
+    level_shapes = [shape(4, LANES, chunk), shape(4, LANES, chunk), shape(4, chunk, LANES)]
+    whole_shapes = [shape(4, 4, LANES, chunk), shape(4, 4, LANES, chunk), shape(4, 4, chunk, LANES)]
+    gains_shape = (4, 4, *gains.shape)
+    x_own, cot_own, attn_in, all_marks, all_gains, qkv_all, out_all, *level = call(
         start_kernel,
         "start",
         [
             shape(own, width), shape(own, width), shape(8, own, width),
-            shape(4, *table.shape, dtype=WIDE), shape(4, *marks.shape, dtype=WIDE),
-            shape(4, 4, *gains.shape, dtype=WIDE),
+            shape(4, *marks.shape, dtype=WIDE), shape(*gains_shape, dtype=WIDE),
             shape(4, 4, LANES, wqkv.shape[1] // 4), shape(4, 4, wo.shape[0] // 4, LANES),
-            shape(4, 4, LANES, chunk), shape(4, 4, LANES, chunk), shape(4, 4, chunk, LANES),
+            *level_shapes, *level_shapes,
         ],
-        (
-            hidden_in.reshape(own, width), cotangent.reshape(own, width), table, marks, gains,
-            wqkv, wo, w_gate, w_up, w_down,
-        ),
-        [pltpu.VMEM((own, width), NARROW), pltpu.VMEM((own, width), NARROW), pltpu.VMEM((4, 4, 8, LANES), WIDE)],
-        80, 32, 1,
+        (hidden_in.reshape(own, width), cotangent.reshape(own, width), marks, gains, wqkv, wo, *shards),
+        [pltpu.VMEM((own, width), NARROW), pltpu.VMEM((own, width), NARROW), pltpu.VMEM(gains_shape, WIDE)],
+        72, 24, 1,
     )
-    levels = (gate_lvl, up_lvl, down_lvl)
-    jobs_a = Jobs((0, 0), (1, 0))
-    jobs_b = Jobs((2, 0), (0, 1), (1, 1), (2, 1))
-    jobs_c = Jobs(*((a, j) for j in (2, 3) for a in range(3)))
-    queries, keys, values, mixed, dy, *climb_a = call(
-        functools.partial(attend_kernel, jobs_a),
+    queries, keys, values, mixed, dy, *more = call(
+        attend_kernel,
         "attend",
         [
             shape(2, 1024, 256), shape(2, 1024, 128), shape(2, 1024, 128), shape(8, own, 256),
-            shape(8, own, width), *jobs_a.shapes(levels),
+            shape(8, own, width), *whole_shapes, *level_shapes,
         ],
-        (attn_in, qkv_all, tables, all_marks, cot_own, *levels),
+        (attn_in, qkv_all, inverse, all_marks, cot_own, *shards, *level[:3]),
         [
             pltpu.VMEM((2, 8, ROWS, width), NARROW), pltpu.VMEM(qkv_all.shape, NARROW),
-            pltpu.VMEM(tables.shape, WIDE), pltpu.VMEM(all_marks.shape, WIDE),
+            pltpu.VMEM(inverse.shape, WIDE), pltpu.VMEM(all_marks.shape, WIDE),
             pltpu.VMEM((2, 1024, 256), NARROW), pltpu.VMEM((2, 1024, 128), NARROW),
             pltpu.VMEM((2, 1024, 128), NARROW), pltpu.VMEM((8, own, 256), NARROW),
         ],
         40, 24, 2,
     )
-    mid_own, ffn_in, *climb_b = call(
-        functools.partial(middle_kernel, jobs_b),
+    whole, level = more[:3], level + more[3:]
+    mid_own, ffn_in, *more = call(
+        middle_kernel,
         "middle",
-        [shape(own, width, dtype=WIDE), shape(8, own, width), *jobs_b.shapes(levels)],
-        (mixed, out_all, x_own, all_gains, *levels),
+        [
+            shape(own, width, dtype=WIDE), shape(8, own, width), *whole_shapes, whole_shapes[0], *level_shapes,
+        ],
+        (mixed, out_all, x_own, all_gains, *shards, *level[3:7]),
         [
             pltpu.VMEM((8, own, 256), NARROW), pltpu.VMEM((256, width), NARROW),
-            pltpu.VMEM((own, width), NARROW), pltpu.VMEM((4, 4, 8, LANES), WIDE),
+            pltpu.VMEM((own, width), NARROW), pltpu.VMEM(gains_shape, WIDE),
             pltpu.VMEM((2, ROWS, width), NARROW), *Fold.scratch(width),
         ],
-        60, 40, 3,
+        52, 32, 3,
     )
-    have = dict(zip(jobs_a.wanted + jobs_b.wanted, climb_a + climb_b))
-    hidden, grads_pre, parts, *climb_c = call(
-        functools.partial(ffn_kernel, jobs_c),
+    whole, level = whole + more[:4], level + more[4:]
+    hidden, grads_pre, parts, ends_a, ends_b, mates_a, *more = call(
+        ffn_kernel,
         "ffn",
         [
             shape(8, own, ff // 4), shape(8, own, ff // 2), shape(12, 4, 4, chunk, LANES),
-            *jobs_c.shapes(levels),
+            shape(3, 4, 3, chunk, LANES), shape(3, 4, 3, chunk, LANES), shape(3, 4, 2, chunk, LANES),
+            *whole_shapes[1:], *whole_shapes,
         ],
-        (ffn_in, dy, *(have[a, j] for j in range(2) for a in range(3)), *levels),
+        (ffn_in, dy, *whole, *level[7:]),
         [
             pltpu.VMEM((8, own, width), NARROW), pltpu.VMEM((8, own, width), NARROW),
             pltpu.VMEM((2, 4, 4, LANES, chunk), NARROW), pltpu.VMEM((2, 4, 4, LANES, chunk), NARROW),
             pltpu.VMEM((2, chunk, width), NARROW), pltpu.VMEM((3, 8, own, chunk), NARROW),
             pltpu.VMEM((3, chunk, 8 * own), NARROW), pltpu.VMEM((3, 16, chunk, LANES), NARROW),
+            *middle_scratch(1, 3),
         ],
-        24, 160, 4,
+        48, 160, 4,
     )
-    have.update(zip(jobs_c.wanted, climb_c))
-    count_a = 7
+    whole = whole + more
     fold_scratch = Fold.scratch(width)
-    grad_mid_own, grad_mid, gain_ffn_part, got_a = call(
-        functools.partial(back_kernel, 0, count_a),
+    grad_mid_own, grad_mid, gain_ffn_part, ends_c, mates_b, outer_a = call(
+        back_kernel,
         "back",
         [
             shape(own, width, dtype=WIDE), shape(8, own, width), shape(8, width, dtype=WIDE),
-            shape(count_a, 2, 4, chunk, LANES),
+            shape(5, 4, 3, chunk, LANES), shape(3, 4, 2, chunk, LANES), shape(3, 4, chunk, LANES),
         ],
-        (
-            grads_pre, mid_own, cot_own, all_gains, parts,
-            *(have[a, j] for a in range(2) for j in range(4)),
-        ),
+        (grads_pre, mid_own, cot_own, all_gains, parts, ends_b, mates_a, *whole[0::3], *whole[1::3]),
         [
             pltpu.VMEM((8, own, ff // 2), NARROW), pltpu.VMEM((4, 4, LANES, ff // 2), NARROW),
             pltpu.VMEM((own, width), WIDE), pltpu.VMEM((own, width), NARROW),
-            pltpu.VMEM((4, 4, 8, LANES), WIDE), pltpu.VMEM((2, ROWS, width), NARROW),
-            pltpu.VMEM((8, width), WIDE), *fold_scratch,
+            pltpu.VMEM(gains_shape, WIDE), pltpu.VMEM((2, ROWS, width), NARROW),
+            pltpu.VMEM((8, width), WIDE), *middle_scratch(1, 3), *middle_scratch(2, 3), *fold_scratch,
         ],
         48, 32, 5,
     )
-    grad_proj, parts_attn, hidden_out, got_b = call(
-        functools.partial(attend_back_kernel, count_a, 12 - count_a),
+    grad_proj, parts_attn, hidden_out, ends_d, mates_c, outer_b = call(
+        attend_back_kernel,
         "attend_back",
         [
             shape(8, own, 512), shape(4, 4, 768, LANES), shape(own, width),
-            shape(12 - count_a, 2, 4, chunk, LANES),
+            shape(1, 4, 3, chunk, LANES), shape(5, 4, 2, chunk, LANES), shape(3, 4, chunk, LANES),
         ],
         (
-            grad_mid, queries, keys, values, all_marks, tables, out_all, mixed, attn_in, hidden, mid_own, parts,
-            *(have[2, j] for j in range(4)),
+            grad_mid, queries, keys, values, all_marks, inverse, out_all, mixed, attn_in, hidden, mid_own, parts,
+            ends_c, mates_b, *whole[2::3],
         ),
         [
             pltpu.VMEM((8, own, width), NARROW), pltpu.VMEM((2, 1024, 256), NARROW),
             pltpu.VMEM((2, 1024, 128), NARROW), pltpu.VMEM((2, 1024, 128), NARROW),
-            pltpu.VMEM(all_marks.shape, WIDE), pltpu.VMEM(tables.shape, WIDE),
+            pltpu.VMEM(all_marks.shape, WIDE), pltpu.VMEM(inverse.shape, WIDE),
             pltpu.VMEM((256, width), NARROW), pltpu.VMEM((8, own, 256), NARROW),
             pltpu.VMEM((8, own, ff // 4), NARROW), pltpu.VMEM((ff // 4, width), NARROW),
             pltpu.VMEM((8, own, 512), NARROW), pltpu.VMEM((1024, 128), WIDE),
-            pltpu.VMEM((1024, 128), WIDE), pltpu.VMEM((256, 8 * own), NARROW),
-            pltpu.VMEM((512, 8 * own), NARROW), pltpu.VMEM((2, 8, own, TILE), NARROW),
+            pltpu.VMEM((1024, 128), WIDE),
             pltpu.VMEM((4, 4, 768, LANES), NARROW), pltpu.VMEM((own, width), WIDE),
-            pltpu.VMEM((own, width), NARROW), *fold_scratch,
+            pltpu.VMEM((own, width), NARROW), *middle_scratch(1, 5), *middle_scratch(2, 3), *fold_scratch,
         ],
         32, 128, 6,
     )
-    out_home, grad_home, gain_sums, ffn_sums, attn_sums = call(
+    out_home, grad_home, gain_sums, _, *sums = call(
         end_kernel,
         "end",
         [
             shape(own, width), shape(own, width), shape(8, LANES, dtype=WIDE),
-            shape(4, 12, chunk, LANES), shape(4, 768, LANES),
+            shape(1, 4, 2, chunk, LANES), *[shape(4, 4, chunk, LANES)] * 3, shape(4, 256, LANES), shape(4, 512, LANES),
         ],
         (
-            grad_proj, qkv_all, x_own, all_gains, grad_mid_own, hidden_out, gain_ffn_part, parts, got_a, got_b, parts_attn
+            grad_proj, qkv_all, x_own, all_gains, grad_mid_own, hidden_out, gain_ffn_part, parts, parts_attn,
+            ends_a, ends_b, ends_c, ends_d, mates_a, mates_b, mates_c, outer_a, outer_b,
         ),
         [
             pltpu.VMEM((8, own, 512), NARROW), pltpu.VMEM(qkv_all.shape, NARROW),
-            pltpu.VMEM((own, width), NARROW), pltpu.VMEM((4, 4, 8, LANES), WIDE),
+            pltpu.VMEM((own, width), NARROW), pltpu.VMEM(gains_shape, WIDE),
             pltpu.VMEM((own, width), WIDE), pltpu.VMEM((own, width), NARROW),
             pltpu.VMEM((8, width), WIDE), pltpu.VMEM((5, 8, width), WIDE),
-            *[pltpu.VMEM((12, 4, chunk, LANES), NARROW)] * 5,
+            *[pltpu.VMEM((12, 4, chunk, LANES), NARROW)] * 3,
+            pltpu.VMEM((5, 4, chunk, LANES), NARROW), pltpu.VMEM((1, 4, chunk, LANES), NARROW),
             pltpu.VMEM((4, 768, LANES), NARROW), pltpu.VMEM((4, 768, LANES), NARROW),
             pltpu.VMEM((2, 4, 768, LANES), NARROW), pltpu.VMEM((4, 768, LANES), NARROW),
-            *fold_scratch,
+            *middle_scratch(1, 1), *middle_scratch(2, 5), *middle_scratch(2, 1), *fold_scratch,
         ],
-        40, 40, 7,
+        80, 64, 7,
     )
-    grads = ffn_sums.reshape(4, 4, 3, chunk, LANES).transpose(2, 0, 1, 3, 4)
-    grads = grads.reshape(3, ff, LANES)
-    grad_qkv = attn_sums[:, 256:].reshape(-1, LANES)
-    grad_out = attn_sums[:, :256].reshape(-1, LANES)
+    gate, up, down, out, qkv = (array.reshape(-1, LANES) for array in sums)
+    grad_gate, grad_up, grad_down, grad_qkv, grad_out = pl.pallas_call(
+        home_kernel,
+        out_shape=[
+            jax.ShapeDtypeStruct(array.shape, WIDE) for array in (w_gate, w_up, w_down, wqkv, wo)
+        ],
+        compiler_params=pltpu.CompilerParams(vmem_limit_bytes=48 << 20),
+        name="home",
+    )(gate, up, down, qkv, out)
     return (
         out_home.reshape(hidden_in.shape),
         grad_home.reshape(hidden_in.shape),
         gain_sums[0],
-        grad_qkv.T.astype(WIDE),
-        grad_out.astype(WIDE),
+        grad_qkv,
+        grad_out,
         gain_sums[1],
-        grads[0].T.astype(WIDE),
-        grads[1].T.astype(WIDE),
-        grads[2].astype(WIDE),
+        grad_gate,
+        grad_up,
+        grad_down,
     )
 
 

time: 875 us -> 798 us (0.912)
  Pallas kernels: 833 us -> 775 us
    pallas_call x7, Pallas kernels: 833 us -> 771 us  [call(): pl.pallas_call(inner, out_shape=outs, in_specs=[ANYWHERE] * n_in, out_spe...]
where the time goes in v3:
time: 798 us; the launch traced here: 788 us
  Pallas kernels  775 us (97%)
  local copies, waits for them, and re-layouts  11.4 us (1%)
    pallas_call x7, Pallas kernels, call(): pl.pallas_call(inner, out_shape=outs, in_specs=[ANYWHERE] * n_in, out_spe...  771 us

profile of v3, /device:TPU:1, one launch (start us, length us, event | category | flops | bytes accessed | tf_op | source)
XLA Modules:
  0.0 788.4 jit_solution(7167005262298212272)
XLA Ops:
  0.6 0.0 copy-start
  0.7 0.1 pad_maximum_fusion
  0.8 0.6 copy-done
  1.3 0.7 copy_bitcast_fusion
  2.0 0.6 broadcast_in_dim.3.refs_2_.refs_5_
  2.6 0.6 pad.10.refs_2_
  3.2 1.3 fusion.3.refs_3_
  4.5 117.6 %start.1 = (bf16[256,2048]{1,0:T(8,128)(2,1)}, bf16[256,2048]{1,0:T(8,128)(2,1)}, bf16[8,256,2048]{2,1,0:T(8,128)(2,1)}, f32[4,8,256]{2,1,0:T(8,128)}, f32[4,4,8...) custom-call(bf16[256,2048]{1,0:T(8,128)(2,1)} %bitcast.28, ...), custom_call_target="tpu_custom_call" | custom-call | tf_op jit(solution)/shard_map/start/pallas_call | solution.py:660
  122.1 75.6 %attend.1 = (bf16[2,1024,256]{2,1,0:T(8,128)(2,1)}, bf16[2,1024,128]{2,1,0:T(8,128)(2,1)}, bf16[2,1024,128]{2,1,0:T(8,128)(2,1)}, bf16[8,256,256]{2,1,0:T(8,128)...) custom-call(bf16[8,256,2048]{2,1,0:T(8,128)(2,1)} %get-tuple-element, ...), custom_call_target="tpu_custom_call" | custom-call | tf_op jit(solution)/shard_map/attend/pallas_call | solution.py:660
  197.7 90.5 %middle.1 = (f32[256,2048]{1,0:T(8,128)}, bf16[8,256,2048]{2,1,0:T(8,128)(2,1)}, bf16[4,4,128,256]{3,2,1,0:T(8,128)(2,1)}, bf16[4,4,128,256]{3,2,1,0:T(8,128)(2,...) custom-call(bf16[8,256,256]{2,1,0:T(8,128)(2,1)} %get-tuple-element., ...), custom_call_target="tpu_custom_call" | custom-call | tf_op jit(solution)/shard_map/middle/pallas_call | solution.py:660
  288.2 132.2 %ffn.1 = (bf16[8,256,1024]{2,1,0:T(8,128)(2,1)}, bf16[8,256,2048]{2,1,0:T(8,128)(2,1)}, bf16[12,4,4,256,128]{4,3,2,1,0:T(8,128)(2,1)}, bf16[3,4,3,256,128]{4,3,2...) custom-call(bf16[8,256,2048]{2,1,0:T(8,128)(2,1)} %get-tuple-element, ...), custom_call_target="tpu_custom_call" | custom-call | tf_op jit(solution)/shard_map/ffn/pallas_call | solution.py:660
  420.4 97.6 %back.1 = (f32[256,2048]{1,0:T(8,128)}, bf16[8,256,2048]{2,1,0:T(8,128)(2,1)}, f32[8,2048]{1,0:T(8,128)}, bf16[5,4,3,256,128]{4,3,2,1,0:T(8,128)(2,1)}, bf16[3,4...) custom-call(bf16[8,256,2048]{2,1,0:T(8,128)(2,1)} %get-tuple-element.107.refs_0_, ...), custom_call_target="tpu_custom_call" | custom-call | tf_op jit(solution)/shard_map/back/pallas_call | solution.py:660
  518.0 71.4 %attend_back.1 = (bf16[8,256,512]{2,1,0:T(8,128)(2,1)}, bf16[4,4,768,128]{3,2,1,0:T(8,128)(2,1)}, bf16[256,2048]{1,0:T(8,128)(2,1)}, bf16[1,4,3,256,128]{4,3,2,1...) custom-call(bf16[8,256,2048]{2,1,0:T(8,128)(2,1)} %get-tuple-element.115.refs_0_, ...), custom_call_target="tpu_custom_call" | custom-call | tf_op jit(solution)/shard_map/attend_back/pallas_call | solution.py:660
  589.5 186.4 %end.1 = (bf16[256,2048]{1,0:T(8,128)(2,1)}, bf16[256,2048]{1,0:T(8,128)(2,1)}, f32[8,128]{1,0:T(8,128)}, bf16[1,4,2,256,128]{4,3,2,1,0:T(8,128)(2,1)}, bf16[4,4...) custom-call(bf16[8,256,512]{2,1,0:T(8,128)(2,1)} %get-tuple-element., ...), custom_call_target="tpu_custom_call" | custom-call | tf_op jit(solution)/shard_map/end/pallas_call | solution.py:660
  775.9 1.3 slice_bitcast_fusion
  777.1 0.0 copy-start.2
  777.1 1.2 copy-done.2
  778.4 0.0 copy-start.3
  778.4 1.2 copy-done.3
  779.6 0.0 copy-start.4
  779.6 1.2 copy-done.4
  780.8 0.0 copy-start.5
  780.8 1.0 copy-done.5
  781.9 0.0 copy-start.6
  781.9 0.9 copy-done.6
  782.8 0.0 copy-start.8
  782.8 0.0 copy-start.7
  782.8 0.0 copy-start.1
  782.8 3.5 home.1
  786.3 0.0 copy-done.8
  786.3 1.0 copy.28
  787.2 0.0 copy-done.7
  787.2 1.0 copy.29
  788.2 0.0 copy-done.1
  (3 shorter events, 0.0 us)
Async XLA Ops:
  0.6 0.7 copy-start
  777.1 1.2 copy-start.2
  778.4 1.2 copy-start.3
  779.6 1.2 copy-start.4
  780.8 1.0 copy-start.5
  781.9 0.9 copy-start.6
  782.8 3.5 copy-start.8
  782.8 4.4 copy-start.7
  782.8 5.4 copy-start.1

commit v4 on v3

--- a/solution.py
+++ b/solution.py
@@ -273,6 +273,11 @@
         self.is_end, self.is_mid = c * (3 - c) == 0, c * (3 - c) != 0
         self.c_near, self.c_mate, self.c_outer = 1 + c // 3, 3 - c, 3 * c - 3
         self.z3 = (f, 3 - c, t)
+        self.core_side, self.row_side = (fs, c, 1 - t), (fy, c, 1 - t)
+        self.cross_side = (fd, c, 1 - t)
+        self.level = (
+            self.side, self.core, self.row, self.cross, self.core_side, self.row_side, self.cross_side
+        )
         y, k, high, low = f // 2, f % 2, c // 2, c % 2
         self.to_f, to_c = (low + y) % 2 * 2 + high, k * 2 + y
         self.to = (self.to_f, to_c, t)
@@ -455,38 +460,39 @@
             pltpu.VMEM((4, ROWS, width), WIDE),
         ]
 
-    def to_core(self, slot, block):
-        self.give[slot] = self.part(block).astype(NARROW)
-        return self.post.send(self.give.at[slot], self.got.at[slot], self.at.core, self.got.at[slot])
+    def pair(self, slot, for_core, for_own):
+        both = self.part(for_core, for_own)
+        self.give[slot] = both[: 2 * ROWS].astype(NARROW)
+        sent = self.post.send(
+            self.give.at[slot], self.got.at[slot], self.at.core, self.got.at[slot]
+        )
+        return sent, both[2 * ROWS :]
+
+    def add_core(self, slot, pair):
+        sent, value = pair
+        sent.arrive()
+        return value + self.got[slot].astype(WIDE)
 
     def first(self):
         at, post = self.at, self.post
-        sent = self.to_core(3, at.b_core_far)
-        value = self.part(at.b_far)
-        sent.arrive()
-        value = (value + self.got[3].astype(WIDE)).astype(NARROW)
+        far = self.pair(3, at.b_core_far, at.b_far)
+        side = self.pair(1, at.b_core_side, at.b_side)
+        value = self.add_core(3, far).astype(NARROW)
         self.far[0] = value[:ROWS]
         self.far[1] = value[ROWS:]
         self.far_x = post.send(self.far.at[0], self.gx.at[0], at.side, self.gx.at[0])
         self.far_y = post.send(self.far.at[1], self.gy.at[0], at.row, self.gy.at[0])
-        sent = self.to_core(1, at.b_core_side)
-        value = self.part(at.b_side)
-        sent.arrive()
-        value = value + self.got[1].astype(WIDE)
+        row = self.pair(2, at.b_core_row, at.b_row)
+        value = self.add_core(1, side)
         self.side[0] = value[:ROWS].astype(NARROW)
         self.held[2] = value[ROWS:]
         self.side_x = post.send(self.side.at[0], self.gx.at[1], at.side, self.gx.at[1])
-        sent = self.to_core(2, at.b_core_row)
-        value = self.part(at.b_row)
-        sent.arrive()
-        value = value + self.got[2].astype(WIDE)
+        own = self.pair(0, at.b_core, at.b)
+        value = self.add_core(2, row)
         self.row[1] = value[ROWS:].astype(NARROW)
         self.held[3] = value[:ROWS]
         self.row_y = post.send(self.row.at[1], self.gy.at[1], at.row, self.gy.at[1])
-        sent = self.to_core(0, at.b_core)
-        value = self.part(at.b)
-        sent.arrive()
-        value = value + self.got[0].astype(WIDE)
+        value = self.add_core(0, own)
         self.held[0] = value[:ROWS]
         self.held[1] = value[ROWS:]
 
@@ -572,7 +578,8 @@
 
 
 class Ends:
-    def __init__(self, post, at, parts, first, got):
+    def __init__(self, post, at, parts, first, got, start=0, count=None):
+        count = got.shape[0] if count is None else count
         self.gates = [
             Gate(
                 post, at.is_end, at.is_mid,
@@ -581,7 +588,7 @@
                 ),
                 lambda q=q: got.at[q],
             ).start()
-            for q in range(got.shape[0])
+            for q in range(start, start + count)
         ]
 
     def finish(self):
@@ -724,7 +731,7 @@
 
 def meet_swap(at):
     bar = pltpu.get_barrier_semaphore()
-    partners = (at.side, at.core, at.row, at.cross, at.z1, at.z2, at.z3)
+    partners = (*at.level, at.z1, at.z2, at.z3)
     for device in partners:
         pl.semaphore_signal(bar, inc=1, device_id=device, device_id_type=MESH)
 
@@ -762,8 +769,8 @@
 
 
 def start_kernel(post, at, ins, outs, scratch):
-    hidden, cot, marks, gains, wqkv, wo, *shards = ins
-    x_own, cot_own, attn_in, all_marks, all_gains, qkv_all, out_all, *levels_out = outs
+    hidden, marks, gains, wqkv, wo, *shards = ins
+    x_own, attn_in, all_marks, all_gains, qkv_all, out_all, *levels_out = outs
     rows_in, rows_out, gain_buf = scratch
     f, c = at.f, at.c
     meet_swap(at)
@@ -833,7 +840,6 @@
     for far, close, there, out in levels:
         far.arrive()
         forwards.append((post.send(there, there, at.z1, out.at[:, at.c3]), close))
-    cot_moved = [swap(cot.at[half], cot_own.at[half], cot_own.at[half]) for half in HALVES]
     deals = [Deal(post, at, shards, j, levels_out[3 * j : 3 * j + 3]) for j in range(2)]
     spread.corner()
     for last, close in forwards:
@@ -843,8 +849,6 @@
     smaller.arrive()
     for deal in deals:
         deal.finish()
-    for arrive in cot_moved:
-        arrive()
     swap.finish()
 
 
@@ -901,12 +905,14 @@
 
 
 def attend_kernel(post, at, ins, outs, scratch):
-    attn_in, qkv_all, inverse_in, marks_in, cot_own, *shards = ins[:8]
+    attn_in, qkv_all, inverse_in, marks_in, cot, *shards = ins[:8]
     levels = ins[8:]
-    queries, keys, values, mixed, dy, *more = outs
+    queries, keys, values, mixed, dy, cot_own, *more = outs
     climbed, dealt = more[: len(levels)], more[len(levels) :]
     rows, weight, inverse, marks, q_buf, k_buf, v_buf, mix_buf = scratch
-    meet((at.side, at.core, at.row, at.cross, at.z1, at.z2))
+    meet_swap(at)
+    swap = Swap(post, at)
+    cot_moved = [swap(cot.at[half], cot_own.at[half], cot_own.at[half]) for half in HALVES]
     local = [
         post.keep(inverse_in, inverse),
         post.keep(marks_in, marks),
@@ -915,9 +921,6 @@
         post.keep(attn_in.at[:, pl.ds(ROWS, ROWS)], rows.at[1]),
     ]
     spread = Spread(post, at, dy)
-    for half in range(2):
-        spread.own(half, cot_own.at[pl.ds(half * ROWS, ROWS)])
-    climbs = [Climb(post, at, level, out) for level, out in zip(levels, climbed)]
     deal = Deal(post, at, shards, 2, dealt)
     post.settle(local)
     width = rows.shape[-1]
@@ -934,7 +937,6 @@
                 q_buf[m, place, lane] = rope(projected[:, lane], cos_full, sin_full).astype(NARROW)
             k_buf[m, place] = rope(projected[:, 256:384], cos_full, sin_full).astype(NARROW)
             v_buf[m, place] = projected[:, 384:512].astype(NARROW)
-    spread.relay(0)
     for m in range(2):
         for i in range(4):
             n = min(i + 2, 4) * TILE
@@ -952,16 +954,22 @@
                         h * ROWS : (h + 1) * ROWS
                     ]
         if m == 0:
-            spread.relay(1)
-            for climb in climbs:
-                climb.forward()
+            climbs = [Climb(post, at, level, out) for level, out in zip(levels, climbed)]
     for source, target in ((q_buf, queries), (k_buf, keys), (v_buf, values), (mix_buf, mixed)):
         post.keep(source, target)
+    for half in range(2):
+        cot_moved[half]()
+        spread.own(half, cot_own.at[HALVES[half]])
+    spread.relay(0)
+    spread.relay(1)
+    for climb in climbs:
+        climb.forward()
     spread.corner()
     spread.finish()
     for climb in climbs:
         climb.finish()
     deal.finish()
+    swap.finish()
 
 
 def middle_kernel(post, at, ins, outs, scratch):
@@ -979,8 +987,8 @@
     post.settle(local)
     climbs = [Climb(post, at, level, out) for level, out in zip(levels, climbed)]
 
-    def part(block):
-        return mm(mix_buf[block], weight[...])
+    def part(*blocks):
+        return mm(jnp.concatenate([mix_buf[block] for block in blocks]), weight[...])
 
     fold = Fold(post, at, part, fold_scratch)
     fold.first()
@@ -1019,10 +1027,10 @@
 
 def ffn_kernel(post, at, ins, outs, scratch):
     ffn_in, dy = ins[:2]
-    ready = ins[2:9]
-    levels = ins[9:]
-    hidden, grads_pre, parts, ends_a, ends_b, mates, *climbed = outs
-    x_buf, dy_buf, gate_buf, up_buf, down_buf, act, act_t, staged, *sum_bufs = scratch
+    ready = ins[2:10]
+    levels = ins[10:]
+    hidden, grads_pre, parts, ends_a, *climbed = outs
+    x_buf, dy_buf, gate_buf, up_buf, down_buf, act, act_t, staged = scratch
     meet((at.z1, at.z3))
     climbs = [LineClimb(post, at, level, out) for level, out in zip(levels, climbed)]
     local = [post.keep(ffn_in, x_buf), post.keep(dy, dy_buf)]
@@ -1045,7 +1053,7 @@
     for j in range(4):
         slot = j % 2
         if loading is None:
-            for climb in climbs[:2] if j == 2 else climbs[2:]:
+            for climb in climbs[:1] if j == 2 else climbs[1:]:
                 climb.finish()
             loading = load(j)
         post.settle(loading)
@@ -1053,7 +1061,8 @@
         post.settle(saved)
 
         def rows(i, carry):
-            x, grad = x_buf[i], dy_buf[i]
+            blocks = pl.ds(i * 2, 2)
+            x, grad = (buf[blocks].reshape(2 * TILE, width) for buf in (x_buf, dy_buf))
             gate = mm(x, gate_buf[slot].reshape(width, -1))
             up = mm(x, up_buf[slot].reshape(width, -1))
             grad_hidden = mm(grad, down_buf[slot], ((1,), (1,)))
@@ -1064,13 +1073,13 @@
                 grad_hidden * silu,
                 silu * up,
             )
-            place = pl.ds(pl.multiple_of(i * TILE, TILE), TILE)
+            place = pl.ds(pl.multiple_of(i * 2 * TILE, 2 * TILE), 2 * TILE)
             for k in range(3):
-                act[k, i] = values[k].astype(NARROW)
+                act[k, blocks] = values[k].astype(NARROW).reshape(2, TILE, -1)
                 act_t[k, :, place] = values[k].T.astype(NARROW)
             return carry
 
-        lax.fori_loop(0, 8, rows, 0)
+        lax.fori_loop(0, 4, rows, 0)
         chunk = act.shape[-1]
         lane = pl.ds(j * chunk, chunk)
         saved = [
@@ -1078,17 +1087,17 @@
             post.keep(act.at[1], grads_pre.at[:, :, pl.ds((4 + j) * chunk, chunk)]),
             post.keep(act.at[2], hidden.at[:, :, lane]),
         ]
-        for climb in climbs[:2] if j == 1 else climbs[2:] if j == 2 else ():
+        for climb in climbs[:1] if j == 1 else climbs[1:] if j == 2 else ():
             climb.last()
-        for climb in climbs[:2] if j == 0 else climbs[2:] if j == 1 else ():
+        for climb in climbs[:1] if j == 0 else climbs[1:] if j == 1 else ():
             climb.forward()
 
         def sums(n, carry):
             place = pl.ds(pl.multiple_of(n * TILE, TILE), TILE)
             x = x_buf[:, :, place].reshape(8 * TILE, TILE)
             grad = dy_buf[:, :, place].reshape(8 * TILE, TILE)
-            for k in range(3):
-                value = mm(act_t[k], grad if k == 2 else x).astype(NARROW)
+            both = mm(act_t[0:2].reshape(2 * chunk, -1), x).astype(NARROW)
+            for k, value in enumerate((both[:chunk], both[chunk:], mm(act_t[2], grad).astype(NARROW))):
                 staged[k, 2 * n] = value[:, :LANES]
                 staged[k, 2 * n + 1] = value[:, LANES:]
             return carry
@@ -1101,15 +1110,11 @@
         ]
         if j < 2:
             post.settle(stored)
-            sums_0.append(Ends(post, at, parts, 3 * j, (ends_a, ends_b)[j]))
+            sums_0.append(Ends(post, at, parts, 0, ends_a, 3 * j, (3, 1)[j]))
         else:
             saved += stored
-        if j == 2:
-            sums_0[0].finish()
-            sums_1 = Middle(post, at, 1, parts, 0, ends_a, mates, *sum_bufs)
-            sums_1.send()
-    sums_0[1].finish()
-    sums_1.finish()
+    for step in sums_0:
+        step.finish()
 
 
 class Descend:
@@ -1130,15 +1135,14 @@
 
 
 def back_kernel(post, at, ins, outs, scratch):
-    grads_pre, mid_own, cot_own, gains_in, parts, ends_b, mates_a, *weights = ins
-    grad_mid_own, grad_mid, gain_part, ends_c, mates_b, outer_a = outs
+    grads_pre, mid_own, cot_own, gains_in, parts, ends_a, *weights = ins
+    grad_mid_own, grad_mid, gain_part, ends_c, mates_b = outs
     pre_buf, weight, mid_buf, cot_buf, gains, rows_out, gain_out = scratch[:7]
-    bufs_1, bufs_2, fold_scratch = scratch[7:9], scratch[9:11], scratch[11:]
+    bufs_1, fold_scratch = scratch[7:9], scratch[9:]
     meet((at.side, at.core, at.row, at.z1, at.z3))
     downs = [
-        Middle(post, at, 1, parts, 3, ends_b, mates_b, *bufs_1),
-        Middle(post, at, 2, parts, 0, mates_a, outer_a, *bufs_2),
-        Ends(post, at, parts, 6, ends_c),
+        Middle(post, at, 1, parts, 0, ends_a, mates_b, *bufs_1),
+        Ends(post, at, parts, 4, ends_c),
     ]
     chunk = pre_buf.shape[-1] // 8
     local = [post.keep(grads_pre, pre_buf)]
@@ -1150,11 +1154,11 @@
     post.settle(local)
     width = mid_buf.shape[-1]
 
-    def part(block):
-        return mm(pre_buf[block], weight[...].reshape(width, -1), ((1,), (1,)))
-
-    for down in downs[:2]:
-        down.send()
+    def part(*blocks):
+        rows = jnp.concatenate([pre_buf[block] for block in blocks])
+        return mm(rows, weight[...].reshape(width, -1), ((1,), (1,)))
+
+    downs[0].send()
     fold = Fold(post, at, part, fold_scratch)
     fold.first()
     fold.second()
@@ -1186,17 +1190,18 @@
         grad_mid, queries, keys, values, marks_in, inverse_in, out_all, mixed, attn_in, hidden, mid_own, parts,
         ends_c, mates_b, *downs_in
     ) = ins
-    grad_proj, parts_attn, hidden_out, ends_d, mates_c, outer_b = outs
+    grad_proj, parts_q, parts_o, got_o, out_home, ends_d, mates_c, outer_b = outs
     (
         gm_buf, q_buf, k_buf, v_buf, marks, inverse, weight, mix_buf, hid_buf, down_buf, gp_buf, gk_buf, gv_buf,
-        staged, mid_buf, out_buf
-    ) = scratch[:16]
-    bufs_1, bufs_2, fold_scratch = scratch[16:18], scratch[18:20], scratch[20:]
-    meet((at.side, at.core, at.row, at.z1, at.z3))
+        staged, staged_o, mid_buf, out_buf
+    ) = scratch[:17]
+    bufs_1, bufs_2, fold_scratch = scratch[17:19], scratch[19:21], scratch[21:]
+    meet_swap(at)
+    swap = Swap(post, at, home=True)
     steps = [
-        Middle(post, at, 1, parts, 6, ends_c, mates_c, *bufs_1),
-        Middle(post, at, 2, parts, 3, mates_b, outer_b, *bufs_2),
-        Ends(post, at, parts, 11, ends_d),
+        Middle(post, at, 1, parts, 4, ends_c, mates_c, *bufs_1),
+        Middle(post, at, 2, parts, 0, mates_b, outer_b, *bufs_2),
+        Ends(post, at, parts, 9, ends_d),
     ]
 
     chunk = hid_buf.shape[-1] // 4
@@ -1219,7 +1224,11 @@
     post.settle(early)
     for step in steps[:2]:
         step.send()
-    fold = Fold(post, at, lambda block: mm(hid_buf[block], down_buf[...]), fold_scratch)
+
+    def part(*blocks):
+        return mm(jnp.concatenate([hid_buf[block] for block in blocks]), down_buf[...])
+
+    fold = Fold(post, at, part, fold_scratch)
     fold.first()
     post.settle(late)
 
@@ -1233,6 +1242,16 @@
     mix_t, gp_t = down_buf.at[pl.ds(512, 256)], down_buf.at[pl.ds(0, 512)]
     fetched = fetch(0)
     width = gm_buf.shape[-1]
+    for i in range(8):
+        mix_t[:, i * TILE : (i + 1) * TILE] = mix_buf[i].astype(WIDE).T.astype(NARROW)
+    for n in range(8):
+        place = slice(n * TILE, (n + 1) * TILE)
+        value = mm(mix_t[...], gm_buf[:, :, place].reshape(8 * TILE, TILE)).astype(NARROW)
+        for h in range(2):
+            block = 2 * n + h
+            staged_o[block // 4, block % 4] = value[:, h * LANES : (h + 1) * LANES]
+    post.settle([post.keep(staged_o, parts_o)])
+    step_o = Descend(post, at, parts_o, got_o)
     for m in range(2):
         for i in range(4):
             q = quarter(at, i)
@@ -1263,6 +1282,12 @@
                 done = rope_back(grad_query, cos_full, sin_full).astype(NARROW)
                 for h in range(2):
                     gp_buf[2 * q + h, m * ROWS : (m + 1) * ROWS, lane] = done[h * ROWS : (h + 1) * ROWS]
+            if m == 1 and i == 1:
+                fold.third()
+                for half in HALVES:
+                    k = half.start // ROWS
+                    out_buf[half] = (fold.held[k] + mid_buf[half]).astype(NARROW)
+                moved = [swap(out_buf.at[half], out_home.at[half], out_home.at[half]) for half in HALVES]
         for i in range(4):
             q = quarter(at, i)
             place = slice(i * TILE, (i + 1) * TILE)
@@ -1278,108 +1303,166 @@
         if m == 0:
             fold.second()
     post.keep(gp_buf, grad_proj)
-    fold.third()
-    for half in range(2):
-        out_buf[HALVES[half]] = (fold.held[half] + mid_buf[HALVES[half]]).astype(NARROW)
-    post.keep(out_buf, hidden_out)
     for i in range(8):
         place = slice(i * TILE, (i + 1) * TILE)
-        mix_t[:, place] = mix_buf[i].astype(WIDE).T.astype(NARROW)
         gp_t[:, place] = gp_buf[i].astype(WIDE).T.astype(NARROW)
-    span = mix_t.shape[0]
     for n in range(8):
         post.settle([fetched])
         if n < 7:
             fetched = fetch(n + 1)
-        place = slice(n * TILE, (n + 1) * TILE)
-        value = mm(mix_t[...], gm_buf[:, :, place].reshape(8 * TILE, TILE)).astype(NARROW)
         other = mm(gp_t[...], column(n)[...].reshape(8 * TILE, TILE)).astype(NARROW)
         for h in range(2):
             block = 2 * n + h
-            lane = slice(h * LANES, (h + 1) * LANES)
-            staged[block // 4, block % 4, :span] = value[:, lane]
-            staged[block // 4, block % 4, span:] = other[:, lane]
-    post.keep(staged, parts_attn)
+            staged[block // 4, block % 4] = other[:, h * LANES : (h + 1) * LANES]
+    post.keep(staged, parts_q)
+    step_o.finish()
+    for arrive in moved:
+        arrive()
+    swap.finish()
     for step in steps:
         step.finish()
 
 
+class Own:
+    def __init__(self, post, at, parts, first, n, pieces, own, one, two):
+        self.post, self.at, self.first, self.n = post, at, first, n
+        self.own, self.one, self.two = own, one, two
+        self.pieces = pieces
+        count = 1 + max(len(pieces[0]) + len(pieces[1]), len(pieces[2]))
+        self.sems = [post.local_sems.at[post.n_local + k] for k in range(count)]
+        post.n_local += count
+        self.parts = parts
+
+        @pl.when(at.is_mid)
+        def _():
+            for copy in self.mid_copies():
+                copy.start()
+
+        @pl.when(at.is_end)
+        def _():
+            for copy in self.end_copies():
+                copy.start()
+
+    def laid(self, arrays, index, target):
+        place, pairs = self.first, []
+        for array in arrays:
+            n = array.shape[0]
+            source = array if index is None else array.at[:, :, index]
+            pairs.append((source, target.at[pl.ds(place, n)]))
+            place += n
+        return pairs
+
+    def copies(self, pairs):
+        rows = pl.ds(self.first, self.n)
+        pairs = [(self.parts.at[rows, :, self.at.c], self.own.at[rows])] + pairs
+        return [pltpu.make_async_copy(*pair, sem) for pair, sem in zip(pairs, self.sems)]
+
+    def mid_copies(self):
+        c = self.at.c
+        ends, mates, _ = self.pieces
+        return self.copies(self.laid(ends, 2 * (c - 1), self.one) + self.laid(mates, 2 - c, self.two))
+
+    def end_copies(self):
+        return self.copies(self.laid(self.pieces[2], None, self.two))
+
+    def add(self):
+        def both(p, carry):
+            value = self.own[p].astype(WIDE) + self.one[p].astype(WIDE) + self.two[p].astype(WIDE)
+            self.own[p] = value.astype(NARROW)
+            return carry
+
+        def single(p, carry):
+            self.own[p] = (self.own[p].astype(WIDE) + self.two[p].astype(WIDE)).astype(NARROW)
+            return carry
+
+        @pl.when(self.at.is_mid)
+        def _():
+            for copy in self.mid_copies():
+                copy.wait()
+            lax.fori_loop(self.first, self.first + self.n, both, 0)
+
+        @pl.when(self.at.is_end)
+        def _():
+            for copy in self.end_copies():
+                copy.wait()
+            lax.fori_loop(self.first, self.first + self.n, single, 0)
+
+
 def end_kernel(post, at, ins, outs, scratch):
     (
-        grad_proj, qkv_all, x_own, gains_in, grad_mid_own, hidden_out, gain_ffn_part, parts, parts_attn,
-        ends_a, ends_b, ends_c, ends_d, mates_a, mates_b, mates_c, outer_a, outer_b
+        grad_proj, qkv_all, x_own, gains_in, grad_mid_own, gain_ffn_part, parts, parts_q, parts_o, got_o,
+        ends_a, ends_c, ends_d, mates_b, mates_c, outer_b
     ) = ins
-    out_home, grad_home, gain_sums, mates_d, *home_sums = outs
+    grad_home, gain_sums, mates_d, outer_c, outer_d, *home_sums = outs
     (
-        gp_buf, weight, x_buf, gains, mid_buf, rows_out, gain_buf, gain_got,
-        own_ffn, one_ffn, two_ffn, outer_c, outer_d, own_attn, far_attn, got_attn, end_attn
-    ) = scratch[:17]
-    bufs_1, bufs_2, bufs_3, fold_scratch = scratch[17:19], scratch[19:21], scratch[21:23], scratch[23:]
+        gp_buf, weight, x_buf, gains, mid_buf, rows_out, gain_buf, gain_got, own_ffn, one_ffn, two_ffn,
+        own_q, far_q, got_q, end_q, own_o, far_o, one_o, two_o, end_o
+    ) = scratch[:20]
+    bufs_1, bufs_2, bufs_3, fold_scratch = scratch[20:22], scratch[22:24], scratch[24:26], scratch[26:]
     f, c = at.f, at.c
     meet_swap(at)
-    step_attn = Descend(post, at, parts_attn, got_attn)
+    step_q = Descend(post, at, parts_q, got_q)
     steps = [
-        Middle(post, at, 1, parts, 11, ends_d, mates_d, *bufs_1),
-        Middle(post, at, 2, parts, 6, mates_c, outer_c, *bufs_2),
+        Middle(post, at, 1, parts, 9, ends_d, mates_d, *bufs_1),
+        Middle(post, at, 2, parts, 4, mates_c, outer_c, *bufs_2),
     ]
     swap = Swap(post, at, home=True)
-    moved = [swap(hidden_out.at[half], out_home.at[half], out_home.at[half]) for half in HALVES]
+    for_o = [post.keep(parts_o.at[:, at.c2], far_o), post.keep(got_o.at[1], two_o)]
+    early = Own(
+        post, at, parts, 0, 4, ((ends_a,), (mates_b,), (outer_b,)),
+        own_ffn, one_ffn, two_ffn,
+    )
     fold_in = [
         post.keep(grad_proj, gp_buf), post.keep(qkv_all, weight), post.keep(x_own, x_buf),
         post.keep(gains_in, gains), post.keep(grad_mid_own, mid_buf),
         post.keep(gain_ffn_part, gain_buf),
     ]
     later = [
-        post.keep(parts.at[:, :, c], own_ffn),
-        post.keep(parts_attn.at[:, c], own_attn), post.keep(parts_attn.at[:, at.c2], far_attn),
+        post.keep(parts_q.at[:, c], own_q), post.keep(parts_q.at[:, at.c2], far_q),
+        post.keep(parts_o.at[:, c], own_o), post.keep(got_o.at[0], one_o),
     ]
-    sum_sems = [post.local_sems.at[post.n_local + k] for k in range(7)]
-    post.n_local += 7
-
-    def mid_loads():
-        pieces = [
-            (ends_a.at[:, :, 2 * (c - 1)], one_ffn.at[pl.ds(0, 3)]),
-            (ends_b.at[:, :, 2 * (c - 1)], one_ffn.at[pl.ds(3, 3)]),
-            (ends_c.at[:, :, 2 * (c - 1)], one_ffn.at[pl.ds(6, 5)]),
-            (ends_d.at[:, :, 2 * (c - 1)], one_ffn.at[pl.ds(11, 1)]),
-            (mates_a.at[:, :, 2 - c], two_ffn.at[pl.ds(0, 3)]),
-            (mates_b.at[:, :, 2 - c], two_ffn.at[pl.ds(3, 3)]),
-            (mates_c.at[:, :, 2 - c], two_ffn.at[pl.ds(6, 5)]),
-        ]
-        return [pltpu.make_async_copy(*piece, sem) for piece, sem in zip(pieces, sum_sems)]
-
-    def end_loads():
-        pieces = [(outer_a, two_ffn.at[pl.ds(0, 3)]), (outer_b, two_ffn.at[pl.ds(3, 3)])]
-        return [pltpu.make_async_copy(*piece, sem) for piece, sem in zip(pieces, sum_sems)]
-
-    @pl.when(at.is_mid)
-    def _():
-        for copy in mid_loads():
-            copy.start()
-
-    @pl.when(at.is_end)
-    def _():
-        for copy in end_loads():
-            copy.start()
-
     for step in steps:
         step.send()
-
-    def add(left, right):
-        return (left.astype(WIDE) + right.astype(WIDE)).astype(NARROW)
+    post.settle(for_o)
+
+    def add_far(far, came):
+        for k in range(4):
+            far[k] = (far[k].astype(WIDE) + came[k].astype(WIDE)).astype(NARROW)
+
+    def add_own(own, one, end):
+        for k in range(4):
+            own[k] = (own[k].astype(WIDE) + one[k].astype(WIDE) + end[k].astype(WIDE)).astype(NARROW)
+
+    add_far(far_o, two_o)
+    sent_o = post.send(far_o, end_o, at.z2, end_o)
+    trades = []
+    places = ((at.row, at.fy), (at.cross, at.fd), (at.core, at.fs))
+
+    def trade(mine, out, *place):
+        post.keep(mine(f), out.at[(f, *place)])
+        for device, k in places:
+            trades.append(
+                post.send(mine(k), out.at[(f, *place)], device, out.at[(k, *place)])
+            )
+
+    def trade_ffn(p):
+        trade(lambda k: own_ffn.at[p, k], home_sums[p % 3], p // 3)
 
     post.settle(fold_in)
     width = x_buf.shape[-1]
 
-    def part(block):
-        return mm(gp_buf[block], weight[...].reshape(width, -1), ((1,), (1,)))
+    def part(*blocks):
+        rows = jnp.concatenate([gp_buf[block] for block in blocks])
+        return mm(rows, weight[...].reshape(width, -1), ((1,), (1,)))
 
     fold = Fold(post, at, part, fold_scratch)
     fold.first()
+    early.add()
     fold.second()
     fold.third()
     gain = jnp.concatenate([gains[i // 4, i % 4, 0:1, :] for i in range(16)], axis=1)
     total = jnp.zeros((1, width), WIDE)
+    moved = []
     for half in range(2):
         rows = HALVES[half]
         back, piece = norm_back_rows(fold.held[half], x_buf[rows].astype(WIDE), gain)
@@ -1387,83 +1470,55 @@
         rows_out[rows] = (mid_buf[rows] + back).astype(NARROW)
         moved.append(swap(rows_out.at[rows], grad_home.at[rows], grad_home.at[rows]))
     gain_buf[0:1] = total
+    gain_sent = [
+        post.send(gain_buf, gain_got.at[k], device, gain_got.at[k])
+        for k, device in enumerate(at.level)
+    ]
+    for p in range(4):
+        trade_ffn(p)
     post.settle(later)
+    step_q.finish()
+    add_far(far_q, got_q.at[1])
+    sent_q = post.send(far_q, end_q, at.z2, end_q)
     steps[0].finish()
-    steps.append(Middle(post, at, 2, parts, 11, mates_d, outer_d, *bufs_3))
-    step_attn.finish()
-    for k in range(4):
-        far_attn[k] = add(far_attn[k], got_attn[1, k])
-    far_attn_sent = post.send(far_attn, end_attn, at.z2, end_attn)
+    steps.append(Middle(post, at, 2, parts, 9, mates_d, outer_d, *bufs_3))
     steps[2].send()
-    for k, device in enumerate((at.core, at.row, at.side, at.z1, at.z2)):
-        gain_sent = post.send(gain_buf, gain_got.at[k], device, gain_got.at[k])
-        gain_sent.arrive()
-        gain_sent.leave()
-        post.out.pop()
-        gain_buf[...] = gain_buf[...] + gain_got[k]
+    steps[1].finish()
+    late = Own(
+        post, at, parts, 4, 5, ((ends_c,), (mates_c,), (outer_c,)), own_ffn, one_ffn, two_ffn
+    )
+    sent_o.arrive()
+    add_own(own_o, one_o, end_o)
+    trade(lambda k: own_o.at[k], home_sums[3])
+    late.add()
+    for p in range(4, 9):
+        trade_ffn(p)
+    for sent in gain_sent:
+        sent.arrive()
+        sent.leave()
+    post.out = [sent for sent in post.out if not any(sent is gone for gone in gain_sent)]
+    gain_buf[...] = gain_buf[...] + sum(gain_got[k] for k in range(7))
+    gain_sent = [
+        post.send(gain_buf, gain_got.at[7 + k], device, gain_got.at[7 + k])
+        for k, device in enumerate((at.z1, at.z2, at.z3))
+    ]
+    steps[2].finish()
+    last = Own(
+        post, at, parts, 9, 3, ((ends_d,), (mates_d,), (outer_d,)), own_ffn, one_ffn, two_ffn
+    )
+    last.add()
+    for p in range(9, 12):
+        trade_ffn(p)
+    sent_q.arrive()
+    add_own(own_q, got_q.at[0], end_q)
+    trade(lambda k: own_q.at[k], home_sums[4])
+    for sent in gain_sent:
+        sent.arrive()
+        sent.leave()
+    post.out = [sent for sent in post.out if not any(sent is gone for gone in gain_sent)]
+    gain_buf[...] = gain_buf[...] + sum(gain_got[7 + k] for k in range(3))
     place = pl.ds(pl.multiple_of((f * 4 + c) * LANES, LANES), LANES)
     post.keep(gain_buf.at[:, place], gain_sums)
-
-    @pl.when(at.is_mid)
-    def _():
-        copies = mid_loads()
-        for copy in copies:
-            copy.wait()
-        last = pltpu.make_async_copy(mates_d.at[:, :, 2 - c], two_ffn.at[pl.ds(11, 1)], sum_sems[0])
-        last.start()
-        last.wait()
-
-        def add_own(p, carry):
-            value = own_ffn[p].astype(WIDE) + one_ffn[p].astype(WIDE) + two_ffn[p].astype(WIDE)
-            own_ffn[p] = value.astype(NARROW)
-            return carry
-
-        lax.fori_loop(0, 12, add_own, 0)
-
-    for step in steps[1:]:
-        step.finish()
-
-    @pl.when(at.is_end)
-    def _():
-        for copy in end_loads():
-            copy.wait()
-
-        def add_own(first, other):
-            def body(q, carry):
-                own_ffn[first + q] = add(own_ffn[first + q], other[q])
-                return carry
-
-            return body
-
-        lax.fori_loop(0, 6, add_own(0, two_ffn), 0)
-        lax.fori_loop(0, 5, add_own(6, outer_c), 0)
-        lax.fori_loop(0, 1, add_own(11, outer_d), 0)
-
-    trades = []
-    places = ((at.row, at.fy), (at.cross, at.fd), (at.core, at.fs))
-
-    def trade(mine, out):
-        post.keep(mine(f), out.at[f])
-        for device, k in places:
-            trades.append(post.send(mine(k), out.at[f], device, out.at[k]))
-
-    def trade_chunks(n):
-        for j in range(4):
-            post.keep(own_ffn.at[3 * j + n, f], home_sums[n].at[f, j])
-            for device, k in places:
-                trades.append(
-                    post.send(own_ffn.at[3 * j + n, k], home_sums[n].at[f, j], device, home_sums[n].at[k, j])
-                )
-
-    for n in range(3):
-        trade_chunks(n)
-    far_attn_sent.arrive()
-    for k in range(4):
-        value = own_attn[k].astype(WIDE) + got_attn[0, k].astype(WIDE) + end_attn[k].astype(WIDE)
-        own_attn[k] = value.astype(NARROW)
-    span = home_sums[3].shape[1]
-    trade(lambda k: own_attn.at[k, pl.ds(0, span)], home_sums[3])
-    trade(lambda k: own_attn.at[k, pl.ds(span, home_sums[4].shape[1])], home_sums[4])
     for sent in trades:
         sent.arrive()
     for arrive in moved:
@@ -1494,27 +1549,27 @@
     level_shapes = [shape(4, LANES, chunk), shape(4, LANES, chunk), shape(4, chunk, LANES)]
     whole_shapes = [shape(4, 4, LANES, chunk), shape(4, 4, LANES, chunk), shape(4, 4, chunk, LANES)]
     gains_shape = (4, 4, *gains.shape)
-    x_own, cot_own, attn_in, all_marks, all_gains, qkv_all, out_all, *level = call(
+    x_own, attn_in, all_marks, all_gains, qkv_all, out_all, *level = call(
         start_kernel,
         "start",
         [
-            shape(own, width), shape(own, width), shape(8, own, width),
+            shape(own, width), shape(8, own, width),
             shape(4, *marks.shape, dtype=WIDE), shape(*gains_shape, dtype=WIDE),
             shape(4, 4, LANES, wqkv.shape[1] // 4), shape(4, 4, wo.shape[0] // 4, LANES),
             *level_shapes, *level_shapes,
         ],
-        (hidden_in.reshape(own, width), cotangent.reshape(own, width), marks, gains, wqkv, wo, *shards),
+        (hidden_in.reshape(own, width), marks, gains, wqkv, wo, *shards),
         [pltpu.VMEM((own, width), NARROW), pltpu.VMEM((own, width), NARROW), pltpu.VMEM(gains_shape, WIDE)],
         72, 24, 1,
     )
-    queries, keys, values, mixed, dy, *more = call(
+    queries, keys, values, mixed, dy, cot_own, *more = call(
         attend_kernel,
         "attend",
         [
             shape(2, 1024, 256), shape(2, 1024, 128), shape(2, 1024, 128), shape(8, own, 256),
-            shape(8, own, width), *whole_shapes, *level_shapes,
+            shape(8, own, width), shape(own, width), *whole_shapes, *level_shapes,
         ],
-        (attn_in, qkv_all, inverse, all_marks, cot_own, *shards, *level[:3]),
+        (attn_in, qkv_all, inverse, all_marks, cotangent.reshape(own, width), *shards, *level[:3]),
         [
             pltpu.VMEM((2, 8, ROWS, width), NARROW), pltpu.VMEM(qkv_all.shape, NARROW),
             pltpu.VMEM(inverse.shape, WIDE), pltpu.VMEM(all_marks.shape, WIDE),
@@ -1528,9 +1583,10 @@
         middle_kernel,
         "middle",
         [
-            shape(own, width, dtype=WIDE), shape(8, own, width), *whole_shapes, whole_shapes[0], *level_shapes,
+            shape(own, width, dtype=WIDE), shape(8, own, width), *whole_shapes, *whole_shapes[:2],
+            *level_shapes,
         ],
-        (mixed, out_all, x_own, all_gains, *shards, *level[3:7]),
+        (mixed, out_all, x_own, all_gains, *shards, *level[3:8]),
         [
             pltpu.VMEM((8, own, 256), NARROW), pltpu.VMEM((256, width), NARROW),
             pltpu.VMEM((own, width), NARROW), pltpu.VMEM(gains_shape, WIDE),
@@ -1538,49 +1594,49 @@
         ],
         52, 32, 3,
     )
-    whole, level = whole + more[:4], level + more[4:]
-    hidden, grads_pre, parts, ends_a, ends_b, mates_a, *more = call(
+    whole, level = whole + more[:5], level + more[5:]
+    hidden, grads_pre, parts, ends_a, *more = call(
         ffn_kernel,
         "ffn",
         [
             shape(8, own, ff // 4), shape(8, own, ff // 2), shape(12, 4, 4, chunk, LANES),
-            shape(3, 4, 3, chunk, LANES), shape(3, 4, 3, chunk, LANES), shape(3, 4, 2, chunk, LANES),
-            *whole_shapes[1:], *whole_shapes,
+            shape(4, 4, 3, chunk, LANES),
+            whole_shapes[2], *whole_shapes,
         ],
-        (ffn_in, dy, *whole, *level[7:]),
+        (ffn_in, dy, *whole, *level[8:]),
         [
             pltpu.VMEM((8, own, width), NARROW), pltpu.VMEM((8, own, width), NARROW),
             pltpu.VMEM((2, 4, 4, LANES, chunk), NARROW), pltpu.VMEM((2, 4, 4, LANES, chunk), NARROW),
             pltpu.VMEM((2, chunk, width), NARROW), pltpu.VMEM((3, 8, own, chunk), NARROW),
             pltpu.VMEM((3, chunk, 8 * own), NARROW), pltpu.VMEM((3, 16, chunk, LANES), NARROW),
-            *middle_scratch(1, 3),
         ],
         48, 160, 4,
     )
     whole = whole + more
     fold_scratch = Fold.scratch(width)
-    grad_mid_own, grad_mid, gain_ffn_part, ends_c, mates_b, outer_a = call(
+    grad_mid_own, grad_mid, gain_ffn_part, ends_c, mates_b = call(
         back_kernel,
         "back",
         [
             shape(own, width, dtype=WIDE), shape(8, own, width), shape(8, width, dtype=WIDE),
-            shape(5, 4, 3, chunk, LANES), shape(3, 4, 2, chunk, LANES), shape(3, 4, chunk, LANES),
+            shape(5, 4, 3, chunk, LANES), shape(4, 4, 2, chunk, LANES),
         ],
-        (grads_pre, mid_own, cot_own, all_gains, parts, ends_b, mates_a, *whole[0::3], *whole[1::3]),
+        (grads_pre, mid_own, cot_own, all_gains, parts, ends_a, *whole[0::3], *whole[1::3]),
         [
             pltpu.VMEM((8, own, ff // 2), NARROW), pltpu.VMEM((4, 4, LANES, ff // 2), NARROW),
             pltpu.VMEM((own, width), WIDE), pltpu.VMEM((own, width), NARROW),
             pltpu.VMEM(gains_shape, WIDE), pltpu.VMEM((2, ROWS, width), NARROW),
-            pltpu.VMEM((8, width), WIDE), *middle_scratch(1, 3), *middle_scratch(2, 3), *fold_scratch,
+            pltpu.VMEM((8, width), WIDE), *middle_scratch(1, 4), *fold_scratch,
         ],
         48, 32, 5,
     )
-    grad_proj, parts_attn, hidden_out, ends_d, mates_c, outer_b = call(
+    grad_proj, parts_q, parts_o, got_o, out_home, ends_d, mates_c, outer_b = call(
         attend_back_kernel,
         "attend_back",
         [
-            shape(8, own, 512), shape(4, 4, 768, LANES), shape(own, width),
-            shape(1, 4, 3, chunk, LANES), shape(5, 4, 2, chunk, LANES), shape(3, 4, chunk, LANES),
+            shape(8, own, 512), shape(4, 4, 512, LANES), shape(4, 4, 256, LANES), shape(2, 4, 256, LANES),
+            shape(own, width),
+            shape(3, 4, 3, chunk, LANES), shape(5, 4, 2, chunk, LANES), shape(4, 4, chunk, LANES),
         ],
         (
             grad_mid, queries, keys, values, all_marks, inverse, out_all, mixed, attn_in, hidden, mid_own, parts,
@@ -1594,34 +1650,34 @@
             pltpu.VMEM((8, own, ff // 4), NARROW), pltpu.VMEM((ff // 4, width), NARROW),
             pltpu.VMEM((8, own, 512), NARROW), pltpu.VMEM((1024, 128), WIDE),
             pltpu.VMEM((1024, 128), WIDE),
-            pltpu.VMEM((4, 4, 768, LANES), NARROW), pltpu.VMEM((own, width), WIDE),
-            pltpu.VMEM((own, width), NARROW), *middle_scratch(1, 5), *middle_scratch(2, 3), *fold_scratch,
+            pltpu.VMEM((4, 4, 512, LANES), NARROW), pltpu.VMEM((4, 4, 256, LANES), NARROW),
+            pltpu.VMEM((own, width), WIDE), pltpu.VMEM((own, width), NARROW), *middle_scratch(1, 5), *middle_scratch(2, 4), *fold_scratch,
         ],
         32, 128, 6,
     )
-    out_home, grad_home, gain_sums, _, *sums = call(
+    grad_home, gain_sums, _, _, _, *sums = call(
         end_kernel,
         "end",
         [
-            shape(own, width), shape(own, width), shape(8, LANES, dtype=WIDE),
-            shape(1, 4, 2, chunk, LANES), *[shape(4, 4, chunk, LANES)] * 3, shape(4, 256, LANES), shape(4, 512, LANES),
+            shape(own, width), shape(8, LANES, dtype=WIDE), shape(3, 4, 2, chunk, LANES),
+            shape(5, 4, chunk, LANES), shape(3, 4, chunk, LANES),
+            *[shape(4, 4, chunk, LANES)] * 3, shape(4, 256, LANES), shape(4, 512, LANES),
         ],
         (
-            grad_proj, qkv_all, x_own, all_gains, grad_mid_own, hidden_out, gain_ffn_part, parts, parts_attn,
-            ends_a, ends_b, ends_c, ends_d, mates_a, mates_b, mates_c, outer_a, outer_b,
+            grad_proj, qkv_all, x_own, all_gains, grad_mid_own, gain_ffn_part, parts, parts_q, parts_o, got_o,
+            ends_a, ends_c, ends_d, mates_b, mates_c, outer_b,
         ),
         [
             pltpu.VMEM((8, own, 512), NARROW), pltpu.VMEM(qkv_all.shape, NARROW),
             pltpu.VMEM((own, width), NARROW), pltpu.VMEM(gains_shape, WIDE),
             pltpu.VMEM((own, width), WIDE), pltpu.VMEM((own, width), NARROW),
-            pltpu.VMEM((8, width), WIDE), pltpu.VMEM((5, 8, width), WIDE),
+            pltpu.VMEM((8, width), WIDE), pltpu.VMEM((10, 8, width), WIDE),
             *[pltpu.VMEM((12, 4, chunk, LANES), NARROW)] * 3,
-            pltpu.VMEM((5, 4, chunk, LANES), NARROW), pltpu.VMEM((1, 4, chunk, LANES), NARROW),
-            pltpu.VMEM((4, 768, LANES), NARROW), pltpu.VMEM((4, 768, LANES), NARROW),
-            pltpu.VMEM((2, 4, 768, LANES), NARROW), pltpu.VMEM((4, 768, LANES), NARROW),
-            *middle_scratch(1, 1), *middle_scratch(2, 5), *middle_scratch(2, 1), *fold_scratch,
+            *[pltpu.VMEM((4, 512, LANES), NARROW)] * 2, pltpu.VMEM((2, 4, 512, LANES), NARROW),
+            pltpu.VMEM((4, 512, LANES), NARROW), *[pltpu.VMEM((4, 256, LANES), NARROW)] * 5,
+            *middle_scratch(1, 3), *middle_scratch(2, 5), *middle_scratch(2, 3), *fold_scratch,
         ],
-        80, 64, 7,
+        88, 72, 7,
     )
     gate, up, down, out, qkv = (array.reshape(-1, LANES) for array in sums)
     grad_gate, grad_up, grad_down, grad_qkv, grad_out = pl.pallas_call(

time: 798 us -> 729 us (0.914)
  Pallas kernels: 775 us -> 705 us
    pallas_call x7, Pallas kernels: 771 us -> 702 us  [call(): pl.pallas_call(inner, out_shape=outs, in_specs=[ANYWHERE] * n_in, out_spe...]
where the time goes in v4:
time: 729 us; the launch traced here: 719 us
  Pallas kernels  705 us (97%)
  local copies, waits for them, and re-layouts  11.4 us (2%)
    pallas_call x7, Pallas kernels, call(): pl.pallas_call(inner, out_shape=outs, in_specs=[ANYWHERE] * n_in, out_spe...  702 us

profile of v4, /device:TPU:1, one launch (start us, length us, event | category | flops | bytes accessed | tf_op | source)
XLA Modules:
  0.0 719.0 jit_solution(8240281982343213083)
XLA Ops:
  0.6 0.0 copy-start
  0.7 0.1 pad_maximum_fusion
  0.8 0.6 copy-done
  1.3 0.7 copy_bitcast_fusion
  2.0 0.6 broadcast_in_dim.3.refs_2_.refs_5_
  2.6 0.6 pad.10.refs_1_
  3.2 1.3 fusion.3.refs_2_
  4.5 95.6 %start.1 = (bf16[256,2048]{1,0:T(8,128)(2,1)}, bf16[8,256,2048]{2,1,0:T(8,128)(2,1)}, f32[4,8,256]{2,1,0:T(8,128)}, f32[4,4,8,128]{3,2,1,0:T(8,128)}, bf16[4,4,1...) custom-call(bf16[256,2048]{1,0:T(8,128)(2,1)} %bitcast.31, ...), custom_call_target="tpu_custom_call" | custom-call | tf_op jit(solution)/shard_map/start/pallas_call | solution.py:667
  100.1 87.6 %attend.1 = (bf16[2,1024,256]{2,1,0:T(8,128)(2,1)}, bf16[2,1024,128]{2,1,0:T(8,128)(2,1)}, bf16[2,1024,128]{2,1,0:T(8,128)(2,1)}, bf16[8,256,256]{2,1,0:T(8,128)...) custom-call(bf16[8,256,2048]{2,1,0:T(8,128)(2,1)} %get-tuple-element, ...), custom_call_target="tpu_custom_call" | custom-call | tf_op jit(solution)/shard_map/attend/pallas_call | solution.py:667
  187.7 103.5 %middle.1 = (f32[256,2048]{1,0:T(8,128)}, bf16[8,256,2048]{2,1,0:T(8,128)(2,1)}, bf16[4,4,128,256]{3,2,1,0:T(8,128)(2,1)}, bf16[4,4,128,256]{3,2,1,0:T(8,128)(2,...) custom-call(bf16[8,256,256]{2,1,0:T(8,128)(2,1)} %get-tuple-element., ...), custom_call_target="tpu_custom_call" | custom-call | tf_op jit(solution)/shard_map/middle/pallas_call | solution.py:667
  291.2 96.4 %ffn.1 = (bf16[8,256,1024]{2,1,0:T(8,128)(2,1)}, bf16[8,256,2048]{2,1,0:T(8,128)(2,1)}, bf16[12,4,4,256,128]{4,3,2,1,0:T(8,128)(2,1)}, bf16[4,4,3,256,128]{4,3,2...) custom-call(bf16[8,256,2048]{2,1,0:T(8,128)(2,1)} %get-tuple-element, ...), custom_call_target="tpu_custom_call" | custom-call | tf_op jit(solution)/shard_map/ffn/pallas_call | solution.py:667
  387.6 95.9 %back.1 = (f32[256,2048]{1,0:T(8,128)}, bf16[8,256,2048]{2,1,0:T(8,128)(2,1)}, f32[8,2048]{1,0:T(8,128)}, bf16[5,4,3,256,128]{4,3,2,1,0:T(8,128)(2,1)}, bf16[4,4,2,256,128]{4,3,2,1,0:T(8,128)(2,1)}) custom-call(bf16[8,256,2048]{2,1,0:T(8,128)(2,1)} %get-tuple-element.105.refs_0_, f32[256,2048]{1,0:T(8,128)} %get-tuple-element.106.refs_1_.refs_10_, ...), custom_call_target="tpu_custom_call" | custom-call | tf_op jit(solution)/shard_map/back/pallas_call | solution.py:667
  483.5 93.4 %attend_back.1 = (bf16[8,256,512]{2,1,0:T(8,128)(2,1)}, bf16[4,4,512,128]{3,2,1,0:T(8,128)(2,1)}, bf16[4,4,256,128]{3,2,1,0:T(8,128)(2,1)}, bf16[2,4,256,128]{3,...) custom-call(bf16[8,256,2048]{2,1,0:T(8,128)(2,1)} %get-tuple-element, ...), custom_call_target="tpu_custom_call" | custom-call | tf_op jit(solution)/shard_map/attend_back/pallas_call | solution.py:667
  577.0 0.0 copy-start.7
  577.0 129.2 %end.1 = (bf16[256,2048]{1,0:T(8,128)(2,1)}, f32[8,128]{1,0:T(8,128)}, bf16[3,4,2,256,128]{4,3,2,1,0:T(8,128)(2,1)}, bf16[5,4,256,128]{3,2,1,0:T(8,128)(2,1)}, b...) custom-call(bf16[8,256,512]{2,1,0:T(8,128)(2,1)} %get-tuple-element., ...), custom_call_target="tpu_custom_call" | custom-call | tf_op jit(solution)/shard_map/end/pallas_call | solution.py:667
  706.2 1.3 slice_bitcast_fusion
  707.5 0.0 copy-start.2
  707.5 1.2 copy-done.2
  708.7 0.0 copy-start.3
  708.7 1.2 copy-done.3
  709.9 0.0 copy-start.4
  709.9 1.2 copy-done.4
  711.1 0.0 copy-start.5
  711.1 1.0 copy-done.5
  712.2 0.0 copy-start.6
  712.2 0.9 copy-done.6
  713.1 0.0 copy-start.8
  713.1 0.0 copy-start.1
  713.1 3.5 home.1
  716.6 0.0 copy-done.7
  716.6 1.0 copy.28
  717.6 0.0 copy-done.8
  717.6 1.0 copy.29
  718.5 0.0 copy-done.1
  (3 shorter events, 0.0 us)
Async XLA Ops:
  0.6 0.7 copy-start
  577.0 139.6 %copy-start.7 = (bf16[256,2048]{1,0:T(8,128)(2,1)S(1)}, bf16[256,2048]{1,0:T(8,128)(2,1)}, u32[]{:S(2)}) copy-start(bf16[256,2048]{1,0:T(8,128)(2,1)} %get-tuple-element.121) | copy-start | bytes 3145732
  707.5 1.2 copy-start.2
  708.7 1.2 copy-start.3
  709.9 1.2 copy-start.4
  711.1 1.0 copy-start.5
  712.2 0.9 copy-start.6
  713.1 4.4 copy-start.8
  713.1 5.4 copy-start.1

commit v5 on v4

--- a/solution.py
+++ b/solution.py
@@ -279,10 +279,14 @@
             self.side, self.core, self.row, self.cross, self.core_side, self.row_side, self.cross_side
         )
         y, k, high, low = f // 2, f % 2, c // 2, c % 2
-        self.to_f, to_c = (low + y) % 2 * 2 + high, k * 2 + y
-        self.to = (self.to_f, to_c, t)
-        self.whence = (low * 2 + high, k * 2 + (y + low) % 2, t)
-        self.away = (self.to_f - f) * (self.to_f - f) + (to_c - c) * (to_c - c)
+        self.to_f, self.to, self.whence, self.away = [], [], [], []
+        for m in range(2):
+            even = (y + m) % 2
+            to_f, to_c = (low + even) % 2 * 2 + high, k * 2 + even
+            self.to_f.append(to_f)
+            self.to.append((to_f, to_c, t))
+            self.whence.append(((low + m) % 2 * 2 + high, k * 2 + (y + low) % 2, t))
+            self.away.append((to_f - f) * (to_f - f) + (to_c - c) * (to_c - c))
         self.b, self.b_side = f * 2 + t, f * 2 + 1 - t
         self.b_row, self.b_far = fy * 2 + t, fy * 2 + 1 - t
         self.b_core, self.b_core_side = fs * 2 + t, fs * 2 + 1 - t
@@ -591,9 +595,11 @@
             for q in range(start, start + count)
         ]
 
-    def finish(self):
-        for gate in self.gates:
+    def finish(self, count=None):
+        count = len(self.gates) if count is None else count
+        for gate in self.gates[:count]:
             gate.arrive()
+        self.gates = self.gates[count:]
 
 
 class Middle:
@@ -693,39 +699,39 @@
 class Swap:
     def __init__(self, post, at, home=False):
         self.post, self.at, self.moves = post, at, []
-        self.device = at.whence if home else at.to
-
-    def __call__(self, source, target, lands):
-        post, at = self.post, self.at
-        sent = post.make(source, target, self.device, lands)
+        self.devices = at.whence if home else at.to
+
+    def __call__(self, m, source, target, lands):
+        post, away = self.post, self.at.away[m]
+        sent = post.make(source, target, self.devices[m], lands)
         local = pltpu.make_async_copy(source, target, post.local_sems.at[post.n_local])
         post.n_local += 1
 
-        @pl.when(at.away != 0)
+        @pl.when(away != 0)
         def _():
             sent.copy.start()
 
-        @pl.when(at.away == 0)
+        @pl.when(away == 0)
         def _():
             local.start()
 
-        self.moves.append(sent)
+        self.moves.append((away, sent))
 
         def arrive():
-            @pl.when(at.away != 0)
+            @pl.when(away != 0)
             def _():
                 sent.landing.wait_recv()
 
-            @pl.when(at.away == 0)
+            @pl.when(away == 0)
             def _():
                 local.wait()
 
         return arrive
 
     def finish(self):
-        @pl.when(self.at.away != 0)
-        def _():
-            for sent in self.moves:
+        for away, sent in self.moves:
+            @pl.when(away != 0)
+            def _(sent=sent):
                 sent.copy.wait_send()
 
 
@@ -734,16 +740,13 @@
     partners = (*at.level, at.z1, at.z2, at.z3)
     for device in partners:
         pl.semaphore_signal(bar, inc=1, device_id=device, device_id_type=MESH)
-
-    @pl.when(at.away != 0)
-    def _():
-        for device in (at.to, at.whence):
-            pl.semaphore_signal(bar, inc=1, device_id=device, device_id_type=MESH)
-        pl.semaphore_wait(bar, len(partners) + 2)
-
-    @pl.when(at.away == 0)
-    def _():
-        pl.semaphore_wait(bar, len(partners))
+    for m in range(2):
+        @pl.when(at.away[m] != 0)
+        def _(m=m):
+            for device in (at.to[m], at.whence[m]):
+                pl.semaphore_signal(bar, inc=1, device_id=device, device_id_type=MESH)
+
+    pl.semaphore_wait(bar, len(partners) + sum(2 * ((away + 18) // 19) for away in at.away))
 
 
 class Deal:
@@ -775,7 +778,9 @@
     f, c = at.f, at.c
     meet_swap(at)
     swap = Swap(post, at)
-    x_moved = [swap(hidden.at[half], rows_in.at[half], rows_in.at[half]) for half in HALVES]
+    x_moved = [
+        swap(m, hidden.at[half], rows_in.at[half], rows_in.at[half]) for m, half in enumerate(HALVES)
+    ]
     heads = wqkv.shape[1] // 4
     span = wo.shape[0] // 4
     first = []
@@ -788,7 +793,9 @@
     own = [post.keep(wqkv.at[:, lane], qkv_all.at[f, c])]
     row = pl.ds(pl.multiple_of(f * span, LANES), span)
     own.append(post.keep(wo.at[row], out_all.at[f, c]))
-    marks_moved = swap(marks, all_marks.at[at.to_f], all_marks.at[f])
+    marks_moved = [
+        swap(m, marks, all_marks.at[m, at.to_f[m]], all_marks.at[m, f]) for m in range(2)
+    ]
 
     mine = gain_buf.at[f, c]
     post.settle([post.keep(gains, mine)])
@@ -828,13 +835,14 @@
         spread.own(half, rows_out.at[HALVES[half]])
         post.keep(rows_in.at[HALVES[half]], x_own.at[HALVES[half]])
 
-    marks_moved()
-    here = all_marks.at[f]
-    small = post.send(here, here, at.core, all_marks.at[at.fs])
+    for arrive in marks_moved:
+        arrive()
+    here = all_marks.at[:, f]
+    small = post.send(here, here, at.core, all_marks.at[:, at.fs])
     spread.relay(0)
     small.arrive()
-    pair = all_marks.at[pl.ds(f // 2 * 2, 2)]
-    smaller = post.send(pair, pair, at.row, all_marks.at[pl.ds(at.fy // 2 * 2, 2)])
+    pair = all_marks.at[:, pl.ds(f // 2 * 2, 2)]
+    smaller = post.send(pair, pair, at.row, all_marks.at[:, pl.ds(at.fy // 2 * 2, 2)])
     spread.relay(1)
     forwards = []
     for far, close, there, out in levels:
@@ -901,7 +909,7 @@
 
 
 def id_rows(at, marks, m, tiles):
-    return jnp.concatenate([marks[quarter(at, i), m : m + 1, :] for i in range(tiles)], axis=1)
+    return jnp.concatenate([marks[m, quarter(at, i), m : m + 1, :] for i in range(tiles)], axis=1)
 
 
 def attend_kernel(post, at, ins, outs, scratch):
@@ -912,7 +920,9 @@
     rows, weight, inverse, marks, q_buf, k_buf, v_buf, mix_buf = scratch
     meet_swap(at)
     swap = Swap(post, at)
-    cot_moved = [swap(cot.at[half], cot_own.at[half], cot_own.at[half]) for half in HALVES]
+    cot_moved = [
+        swap(m, cot.at[half], cot_own.at[half], cot_own.at[half]) for m, half in enumerate(HALVES)
+    ]
     local = [
         post.keep(inverse_in, inverse),
         post.keep(marks_in, marks),
@@ -930,7 +940,7 @@
             q = quarter(at, i)
             here = rows[m, pl.ds(2 * q, 2)].reshape(TILE, width)
             projected = mm(here, weight[...].reshape(width, columns))
-            cos_full, sin_full = rope_full(marks[q], m, inverse[0:1])
+            cos_full, sin_full = rope_full(marks[m, q], m, inverse[0:1])
             place = pl.ds(i * TILE, TILE)
             for g in range(2):
                 lane = slice(g * HEAD_DIM, (g + 1) * HEAD_DIM)
@@ -941,7 +951,7 @@
         for i in range(4):
             n = min(i + 2, 4) * TILE
             q = quarter(at, i)
-            id_col = marks[q].T[:, m : m + 1]
+            id_col = marks[m, q].T[:, m : m + 1]
             id_row = id_rows(at, marks, m, n // TILE)
             for g in range(2):
                 lane = slice(g * HEAD_DIM, (g + 1) * HEAD_DIM)
@@ -1136,9 +1146,9 @@
 
 def back_kernel(post, at, ins, outs, scratch):
     grads_pre, mid_own, cot_own, gains_in, parts, ends_a, *weights = ins
-    grad_mid_own, grad_mid, gain_part, ends_c, mates_b = outs
+    grad_mid_own, grad_mid, gain_part, ends_c, mates_b, mates_e = outs
     pre_buf, weight, mid_buf, cot_buf, gains, rows_out, gain_out = scratch[:7]
-    bufs_1, fold_scratch = scratch[7:9], scratch[9:]
+    bufs_1, bufs_e, fold_scratch = scratch[7:9], scratch[9:11], scratch[11:]
     meet((at.side, at.core, at.row, at.z1, at.z3))
     downs = [
         Middle(post, at, 1, parts, 0, ends_a, mates_b, *bufs_1),
@@ -1177,7 +1187,10 @@
         post.keep(fold.held.at[half], grad_mid_own.at[rows])
     gain_out[...] = jnp.broadcast_to(total, gain_out.shape)
     post.keep(gain_out, gain_part)
+    downs[1].finish(2)
+    downs.append(Middle(post, at, 1, parts, 4, ends_c.at[pl.ds(0, 2)], mates_e, *bufs_e))
     spread.relay(0)
+    downs[2].send()
     spread.relay(1)
     spread.corner()
     spread.finish()
@@ -1188,19 +1201,20 @@
 def attend_back_kernel(post, at, ins, outs, scratch):
     (
         grad_mid, queries, keys, values, marks_in, inverse_in, out_all, mixed, attn_in, hidden, mid_own, parts,
-        ends_c, mates_b, *downs_in
+        ends_c, mates_b, mates_e, *downs_in
     ) = ins
-    grad_proj, parts_q, parts_o, got_o, out_home, ends_d, mates_c, outer_b = outs
+    grad_proj, parts_q, sums_o, out_home, ends_d, mates_c, outer_b, outer_e = outs
     (
         gm_buf, q_buf, k_buf, v_buf, marks, inverse, weight, mix_buf, hid_buf, down_buf, gp_buf, gk_buf, gv_buf,
-        staged, staged_o, mid_buf, out_buf
-    ) = scratch[:17]
-    bufs_1, bufs_2, fold_scratch = scratch[17:19], scratch[19:21], scratch[21:]
+        staged, staged_o, got_o, far_o, end_o, mid_buf, out_buf
+    ) = scratch[:20]
+    bufs_1, bufs_2, bufs_e, fold_scratch = scratch[20:22], scratch[22:24], scratch[24:26], scratch[26:]
     meet_swap(at)
     swap = Swap(post, at, home=True)
     steps = [
-        Middle(post, at, 1, parts, 4, ends_c, mates_c, *bufs_1),
+        Middle(post, at, 1, parts, 6, ends_c.at[pl.ds(2, 3)], mates_c, *bufs_1),
         Middle(post, at, 2, parts, 0, mates_b, outer_b, *bufs_2),
+        Middle(post, at, 2, parts, 4, mates_e, outer_e, *bufs_e),
         Ends(post, at, parts, 9, ends_d),
     ]
 
@@ -1222,7 +1236,7 @@
         for i in range(16)
     ]
     post.settle(early)
-    for step in steps[:2]:
+    for step in steps[:3]:
         step.send()
 
     def part(*blocks):
@@ -1250,16 +1264,15 @@
         for h in range(2):
             block = 2 * n + h
             staged_o[block // 4, block % 4] = value[:, h * LANES : (h + 1) * LANES]
-    post.settle([post.keep(staged_o, parts_o)])
-    step_o = Descend(post, at, parts_o, got_o)
+    step_o = Descend(post, at, staged_o, got_o)
     for m in range(2):
         for i in range(4):
             q = quarter(at, i)
             n = min(i + 2, 4) * TILE
             place = slice(i * TILE, (i + 1) * TILE)
-            id_col = marks[q].T[:, m : m + 1]
+            id_col = marks[m, q].T[:, m : m + 1]
             id_row = id_rows(at, marks, m, n // TILE)
-            cos_full, sin_full = rope_full(marks[q], m, inverse[0:1])
+            cos_full, sin_full = rope_full(marks[m, q], m, inverse[0:1])
             rows = gm_buf[pl.ds(2 * q, 2), m * ROWS : (m + 1) * ROWS].reshape(TILE, width)
             grad_mixed = mm(rows, weight[...], ((1,), (1,))).astype(NARROW)
             for g in range(2):
@@ -1287,11 +1300,14 @@
                 for half in HALVES:
                     k = half.start // ROWS
                     out_buf[half] = (fold.held[k] + mid_buf[half]).astype(NARROW)
-                moved = [swap(out_buf.at[half], out_home.at[half], out_home.at[half]) for half in HALVES]
+                moved = [
+                    swap(k, out_buf.at[half], out_home.at[half], out_home.at[half])
+                    for k, half in enumerate(HALVES)
+                ]
         for i in range(4):
             q = quarter(at, i)
             place = slice(i * TILE, (i + 1) * TILE)
-            cos_full, sin_full = rope_full(marks[q], m, inverse[0:1])
+            cos_full, sin_full = rope_full(marks[m, q], m, inverse[0:1])
             done = (
                 rope_back(gk_buf[place], cos_full, sin_full).astype(NARROW),
                 gv_buf[place].astype(NARROW),
@@ -1316,6 +1332,15 @@
             staged[block // 4, block % 4] = other[:, h * LANES : (h + 1) * LANES]
     post.keep(staged, parts_q)
     step_o.finish()
+    for k in range(4):
+        value = staged_o[k, at.c2].astype(WIDE) + got_o[1, k].astype(WIDE)
+        far_o[k] = value.astype(NARROW)
+    sent_o = post.send(far_o, end_o, at.z2, end_o)
+    sent_o.arrive()
+    for k in range(4):
+        value = staged_o[k, at.c].astype(WIDE) + got_o[0, k].astype(WIDE) + end_o[k].astype(WIDE)
+        got_o[1, k] = value.astype(NARROW)
+    post.keep(got_o.at[1], sums_o)
     for arrive in moved:
         arrive()
     swap.finish()
@@ -1390,26 +1415,26 @@
 
 def end_kernel(post, at, ins, outs, scratch):
     (
-        grad_proj, qkv_all, x_own, gains_in, grad_mid_own, gain_ffn_part, parts, parts_q, parts_o, got_o,
-        ends_a, ends_c, ends_d, mates_b, mates_c, outer_b
+        grad_proj, qkv_all, x_own, gains_in, grad_mid_own, gain_ffn_part, parts, parts_q, sums_o,
+        ends_a, ends_c, ends_d, mates_b, mates_c, mates_e, outer_b, outer_e
     ) = ins
     grad_home, gain_sums, mates_d, outer_c, outer_d, *home_sums = outs
     (
         gp_buf, weight, x_buf, gains, mid_buf, rows_out, gain_buf, gain_got, own_ffn, one_ffn, two_ffn,
-        own_q, far_q, got_q, end_q, own_o, far_o, one_o, two_o, end_o
-    ) = scratch[:20]
-    bufs_1, bufs_2, bufs_3, fold_scratch = scratch[20:22], scratch[22:24], scratch[24:26], scratch[26:]
+        own_q, far_q, got_q, end_q
+    ) = scratch[:15]
+    bufs_1, bufs_2, bufs_3, fold_scratch = scratch[15:17], scratch[17:19], scratch[19:21], scratch[21:]
     f, c = at.f, at.c
     meet_swap(at)
     step_q = Descend(post, at, parts_q, got_q)
     steps = [
         Middle(post, at, 1, parts, 9, ends_d, mates_d, *bufs_1),
-        Middle(post, at, 2, parts, 4, mates_c, outer_c, *bufs_2),
+        Middle(post, at, 2, parts, 6, mates_c, outer_c, *bufs_2),
     ]
     swap = Swap(post, at, home=True)
-    for_o = [post.keep(parts_o.at[:, at.c2], far_o), post.keep(got_o.at[1], two_o)]
     early = Own(
-        post, at, parts, 0, 4, ((ends_a,), (mates_b,), (outer_b,)),
+        post, at, parts, 0, 6,
+        ((ends_a, ends_c.at[pl.ds(0, 2)]), (mates_b, mates_e), (outer_b, outer_e)),
         own_ffn, one_ffn, two_ffn,
     )
     fold_in = [
@@ -1419,11 +1444,9 @@
     ]
     later = [
         post.keep(parts_q.at[:, c], own_q), post.keep(parts_q.at[:, at.c2], far_q),
-        post.keep(parts_o.at[:, c], own_o), post.keep(got_o.at[0], one_o),
     ]
     for step in steps:
         step.send()
-    post.settle(for_o)
 
     def add_far(far, came):
         for k in range(4):
@@ -1433,8 +1456,6 @@
         for k in range(4):
             own[k] = (own[k].astype(WIDE) + one[k].astype(WIDE) + end[k].astype(WIDE)).astype(NARROW)
 
-    add_far(far_o, two_o)
-    sent_o = post.send(far_o, end_o, at.z2, end_o)
     trades = []
     places = ((at.row, at.fy), (at.cross, at.fd), (at.core, at.fs))
 
@@ -1459,6 +1480,10 @@
     fold.first()
     early.add()
     fold.second()
+    post.settle(later)
+    step_q.finish()
+    add_far(far_q, got_q.at[1])
+    sent_q = post.send(far_q, end_q, at.z2, end_q)
     fold.third()
     gain = jnp.concatenate([gains[i // 4, i % 4, 0:1, :] for i in range(16)], axis=1)
     total = jnp.zeros((1, width), WIDE)
@@ -1468,30 +1493,27 @@
         back, piece = norm_back_rows(fold.held[half], x_buf[rows].astype(WIDE), gain)
         total = total + piece
         rows_out[rows] = (mid_buf[rows] + back).astype(NARROW)
-        moved.append(swap(rows_out.at[rows], grad_home.at[rows], grad_home.at[rows]))
+        moved.append(swap(half, rows_out.at[rows], grad_home.at[rows], grad_home.at[rows]))
     gain_buf[0:1] = total
     gain_sent = [
         post.send(gain_buf, gain_got.at[k], device, gain_got.at[k])
         for k, device in enumerate(at.level)
     ]
-    for p in range(4):
-        trade_ffn(p)
-    post.settle(later)
-    step_q.finish()
-    add_far(far_q, got_q.at[1])
-    sent_q = post.send(far_q, end_q, at.z2, end_q)
     steps[0].finish()
     steps.append(Middle(post, at, 2, parts, 9, mates_d, outer_d, *bufs_3))
     steps[2].send()
+    for p in range(6):
+        trade_ffn(p)
+    trade(lambda k: sums_o.at[k], home_sums[3])
+    sent_q.arrive()
+    add_own(own_q, got_q.at[0], end_q)
+    trade(lambda k: own_q.at[k], home_sums[4])
     steps[1].finish()
     late = Own(
-        post, at, parts, 4, 5, ((ends_c,), (mates_c,), (outer_c,)), own_ffn, one_ffn, two_ffn
-    )
-    sent_o.arrive()
-    add_own(own_o, one_o, end_o)
-    trade(lambda k: own_o.at[k], home_sums[3])
+        post, at, parts, 6, 3, ((ends_c.at[pl.ds(2, 3)],), (mates_c,), (outer_c,)), own_ffn, one_ffn, two_ffn
+    )
     late.add()
-    for p in range(4, 9):
+    for p in range(6, 9):
         trade_ffn(p)
     for sent in gain_sent:
         sent.arrive()
@@ -1509,9 +1531,6 @@
     last.add()
     for p in range(9, 12):
         trade_ffn(p)
-    sent_q.arrive()
-    add_own(own_q, got_q.at[0], end_q)
-    trade(lambda k: own_q.at[k], home_sums[4])
     for sent in gain_sent:
         sent.arrive()
         sent.leave()
@@ -1554,7 +1573,7 @@
         "start",
         [
             shape(own, width), shape(8, own, width),
-            shape(4, *marks.shape, dtype=WIDE), shape(*gains_shape, dtype=WIDE),
+            shape(2, 4, *marks.shape, dtype=WIDE), shape(*gains_shape, dtype=WIDE),
             shape(4, 4, LANES, wqkv.shape[1] // 4), shape(4, 4, wo.shape[0] // 4, LANES),
             *level_shapes, *level_shapes,
         ],
@@ -1614,33 +1633,34 @@
     )
     whole = whole + more
     fold_scratch = Fold.scratch(width)
-    grad_mid_own, grad_mid, gain_ffn_part, ends_c, mates_b = call(
+    grad_mid_own, grad_mid, gain_ffn_part, ends_c, mates_b, mates_e = call(
         back_kernel,
         "back",
         [
             shape(own, width, dtype=WIDE), shape(8, own, width), shape(8, width, dtype=WIDE),
-            shape(5, 4, 3, chunk, LANES), shape(4, 4, 2, chunk, LANES),
+            shape(5, 4, 3, chunk, LANES), shape(4, 4, 2, chunk, LANES), shape(2, 4, 2, chunk, LANES),
         ],
         (grads_pre, mid_own, cot_own, all_gains, parts, ends_a, *whole[0::3], *whole[1::3]),
         [
             pltpu.VMEM((8, own, ff // 2), NARROW), pltpu.VMEM((4, 4, LANES, ff // 2), NARROW),
             pltpu.VMEM((own, width), WIDE), pltpu.VMEM((own, width), NARROW),
             pltpu.VMEM(gains_shape, WIDE), pltpu.VMEM((2, ROWS, width), NARROW),
-            pltpu.VMEM((8, width), WIDE), *middle_scratch(1, 4), *fold_scratch,
+            pltpu.VMEM((8, width), WIDE), *middle_scratch(1, 4), *middle_scratch(1, 2), *fold_scratch,
         ],
         48, 32, 5,
     )
-    grad_proj, parts_q, parts_o, got_o, out_home, ends_d, mates_c, outer_b = call(
+    grad_proj, parts_q, sums_o, out_home, ends_d, mates_c, outer_b, outer_e = call(
         attend_back_kernel,
         "attend_back",
         [
-            shape(8, own, 512), shape(4, 4, 512, LANES), shape(4, 4, 256, LANES), shape(2, 4, 256, LANES),
+            shape(8, own, 512), shape(4, 4, 512, LANES), shape(4, 256, LANES),
             shape(own, width),
-            shape(3, 4, 3, chunk, LANES), shape(5, 4, 2, chunk, LANES), shape(4, 4, chunk, LANES),
+            shape(3, 4, 3, chunk, LANES), shape(3, 4, 2, chunk, LANES), shape(4, 4, chunk, LANES),
+            shape(2, 4, chunk, LANES),
         ],
         (
             grad_mid, queries, keys, values, all_marks, inverse, out_all, mixed, attn_in, hidden, mid_own, parts,
-            ends_c, mates_b, *whole[2::3],
+            ends_c, mates_b, mates_e, *whole[2::3],
         ),
         [
             pltpu.VMEM((8, own, width), NARROW), pltpu.VMEM((2, 1024, 256), NARROW),
@@ -1651,7 +1671,9 @@
             pltpu.VMEM((8, own, 512), NARROW), pltpu.VMEM((1024, 128), WIDE),
             pltpu.VMEM((1024, 128), WIDE),
             pltpu.VMEM((4, 4, 512, LANES), NARROW), pltpu.VMEM((4, 4, 256, LANES), NARROW),
-            pltpu.VMEM((own, width), WIDE), pltpu.VMEM((own, width), NARROW), *middle_scratch(1, 5), *middle_scratch(2, 4), *fold_scratch,
+            pltpu.VMEM((2, 4, 256, LANES), NARROW), *[pltpu.VMEM((4, 256, LANES), NARROW)] * 2,
+            pltpu.VMEM((own, width), WIDE), pltpu.VMEM((own, width), NARROW), *middle_scratch(1, 3), *middle_scratch(2, 4),
+            *middle_scratch(2, 2), *fold_scratch,
         ],
         32, 128, 6,
     )
@@ -1660,12 +1682,12 @@
         "end",
         [
             shape(own, width), shape(8, LANES, dtype=WIDE), shape(3, 4, 2, chunk, LANES),
-            shape(5, 4, chunk, LANES), shape(3, 4, chunk, LANES),
+            shape(3, 4, chunk, LANES), shape(3, 4, chunk, LANES),
             *[shape(4, 4, chunk, LANES)] * 3, shape(4, 256, LANES), shape(4, 512, LANES),
         ],
         (
-            grad_proj, qkv_all, x_own, all_gains, grad_mid_own, gain_ffn_part, parts, parts_q, parts_o, got_o,
-            ends_a, ends_c, ends_d, mates_b, mates_c, outer_b,
+            grad_proj, qkv_all, x_own, all_gains, grad_mid_own, gain_ffn_part, parts, parts_q, sums_o,
+            ends_a, ends_c, ends_d, mates_b, mates_c, mates_e, outer_b, outer_e,
         ),
         [
             pltpu.VMEM((8, own, 512), NARROW), pltpu.VMEM(qkv_all.shape, NARROW),
@@ -1674,8 +1696,8 @@
             pltpu.VMEM((8, width), WIDE), pltpu.VMEM((10, 8, width), WIDE),
             *[pltpu.VMEM((12, 4, chunk, LANES), NARROW)] * 3,
             *[pltpu.VMEM((4, 512, LANES), NARROW)] * 2, pltpu.VMEM((2, 4, 512, LANES), NARROW),
-            pltpu.VMEM((4, 512, LANES), NARROW), *[pltpu.VMEM((4, 256, LANES), NARROW)] * 5,
-            *middle_scratch(1, 3), *middle_scratch(2, 5), *middle_scratch(2, 3), *fold_scratch,
+            pltpu.VMEM((4, 512, LANES), NARROW),
+            *middle_scratch(1, 3), *middle_scratch(2, 3), *middle_scratch(2, 3), *fold_scratch,
         ],
         88, 72, 7,
     )

time: 729 us -> 698 us (0.957)
  Pallas kernels: 705 us -> 672 us
    pallas_call x7, Pallas kernels: 702 us -> 669 us  [call(): pl.pallas_call(inner, out_shape=outs, in_specs=[ANYWHERE] * n_in, out_spe...]
where the time goes in v5:
time: 698 us; the launch traced here: 686 us
  Pallas kernels  672 us (96%)
  local copies, waits for them, and re-layouts  11.4 us (2%)
    pallas_call x7, Pallas kernels, call(): pl.pallas_call(inner, out_shape=outs, in_specs=[ANYWHERE] * n_in, out_spe...  669 us

profile of v5, /device:TPU:1, one launch (start us, length us, event | category | flops | bytes accessed | tf_op | source)
XLA Modules:
  0.0 686.2 jit_solution(5845691985176533149)
XLA Ops:
  0.6 0.0 copy-start
  0.7 0.1 pad_maximum_fusion
  0.8 0.6 copy-done
  1.3 0.7 copy_bitcast_fusion
  2.0 0.6 broadcast_in_dim.3.refs_2_.refs_5_
  2.6 0.6 pad.10.refs_1_
  3.2 1.3 fusion.3.refs_2_
  4.5 89.4 %start.1 = (bf16[256,2048]{1,0:T(8,128)(2,1)}, bf16[8,256,2048]{2,1,0:T(8,128)(2,1)}, f32[2,4,8,256]{3,2,1,0:T(8,128)}, f32[4,4,8,128]{3,2,1,0:T(8,128)}, bf16[4...) custom-call(bf16[256,2048]{1,0:T(8,128)(2,1)} %bitcast.31, ...), custom_call_target="tpu_custom_call" | custom-call | tf_op jit(solution)/shard_map/start/pallas_call | solution.py:673
  93.9 75.3 %attend.1 = (bf16[2,1024,256]{2,1,0:T(8,128)(2,1)}, bf16[2,1024,128]{2,1,0:T(8,128)(2,1)}, bf16[2,1024,128]{2,1,0:T(8,128)(2,1)}, bf16[8,256,256]{2,1,0:T(8,128)...) custom-call(bf16[8,256,2048]{2,1,0:T(8,128)(2,1)} %get-tuple-element, ...), custom_call_target="tpu_custom_call" | custom-call | tf_op jit(solution)/shard_map/attend/pallas_call | solution.py:673
  169.2 97.2 %middle.1 = (f32[256,2048]{1,0:T(8,128)}, bf16[8,256,2048]{2,1,0:T(8,128)(2,1)}, bf16[4,4,128,256]{3,2,1,0:T(8,128)(2,1)}, bf16[4,4,128,256]{3,2,1,0:T(8,128)(2,...) custom-call(bf16[8,256,256]{2,1,0:T(8,128)(2,1)} %get-tuple-element., ...), custom_call_target="tpu_custom_call" | custom-call | tf_op jit(solution)/shard_map/middle/pallas_call | solution.py:673
  266.4 96.1 %ffn.1 = (bf16[8,256,1024]{2,1,0:T(8,128)(2,1)}, bf16[8,256,2048]{2,1,0:T(8,128)(2,1)}, bf16[12,4,4,256,128]{4,3,2,1,0:T(8,128)(2,1)}, bf16[4,4,3,256,128]{4,3,2...) custom-call(bf16[8,256,2048]{2,1,0:T(8,128)(2,1)} %get-tuple-element, ...), custom_call_target="tpu_custom_call" | custom-call | tf_op jit(solution)/shard_map/ffn/pallas_call | solution.py:673
  362.5 94.2 %back.1 = (f32[256,2048]{1,0:T(8,128)}, bf16[8,256,2048]{2,1,0:T(8,128)(2,1)}, f32[8,2048]{1,0:T(8,128)}, bf16[5,4,3,256,128]{4,3,2,1,0:T(8,128)(2,1)}, bf16[4,4...) custom-call(bf16[8,256,2048]{2,1,0:T(8,128)(2,1)} %get-tuple-element.106.refs_0_, ...), custom_call_target="tpu_custom_call" | custom-call | tf_op jit(solution)/shard_map/back/pallas_call | solution.py:673
  456.8 95.5 %attend_back.1 = (bf16[8,256,512]{2,1,0:T(8,128)(2,1)}, bf16[4,4,512,128]{3,2,1,0:T(8,128)(2,1)}, bf16[4,256,128]{2,1,0:T(8,128)(2,1)}, bf16[256,2048]{1,0:T(8,1...) custom-call(bf16[8,256,2048]{2,1,0:T(8,128)(2,1)} %get-tuple-element, ...), custom_call_target="tpu_custom_call" | custom-call | tf_op jit(solution)/shard_map/attend_back/pallas_call | solution.py:673
  552.3 0.0 copy-start.7
  552.3 121.1 %end.1 = (bf16[256,2048]{1,0:T(8,128)(2,1)}, f32[8,128]{1,0:T(8,128)}, bf16[3,4,2,256,128]{4,3,2,1,0:T(8,128)(2,1)}, bf16[3,4,256,128]{3,2,1,0:T(8,128)(2,1)}, b...) custom-call(bf16[8,256,512]{2,1,0:T(8,128)(2,1)} %get-tuple-element., ...), custom_call_target="tpu_custom_call" | custom-call | tf_op jit(solution)/shard_map/end/pallas_call | solution.py:673
  673.4 1.3 slice_bitcast_fusion
  674.6 0.0 copy-start.2
  674.6 1.2 copy-done.2
  675.9 0.0 copy-start.3
  675.9 1.2 copy-done.3
  677.1 0.0 copy-start.4
  677.1 1.2 copy-done.4
  678.3 0.0 copy-start.5
  678.3 1.0 copy-done.5
  679.4 0.0 copy-start.6
  679.4 0.9 copy-done.6
  680.3 0.0 copy-start.8
  680.3 3.5 home.1
  683.8 0.0 copy-start.1
  683.8 0.0 copy-done.7
  683.8 1.0 copy.28
  684.7 0.0 copy-done.8
  684.7 1.0 copy.29
  685.7 0.0 copy-done.1
  (3 shorter events, 0.0 us)
Async XLA Ops:
  0.6 0.7 copy-start
  552.3 131.5 %copy-start.7 = (bf16[256,2048]{1,0:T(8,128)(2,1)S(1)}, bf16[256,2048]{1,0:T(8,128)(2,1)}, u32[]{:S(2)}) copy-start(bf16[256,2048]{1,0:T(8,128)(2,1)} %get-tuple-element.123) | copy-start | bytes 3145732
  674.6 1.2 copy-start.2
  675.9 1.2 copy-start.3
  677.1 1.2 copy-start.4
  678.3 1.0 copy-start.5
  679.4 0.9 copy-start.6
  680.3 4.4 copy-start.8
  683.8 2.0 copy-start.1

commit v6 on v5

--- a/solution.py
+++ b/solution.py
@@ -1201,14 +1201,15 @@
 def attend_back_kernel(post, at, ins, outs, scratch):
     (
         grad_mid, queries, keys, values, marks_in, inverse_in, out_all, mixed, attn_in, hidden, mid_own, parts,
-        ends_c, mates_b, mates_e, *downs_in
+        ends_a, ends_c, mates_b, mates_e, *downs_in
     ) = ins
-    grad_proj, parts_q, sums_o, out_home, ends_d, mates_c, outer_b, outer_e = outs
+    grad_proj, parts_q, sums_o, out_home, ends_d, mates_c, outer_b, outer_e, first_sums = outs
     (
         gm_buf, q_buf, k_buf, v_buf, marks, inverse, weight, mix_buf, hid_buf, down_buf, gp_buf, gk_buf, gv_buf,
         staged, staged_o, got_o, far_o, end_o, mid_buf, out_buf
     ) = scratch[:20]
-    bufs_1, bufs_2, bufs_e, fold_scratch = scratch[20:22], scratch[22:24], scratch[24:26], scratch[26:]
+    bufs_1, bufs_2, bufs_e, bufs_own = scratch[20:22], scratch[22:24], scratch[24:26], scratch[26:29]
+    fold_scratch = scratch[29:]
     meet_swap(at)
     swap = Swap(post, at, home=True)
     steps = [
@@ -1322,6 +1323,11 @@
     for i in range(8):
         place = slice(i * TILE, (i + 1) * TILE)
         gp_t[:, place] = gp_buf[i].astype(WIDE).T.astype(NARROW)
+    steps[1].finish()
+    early = Own(
+        post, at, parts, 0, 3,
+        ((ends_a.at[pl.ds(0, 3)],), (mates_b.at[pl.ds(0, 3)],), (outer_b.at[pl.ds(0, 3)],)), *bufs_own,
+    )
     for n in range(8):
         post.settle([fetched])
         if n < 7:
@@ -1331,6 +1337,14 @@
             block = 2 * n + h
             staged[block // 4, block % 4] = other[:, h * LANES : (h + 1) * LANES]
     post.keep(staged, parts_q)
+    early.add()
+    trades = []
+    for p in range(3):
+        post.keep(bufs_own[0].at[p, at.f], first_sums.at[at.f, p])
+        for device, k in ((at.row, at.fy), (at.cross, at.fd), (at.core, at.fs)):
+            trades.append(
+                post.send(bufs_own[0].at[p, k], first_sums.at[at.f, p], device, first_sums.at[k, p])
+            )
     step_o.finish()
     for k in range(4):
         value = staged_o[k, at.c2].astype(WIDE) + got_o[1, k].astype(WIDE)
@@ -1344,6 +1358,9 @@
     for arrive in moved:
         arrive()
     swap.finish()
+    for sent in trades:
+        sent.arrive()
+    steps.pop(1)
     for step in steps:
         step.finish()
 
@@ -1433,8 +1450,12 @@
     ]
     swap = Swap(post, at, home=True)
     early = Own(
-        post, at, parts, 0, 6,
-        ((ends_a, ends_c.at[pl.ds(0, 2)]), (mates_b, mates_e), (outer_b, outer_e)),
+        post, at, parts, 3, 3,
+        (
+            (ends_a.at[pl.ds(3, 1)], ends_c.at[pl.ds(0, 2)]),
+            (mates_b.at[pl.ds(3, 1)], mates_e),
+            (outer_b.at[pl.ds(3, 1)], outer_e),
+        ),
         own_ffn, one_ffn, two_ffn,
     )
     fold_in = [
@@ -1467,7 +1488,7 @@
             )
 
     def trade_ffn(p):
-        trade(lambda k: own_ffn.at[p, k], home_sums[p % 3], p // 3)
+        trade(lambda k: own_ffn.at[p, k], home_sums[p % 3], p // 3 - 1)
 
     post.settle(fold_in)
     width = x_buf.shape[-1]
@@ -1502,7 +1523,7 @@
     steps[0].finish()
     steps.append(Middle(post, at, 2, parts, 9, mates_d, outer_d, *bufs_3))
     steps[2].send()
-    for p in range(6):
+    for p in range(3, 6):
         trade_ffn(p)
     trade(lambda k: sums_o.at[k], home_sums[3])
     sent_q.arrive()
@@ -1545,13 +1566,30 @@
     swap.finish()
 
 
-def home_kernel(gate, up, down, qkv, out, gate_out, up_out, down_out, qkv_out, out_out):
-    for source, target in ((gate, gate_out), (up, up_out), (qkv, qkv_out)):
-        for n in range(source.shape[0] // 512):
-            place = pl.ds(n * 512, 512)
-            target[:, place] = source[place, :].astype(WIDE).T
-    down_out[...] = down[...].astype(WIDE)
-    out_out[...] = out[...].astype(WIDE)
+def home_kernel(*refs):
+    first, gate, up, down, out, qkv, gate_out, up_out, down_out, qkv_out, out_out = refs[:11]
+    gate_buf, up_buf, down_buf, out_buf, qkv_buf, sems = refs[11:]
+    pairs = []
+    for a, (array, buf) in enumerate(((gate, gate_buf), (up, up_buf), (down, down_buf))):
+        pairs.append((first.at[:, a], buf.at[:, 0]))
+        pairs.append((array, buf.at[:, pl.ds(1, 3)]))
+    pairs += [(out, out_buf), (qkv, qkv_buf)]
+    copies = [pltpu.make_async_copy(*pair, sems.at[n]) for n, pair in enumerate(pairs)]
+    for copy in copies:
+        copy.start()
+    for a, (buf, target) in enumerate(((gate_buf, gate_out), (up_buf, up_out))):
+        for copy in copies[2 * a : 2 * a + 2]:
+            copy.wait()
+        for n in range(8):
+            value = buf[n // 2, pl.ds(n % 2 * 2, 2)].reshape(512, LANES)
+            target[:, pl.ds(n * 512, 512)] = value.astype(WIDE).T
+    for copy in copies[4:]:
+        copy.wait()
+    for n in range(4):
+        rows = pl.ds(n * 1024, 1024)
+        down_out[rows] = down_buf[n].reshape(1024, LANES).astype(WIDE)
+        out_out[pl.ds(n * 256, 256)] = out_buf[n].astype(WIDE)
+        qkv_out[:, pl.ds(n * 512, 512)] = qkv_buf[n].astype(WIDE).T
 
 
 def near_body(
@@ -1649,18 +1687,18 @@
         ],
         48, 32, 5,
     )
-    grad_proj, parts_q, sums_o, out_home, ends_d, mates_c, outer_b, outer_e = call(
+    grad_proj, parts_q, sums_o, out_home, ends_d, mates_c, outer_b, outer_e, first_sums = call(
         attend_back_kernel,
         "attend_back",
         [
             shape(8, own, 512), shape(4, 4, 512, LANES), shape(4, 256, LANES),
             shape(own, width),
             shape(3, 4, 3, chunk, LANES), shape(3, 4, 2, chunk, LANES), shape(4, 4, chunk, LANES),
-            shape(2, 4, chunk, LANES),
+            shape(2, 4, chunk, LANES), shape(4, 3, chunk, LANES),
         ],
         (
             grad_mid, queries, keys, values, all_marks, inverse, out_all, mixed, attn_in, hidden, mid_own, parts,
-            ends_c, mates_b, mates_e, *whole[2::3],
+            ends_a, ends_c, mates_b, mates_e, *whole[2::3],
         ),
         [
             pltpu.VMEM((8, own, width), NARROW), pltpu.VMEM((2, 1024, 256), NARROW),
@@ -1673,9 +1711,9 @@
             pltpu.VMEM((4, 4, 512, LANES), NARROW), pltpu.VMEM((4, 4, 256, LANES), NARROW),
             pltpu.VMEM((2, 4, 256, LANES), NARROW), *[pltpu.VMEM((4, 256, LANES), NARROW)] * 2,
             pltpu.VMEM((own, width), WIDE), pltpu.VMEM((own, width), NARROW), *middle_scratch(1, 3), *middle_scratch(2, 4),
-            *middle_scratch(2, 2), *fold_scratch,
+            *middle_scratch(2, 2), *[pltpu.VMEM((3, 4, chunk, LANES), NARROW)] * 3, *fold_scratch,
         ],
-        32, 128, 6,
+        48, 128, 6,
     )
     grad_home, gain_sums, _, _, _, *sums = call(
         end_kernel,
@@ -1683,7 +1721,7 @@
         [
             shape(own, width), shape(8, LANES, dtype=WIDE), shape(3, 4, 2, chunk, LANES),
             shape(3, 4, chunk, LANES), shape(3, 4, chunk, LANES),
-            *[shape(4, 4, chunk, LANES)] * 3, shape(4, 256, LANES), shape(4, 512, LANES),
+            *[shape(4, 3, chunk, LANES)] * 3, shape(4, 256, LANES), shape(4, 512, LANES),
         ],
         (
             grad_proj, qkv_all, x_own, all_gains, grad_mid_own, gain_ffn_part, parts, parts_q, sums_o,
@@ -1701,15 +1739,19 @@
         ],
         88, 72, 7,
     )
-    gate, up, down, out, qkv = (array.reshape(-1, LANES) for array in sums)
     grad_gate, grad_up, grad_down, grad_qkv, grad_out = pl.pallas_call(
         home_kernel,
         out_shape=[
             jax.ShapeDtypeStruct(array.shape, WIDE) for array in (w_gate, w_up, w_down, wqkv, wo)
         ],
+        in_specs=[ANYWHERE] * 6,
+        scratch_shapes=[
+            *[pltpu.VMEM((4, 4, chunk, LANES), NARROW)] * 3, pltpu.VMEM((4, 256, LANES), NARROW),
+            pltpu.VMEM((4, 512, LANES), NARROW), pltpu.SemaphoreType.DMA((8,)),
+        ],
         compiler_params=pltpu.CompilerParams(vmem_limit_bytes=48 << 20),
         name="home",
-    )(gate, up, down, qkv, out)
+    )(first_sums, *sums)
     return (
         out_home.reshape(hidden_in.shape),
         grad_home.reshape(hidden_in.shape),

time: 698 us -> 699 us (level)
  no operation moved by 1% of the time
where the time goes in v6:
time: 699 us; the launch traced here: 687 us
  Pallas kernels  673 us (96%)
  local copies, waits for them, and re-layouts  11.1 us (2%)
    pallas_call x7, Pallas kernels, call(): pl.pallas_call(inner, out_shape=outs, in_specs=[ANYWHERE] * n_in, out_spe...  669 us

profile of v6, /device:TPU:1, one launch (start us, length us, event | category | flops | bytes accessed | tf_op | source)
XLA Modules:
  0.0 686.7 jit_solution(2334104350151650579)
XLA Ops:
  0.6 0.0 copy-start
  0.7 0.1 pad_maximum_fusion
  0.8 0.6 copy-done
  1.3 0.7 copy_bitcast_fusion
  2.0 0.6 broadcast_in_dim.3.refs_2_.refs_5_
  2.6 0.6 pad.10.refs_1_
  3.2 1.3 fusion.3.refs_2_
  4.5 89.4 %start.1 = (bf16[256,2048]{1,0:T(8,128)(2,1)}, bf16[8,256,2048]{2,1,0:T(8,128)(2,1)}, f32[2,4,8,256]{3,2,1,0:T(8,128)}, f32[4,4,8,128]{3,2,1,0:T(8,128)}, bf16[4...) custom-call(bf16[256,2048]{1,0:T(8,128)(2,1)} %bitcast.21, ...), custom_call_target="tpu_custom_call" | custom-call | tf_op jit(solution)/shard_map/start/pallas_call | solution.py:673
  93.9 75.3 %attend.1 = (bf16[2,1024,256]{2,1,0:T(8,128)(2,1)}, bf16[2,1024,128]{2,1,0:T(8,128)(2,1)}, bf16[2,1024,128]{2,1,0:T(8,128)(2,1)}, bf16[8,256,256]{2,1,0:T(8,128)...) custom-call(bf16[8,256,2048]{2,1,0:T(8,128)(2,1)} %get-tuple-element, ...), custom_call_target="tpu_custom_call" | custom-call | tf_op jit(solution)/shard_map/attend/pallas_call | solution.py:673
  169.2 97.2 %middle.1 = (f32[256,2048]{1,0:T(8,128)}, bf16[8,256,2048]{2,1,0:T(8,128)(2,1)}, bf16[4,4,128,256]{3,2,1,0:T(8,128)(2,1)}, bf16[4,4,128,256]{3,2,1,0:T(8,128)(2,...) custom-call(bf16[8,256,256]{2,1,0:T(8,128)(2,1)} %get-tuple-element., ...), custom_call_target="tpu_custom_call" | custom-call | tf_op jit(solution)/shard_map/middle/pallas_call | solution.py:673
  266.4 96.2 %ffn.1 = (bf16[8,256,1024]{2,1,0:T(8,128)(2,1)}, bf16[8,256,2048]{2,1,0:T(8,128)(2,1)}, bf16[12,4,4,256,128]{4,3,2,1,0:T(8,128)(2,1)}, bf16[4,4,3,256,128]{4,3,2...) custom-call(bf16[8,256,2048]{2,1,0:T(8,128)(2,1)} %get-tuple-element, ...), custom_call_target="tpu_custom_call" | custom-call | tf_op jit(solution)/shard_map/ffn/pallas_call | solution.py:673
  362.6 94.2 %back.1 = (f32[256,2048]{1,0:T(8,128)}, bf16[8,256,2048]{2,1,0:T(8,128)(2,1)}, f32[8,2048]{1,0:T(8,128)}, bf16[5,4,3,256,128]{4,3,2,1,0:T(8,128)(2,1)}, bf16[4,4...) custom-call(bf16[8,256,2048]{2,1,0:T(8,128)(2,1)} %get-tuple-element.107.refs_0_, ...), custom_call_target="tpu_custom_call" | custom-call | tf_op jit(solution)/shard_map/back/pallas_call | solution.py:673
  456.8 96.0 %attend_back.1 = (bf16[8,256,512]{2,1,0:T(8,128)(2,1)}, bf16[4,4,512,128]{3,2,1,0:T(8,128)(2,1)}, bf16[4,256,128]{2,1,0:T(8,128)(2,1)}, bf16[256,2048]{1,0:T(8,1...) custom-call(bf16[8,256,2048]{2,1,0:T(8,128)(2,1)} %get-tuple-element, ...), custom_call_target="tpu_custom_call" | custom-call | tf_op jit(solution)/shard_map/attend_back/pallas_call | solution.py:673
  552.8 0.0 copy-start.2
  552.9 0.0 copy-start.8
  552.9 120.9 %end.1 = (bf16[256,2048]{1,0:T(8,128)(2,1)}, f32[8,128]{1,0:T(8,128)}, bf16[3,4,2,256,128]{4,3,2,1,0:T(8,128)(2,1)}, bf16[3,4,256,128]{3,2,1,0:T(8,128)(2,1)}, b...) custom-call(bf16[8,256,512]{2,1,0:T(8,128)(2,1)} %get-tuple-element., ...), custom_call_target="tpu_custom_call" | custom-call | tf_op jit(solution)/shard_map/end/pallas_call | solution.py:673
  673.7 1.3 slice_bitcast_fusion
  675.0 0.0 copy-done.2
  675.0 0.0 copy-start.3
  675.0 1.1 copy-done.3
  676.1 0.0 copy-start.4
  676.1 1.1 copy-done.4
  677.3 0.0 copy-start.5
  677.3 1.1 copy-done.5
  678.4 0.0 copy-start.6
  678.4 1.0 copy-done.6
  679.5 0.0 copy-start.7
  679.5 0.9 copy-done.7
  680.4 0.0 copy-start.9
  680.4 4.1 home.1
  684.6 0.0 copy-start.1
  684.6 0.0 copy-done.8
  684.6 1.0 copy.28
  685.6 0.0 copy-done.9
  685.6 1.0 copy.29
  686.5 0.0 copy-done.1
  (3 shorter events, 0.0 us)
Async XLA Ops:
  0.6 0.7 copy-start
  552.8 122.2 %copy-start.2 = (bf16[4,3,256,128]{3,2,1,0:T(8,128)(2,1)S(1)}, bf16[4,3,256,128]{3,2,1,0:T(8,128)(2,1)}, u32[]{:S(2)}) copy-start(bf16[4,3,256,128]{3,2,1,0:T(8,128)(2,1)} %get-tuple-element.136.refs_0_) | copy-start | bytes 2359300
  552.9 131.7 %copy-start.8 = (bf16[256,2048]{1,0:T(8,128)(2,1)S(1)}, bf16[256,2048]{1,0:T(8,128)(2,1)}, u32[]{:S(2)}) copy-start(bf16[256,2048]{1,0:T(8,128)(2,1)} %get-tuple-element.124) | copy-start | bytes 3145732
  675.0 1.1 copy-start.3
  676.1 1.1 copy-start.4
  677.3 1.1 copy-start.5
  678.4 1.0 copy-start.6
  679.5 0.9 copy-start.7
  680.4 5.2 copy-start.9
  684.6 2.0 copy-start.1

commit v7 on v6

--- a/solution.py
+++ b/solution.py
@@ -1749,7 +1749,7 @@
             *[pltpu.VMEM((4, 4, chunk, LANES), NARROW)] * 3, pltpu.VMEM((4, 256, LANES), NARROW),
             pltpu.VMEM((4, 512, LANES), NARROW), pltpu.SemaphoreType.DMA((8,)),
         ],
-        compiler_params=pltpu.CompilerParams(vmem_limit_bytes=48 << 20),
+        compiler_params=pltpu.CompilerParams(vmem_limit_bytes=62 << 20),
         name="home",
     )(first_sums, *sums)
     return (

time: 699 us -> 696 us (level)
  no operation moved by 1% of the time
where the time goes in v7:
time: 696 us; the launch traced here: 683 us
  Pallas kernels  674 us (97%)
    pallas_call x7, Pallas kernels, call(): pl.pallas_call(inner, out_shape=outs, in_specs=[ANYWHERE] * n_in, out_spe...  669 us

profile of v7, /device:TPU:1, one launch (start us, length us, event | category | flops | bytes accessed | tf_op | source)
XLA Modules:
  0.0 683.1 jit_solution(16023609197557243545)
XLA Ops:
  0.6 0.0 copy-start
  0.7 0.1 pad_maximum_fusion
  0.8 0.6 copy-done
  1.3 0.7 copy_bitcast_fusion
  2.0 0.6 broadcast_in_dim.3.refs_2_.refs_5_
  2.6 0.6 pad.10.refs_1_
  3.2 1.3 fusion.3.refs_2_
  4.5 89.4 %start.1 = (bf16[256,2048]{1,0:T(8,128)(2,1)}, bf16[8,256,2048]{2,1,0:T(8,128)(2,1)}, f32[2,4,8,256]{3,2,1,0:T(8,128)}, f32[4,4,8,128]{3,2,1,0:T(8,128)}, bf16[4...) custom-call(bf16[256,2048]{1,0:T(8,128)(2,1)} %bitcast.21, ...), custom_call_target="tpu_custom_call" | custom-call | tf_op jit(solution)/shard_map/start/pallas_call | solution.py:673
  93.9 75.3 %attend.1 = (bf16[2,1024,256]{2,1,0:T(8,128)(2,1)}, bf16[2,1024,128]{2,1,0:T(8,128)(2,1)}, bf16[2,1024,128]{2,1,0:T(8,128)(2,1)}, bf16[8,256,256]{2,1,0:T(8,128)...) custom-call(bf16[8,256,2048]{2,1,0:T(8,128)(2,1)} %get-tuple-element, ...), custom_call_target="tpu_custom_call" | custom-call | tf_op jit(solution)/shard_map/attend/pallas_call | solution.py:673
  169.2 97.2 %middle.1 = (f32[256,2048]{1,0:T(8,128)}, bf16[8,256,2048]{2,1,0:T(8,128)(2,1)}, bf16[4,4,128,256]{3,2,1,0:T(8,128)(2,1)}, bf16[4,4,128,256]{3,2,1,0:T(8,128)(2,...) custom-call(bf16[8,256,256]{2,1,0:T(8,128)(2,1)} %get-tuple-element., ...), custom_call_target="tpu_custom_call" | custom-call | tf_op jit(solution)/shard_map/middle/pallas_call | solution.py:673
  266.4 96.2 %ffn.1 = (bf16[8,256,1024]{2,1,0:T(8,128)(2,1)}, bf16[8,256,2048]{2,1,0:T(8,128)(2,1)}, bf16[12,4,4,256,128]{4,3,2,1,0:T(8,128)(2,1)}, bf16[4,4,3,256,128]{4,3,2...) custom-call(bf16[8,256,2048]{2,1,0:T(8,128)(2,1)} %get-tuple-element, ...), custom_call_target="tpu_custom_call" | custom-call | tf_op jit(solution)/shard_map/ffn/pallas_call | solution.py:673
  362.6 94.2 %back.1 = (f32[256,2048]{1,0:T(8,128)}, bf16[8,256,2048]{2,1,0:T(8,128)(2,1)}, f32[8,2048]{1,0:T(8,128)}, bf16[5,4,3,256,128]{4,3,2,1,0:T(8,128)(2,1)}, bf16[4,4...) custom-call(bf16[8,256,2048]{2,1,0:T(8,128)(2,1)} %get-tuple-element.107.refs_0_, ...), custom_call_target="tpu_custom_call" | custom-call | tf_op jit(solution)/shard_map/back/pallas_call | solution.py:673
  456.8 95.9 %attend_back.1 = (bf16[8,256,512]{2,1,0:T(8,128)(2,1)}, bf16[4,4,512,128]{3,2,1,0:T(8,128)(2,1)}, bf16[4,256,128]{2,1,0:T(8,128)(2,1)}, bf16[256,2048]{1,0:T(8,1...) custom-call(bf16[8,256,2048]{2,1,0:T(8,128)(2,1)} %get-tuple-element, ...), custom_call_target="tpu_custom_call" | custom-call | tf_op jit(solution)/shard_map/attend_back/pallas_call | solution.py:673
  552.7 121.0 %end.1 = (bf16[256,2048]{1,0:T(8,128)(2,1)}, f32[8,128]{1,0:T(8,128)}, bf16[3,4,2,256,128]{4,3,2,1,0:T(8,128)(2,1)}, bf16[3,4,256,128]{3,2,1,0:T(8,128)(2,1)}, b...) custom-call(bf16[8,256,512]{2,1,0:T(8,128)(2,1)} %get-tuple-element., ...), custom_call_target="tpu_custom_call" | custom-call | tf_op jit(solution)/shard_map/end/pallas_call | solution.py:673
  673.7 0.0 copy-start.2
  673.8 1.3 slice_bitcast_fusion
  675.0 5.3 home.1
  680.3 0.0 copy-start.3
  680.3 0.0 copy-start.1
  680.3 0.0 copy-done.2
  680.3 1.0 copy.28
  681.3 0.6 copy-done.3
  681.9 1.0 copy.29
  682.9 0.0 copy-done.1
  (3 shorter events, 0.0 us)
Async XLA Ops:
  0.6 0.7 copy-start
  673.7 6.6 copy-start.2
  680.3 1.6 copy-start.3
  680.3 2.6 copy-start.1
